TPU v7x, 32 devices: a whole 2x2x4 slice. The times are simulated.
32 devices in a mesh: dp: 8 (over z, y), mp: 4 (over x, core).
Axes of the slice: x: 2, y: 2, z: 4, core: 2. Of those that a mesh axis runs over, the one named last changes fastest.
Arguments:
- patches: bfloat16 [37632, 1536], P('dp', 'mp'), may hold values from -5 to 13, as said below
- vis_count: int32 [256], P('dp'), may hold values from 24 to 64, as said below
- vis_pos: int32 [256, 64], P('dp'), may hold values from 0 to 146, as said below
- tile_sample: int32 [256], P('dp'), may hold values from 0 to 63, as said below
- tile_quad: int32 [256], P('dp'), may hold values from 0 to 3, as said below
- w_embed: bfloat16 [1536, 768], P('mp'), may hold values from -1 to 1
- b_embed: bfloat16 [768], P('mp'), may hold values from -3 to 3
- norm1_gain: bfloat16 [768], replicated, may hold values from 0.25 to 1.75
- norm1_bias: bfloat16 [768], replicated, may hold values from -3 to 3
- w_query: bfloat16 [768, 768], P(None, 'mp'), may hold values from -0.3125 to 0.3125
- b_query: bfloat16 [768], P('mp'), may hold values from -3 to 3
- w_key: bfloat16 [768, 768], P(None, 'mp'), may hold values from -0.3125 to 0.3125
- w_value: bfloat16 [768, 768], P(None, 'mp'), may hold values from -0.21875 to 0.21875
- b_value: bfloat16 [768], P('mp'), may hold values from -3 to 3
- w_attn_out: bfloat16 [768, 768], P('mp'), may hold values from -0.875 to 0.875
- b_attn_out: bfloat16 [768], P('mp'), may hold values from -3 to 3
- norm2_gain: bfloat16 [768], replicated, may hold values from 0.25 to 1.75
- norm2_bias: bfloat16 [768], replicated, may hold values from -3 to 3
- w_hidden: bfloat16 [768, 3072], P(None, 'mp'), may hold values from -0.21875 to 0.21875
- b_hidden: bfloat16 [3072], P('mp'), may hold values from -3 to 3
- w_mlp_out: bfloat16 [3072, 768], P('mp'), may hold values from -0.21875 to 0.21875
- b_mlp_out: bfloat16 [768], P('mp'), may hold values from -3 to 3
- w_decoder: bfloat16 [768, 512], P(None, 'mp'), may hold values from -0.21875 to 0.21875
- b_decoder: bfloat16 [512], P('mp'), may hold values from -3 to 3
- mask_token: bfloat16 [512], P('mp'), may hold values from -4 to 4
- cotangent: bfloat16 [37632, 512], P('dp', 'mp'), may hold values from -13 to 13
Outputs:
- decoded: bfloat16 [37632, 512], P('dp', 'mp')
- patch_grad: float32 [37632, 1536], P('dp', 'mp')
- grad_w_embed: float32 [1536, 768], P('mp')
- grad_b_embed: float32 [768], P('mp')
- grad_norm1_gain: float32 [768], replicated
- grad_norm1_bias: float32 [768], replicated
- grad_w_query: float32 [768, 768], P(None, 'mp')
- grad_b_query: float32 [768], P('mp')
- grad_w_key: float32 [768, 768], P(None, 'mp')
- grad_w_value: float32 [768, 768], P(None, 'mp')
- grad_b_value: float32 [768], P('mp')
- grad_w_attn_out: float32 [768, 768], P('mp')
- grad_b_attn_out: float32 [768], P('mp')
- grad_norm2_gain: float32 [768], replicated
- grad_norm2_bias: float32 [768], replicated
- grad_w_hidden: float32 [768, 3072], P(None, 'mp')
- grad_b_hidden: float32 [3072], P('mp')
- grad_w_mlp_out: float32 [3072, 768], P('mp')
- grad_b_mlp_out: float32 [768], P('mp')
- grad_w_decoder: float32 [768, 512], P(None, 'mp')
- grad_b_decoder: float32 [512], P('mp')
- grad_mask_token: float32 [512], P('mp')
Inputs may be any that keep to these rules, and one draw needn't show every extreme that they name: `tile_sample`: sample m has four tiles, one of each quadrant, and is processed by block owner m // 8 of dp; at most 4 tiles of one data device belong to the samples of one owner, and some device reaches 4. `tile_quad`: quadrant q covers patch rows from (q // 2) * 7 and patch columns from (q % 2) * 7 of its sample. `vis_count`: some sample has 64 visible tokens in each of its four tiles. `vis_pos`: the entries of a tile are distinct; its first vis_count entries are its visible tokens. `patches`: pixel column c holds band c % 6.
All inputs are finite; a program needn't handle non-finite values.
Results may differ from a plain program's by a relative error of at most 0.035.
Values may be sent and summed in bfloat16 or wider, within the bound.
No kernel may reach another device: no remote copies, remote signals or barrier semaphores. Data moves between devices by JAX's collectives and lax.ppermute only.
A program may use at most 192 MiB of HBM per device.

v0:
```python
import jax
import jax.numpy as jnp
from jax import lax
from jax.sharding import PartitionSpec as P

HEAD_DIM = 64
BANDS = 6
SIDE = 7
SAMP_OWN = 8


norm_eps = 1e-06
band_eps = 1e-06
big_negative = -1000000000.0


def sincos(position, full_width):
    half_width = full_width // 2
    frequency = 1.0 / 10000.0 ** (jnp.arange(half_width, dtype=jnp.float32) / half_width)
    angles = position.astype(jnp.float32)[..., None] * frequency
    return jnp.concatenate([jnp.sin(angles), jnp.cos(angles)], axis=-1)


def position_rows(quadrant, token_index, full_width, side_len):
    tile_area = side_len * side_len
    frame_pos = token_index // tile_area
    inner_pos = token_index % tile_area
    row_pos = quadrant // 2 * side_len + inner_pos // side_len
    col_pos = quadrant % 2 * side_len + inner_pos % side_len
    part_width = full_width // 16 * 6
    return jnp.concatenate(
        [
            sincos(col_pos, part_width),
            sincos(row_pos, part_width),
            sincos(frame_pos, full_width - 2 * part_width),
        ],
        axis=-1,
    )


def widen(part_rows):
    return lax.all_gather(part_rows, "mp", axis=1, tiled=True)


def narrow(term_rows):
    return lax.psum_scatter(
        term_rows.astype(jnp.bfloat16), "mp", scatter_dimension=1, tiled=True
    ).astype(jnp.float32)


def widen_grad(part_rows):
    return lax.all_gather(part_rows, "mp", axis=1, tiled=True)


def whole_sum(term_rows, bias_part, model_index):
    part_width = bias_part.shape[0]
    bias_full = lax.dynamic_update_slice_in_dim(
        jnp.zeros((term_rows.shape[1],), jnp.float32),
        bias_part.astype(jnp.float32),
        model_index * part_width,
        0,
    )
    return lax.psum((term_rows + bias_full).astype(jnp.bfloat16), "mp").astype(jnp.float32)


def gelu_exact(values):
    return jax.nn.gelu(values, approximate=False)


def norm_forward(full_rows, gain_vec, bias_vec):
    values = full_rows.astype(jnp.float32)
    centred = values - jnp.mean(values, axis=-1, keepdims=True)
    inverse_std = lax.rsqrt(jnp.mean(centred * centred, axis=-1, keepdims=True) + norm_eps)
    unit_rows = centred * inverse_std
    normed_low = (unit_rows * gain_vec.astype(jnp.float32) + bias_vec.astype(jnp.float32)).astype(
        jnp.bfloat16
    )
    return (unit_rows, inverse_std, normed_low)


def norm_backward(out_grad, unit_rows, inverse_std, gain_vec):
    scaled = out_grad * gain_vec.astype(jnp.float32)
    first_mean = jnp.mean(scaled, axis=-1, keepdims=True)
    cross_mean = jnp.mean(scaled * unit_rows, axis=-1, keepdims=True)
    input_grad = inverse_std * (scaled - first_mean - unit_rows * cross_mean)
    return (input_grad, jnp.sum(out_grad * unit_rows, axis=0), jnp.sum(out_grad, axis=0))


def attend(queries, key_rows, value_rows, usable, score_scale):
    scores = (
        jnp.einsum("sqhe,skhe->shqk", queries, key_rows, preferred_element_type=jnp.float32)
        * score_scale
    )
    scores = jnp.where(usable[:, None, None, :], scores, big_negative)
    row_top = jnp.max(scores, axis=-1, keepdims=True)
    shifted = jnp.exp(scores - row_top)
    totals = jnp.sum(shifted, axis=-1, keepdims=True)
    probs_low = (shifted / totals).astype(jnp.bfloat16)
    attended = jnp.einsum(
        "shqk,skhe->sqhe", probs_low, value_rows, preferred_element_type=jnp.float32
    )
    return (attended, row_top + jnp.log(totals))


def attend_back(queries, key_rows, value_rows, usable, log_totals, attended_grad, score_scale):
    scores = (
        jnp.einsum("sqhe,skhe->shqk", queries, key_rows, preferred_element_type=jnp.float32)
        * score_scale
    )
    scores = jnp.where(usable[:, None, None, :], scores, big_negative)
    probs = jnp.exp(scores - log_totals)
    probs_low = probs.astype(jnp.bfloat16)
    prob_grad = jnp.einsum(
        "sqhe,skhe->shqk", attended_grad, value_rows, preferred_element_type=jnp.float32
    )
    value_grad = jnp.einsum(
        "shqk,sqhe->skhe", probs_low, attended_grad, preferred_element_type=jnp.float32
    )
    row_delta = jnp.sum(probs * prob_grad, axis=-1, keepdims=True)
    score_grad = (probs * (prob_grad - row_delta)).astype(jnp.bfloat16)
    query_grad = (
        jnp.einsum("shqk,skhe->sqhe", score_grad, key_rows, preferred_element_type=jnp.float32)
        * score_scale
    )
    key_grad = (
        jnp.einsum("shqk,sqhe->skhe", score_grad, queries, preferred_element_type=jnp.float32)
        * score_scale
    )
    return (query_grad, key_grad, value_grad)


def shards(
    patches,
    vis_count,
    vis_pos,
    tile_sample,
    tile_quad,
    w_embed,
    b_embed,
    norm1_gain,
    norm1_bias,
    w_query,
    b_query,
    w_key,
    w_value,
    b_value,
    w_attn_out,
    b_attn_out,
    norm2_gain,
    norm2_bias,
    w_hidden,
    b_hidden,
    w_mlp_out,
    b_mlp_out,
    w_decoder,
    b_decoder,
    mask_token,
    cotangent,
):
    data_size = lax.axis_size("dp")
    model_size = lax.axis_size("mp")
    model_index = lax.axis_index("mp")
    tile_count = vis_count.shape[0]
    visible_max = vis_pos.shape[1]
    grid_count = patches.shape[0]
    tile_tokens = grid_count // tile_count
    pixel_cols = patches.shape[1]
    full_width = w_embed.shape[1]
    part_width = b_embed.shape[0]
    dec_part = b_decoder.shape[0]
    head_part = w_query.shape[1] // HEAD_DIM
    pair_tiles = -(-tile_count // data_size)
    pair_rows = pair_tiles * visible_max
    sample_rows = 4 * visible_max
    owner_rows = SAMP_OWN * sample_rows
    score_scale = HEAD_DIM ** (-0.5)
    zero_low = jnp.zeros((), jnp.bfloat16)
    pixels = patches.astype(jnp.float32)
    first_sum = jnp.sum(jnp.sum(pixels, axis=0).reshape(-1, BANDS), axis=0)
    second_sum = jnp.sum(jnp.sum(pixels * pixels, axis=0).reshape(-1, BANDS), axis=0)
    first_all, second_all = lax.psum((first_sum, second_sum), ("dp", "mp"))
    per_band = float(grid_count * data_size * (pixel_cols // BANDS) * model_size)
    band_mean = first_all / per_band
    band_var = second_all / per_band - band_mean * band_mean
    band_rstd = lax.rsqrt(band_var + band_eps)
    mean_cols = jnp.tile(band_mean, pixel_cols // BANDS)
    rstd_cols = jnp.tile(band_rstd, pixel_cols // BANDS)
    tile_ids = jnp.arange(tile_count, dtype=jnp.int32)
    slot_ids = jnp.arange(visible_max, dtype=jnp.int32)
    usable = slot_ids[None, :] < vis_count[:, None]
    usable_rows = usable.reshape(-1, 1)
    grid_rows = (tile_ids[:, None] * tile_tokens + vis_pos).reshape(-1)
    grid_place = jnp.where(usable, tile_ids[:, None] * tile_tokens + vis_pos, grid_count).reshape(
        -1
    )
    centred_pix = patches[grid_rows].astype(jnp.float32) - mean_cols
    normed_low = (centred_pix * rstd_cols).astype(jnp.bfloat16)
    embed_part = lax.psum_scatter(
        jnp.dot(normed_low, w_embed, preferred_element_type=jnp.float32).astype(jnp.bfloat16),
        "mp",
        scatter_dimension=1,
        tiled=True,
    ).astype(jnp.float32)
    quadrant = jnp.broadcast_to(tile_quad[:, None], vis_pos.shape)
    places = position_rows(quadrant, vis_pos, full_width, SIDE).reshape(-1, full_width)
    places_part = lax.dynamic_slice_in_dim(places, model_index * part_width, part_width, 1)
    start_rows = (embed_part + b_embed.astype(jnp.float32) + places_part).astype(jnp.bfloat16)
    start_rows = jnp.where(usable_rows, start_rows, zero_low)
    owners = tile_sample // SAMP_OWN
    earlier = (owners[:, None] == owners[None, :]) & (tile_ids[None, :] < tile_ids[:, None])
    tile_ranks = jnp.sum(earlier.astype(jnp.int32), axis=1)
    pair_index = owners * pair_tiles + tile_ranks
    send_rows = (pair_index[:, None] * visible_max + slot_ids[None, :]).reshape(-1)
    sending = (
        jnp.zeros((data_size * pair_rows, part_width), jnp.bfloat16).at[send_rows].set(start_rows)
    )
    header_vals = jnp.stack([tile_sample % SAMP_OWN, tile_quad, vis_count], axis=1).astype(
        jnp.float32
    )
    blank_head = jnp.zeros((data_size * pair_tiles, 3), jnp.float32).at[:, 0].set(float(SAMP_OWN))
    headers = blank_head.at[pair_index].set(header_vals).astype(jnp.bfloat16)
    arrived, arrived_head = (
        lax.all_to_all(
            sending.reshape(data_size, pair_rows, part_width),
            "dp",
            split_axis=0,
            concat_axis=0,
            tiled=True,
        ),
        lax.all_to_all(
            headers.reshape(data_size, pair_tiles, 3), "dp", split_axis=0, concat_axis=0, tiled=True
        ),
    )
    head_ints = arrived_head.astype(jnp.int32)
    live_rows = slot_ids[None, None, :] < head_ints[:, :, 2:3]
    target = head_ints[:, :, 0] * sample_rows + head_ints[:, :, 1] * visible_max
    place_rows = jnp.where(
        live_rows, target[:, :, None] + slot_ids[None, None, :], owner_rows
    ).reshape(-1)
    gather_rows = jnp.minimum(place_rows, owner_rows - 1)
    live_flat = live_rows.reshape(-1, 1)
    start_own = (
        jnp.zeros((owner_rows, part_width), jnp.bfloat16)
        .at[place_rows]
        .set(arrived.reshape(-1, part_width), mode="drop")
    )
    tile_counts = (
        jnp.zeros((SAMP_OWN * 4,), jnp.int32)
        .at[head_ints[:, :, 0] * 4 + head_ints[:, :, 1]]
        .set(head_ints[:, :, 2], mode="drop")
    )
    usable_own = (slot_ids[None, :] < tile_counts[:, None]).reshape(SAMP_OWN, sample_rows)
    full_start = widen(start_own)
    unit_one, rstd_one, normed_one = norm_forward(full_start, norm1_gain, norm1_bias)
    queries = (
        jnp.dot(normed_one, w_query, preferred_element_type=jnp.float32)
        + b_query.astype(jnp.float32)
    ).astype(jnp.bfloat16)
    key_rows = jnp.dot(normed_one, w_key, preferred_element_type=jnp.float32).astype(jnp.bfloat16)
    value_rows = (
        jnp.dot(normed_one, w_value, preferred_element_type=jnp.float32)
        + b_value.astype(jnp.float32)
    ).astype(jnp.bfloat16)
    head_shape = (SAMP_OWN, sample_rows, head_part, HEAD_DIM)
    query_heads = queries.reshape(head_shape)
    key_heads = key_rows.reshape(head_shape)
    value_heads = value_rows.reshape(head_shape)
    attended, log_totals = attend(query_heads, key_heads, value_heads, usable_own, score_scale)
    attended_low = attended.reshape(owner_rows, part_width).astype(jnp.bfloat16)
    attn_terms = jnp.dot(attended_low, w_attn_out, preferred_element_type=jnp.float32)
    middle_full = full_start.astype(jnp.float32) + whole_sum(attn_terms, b_attn_out, model_index)
    middle_low = middle_full.astype(jnp.bfloat16)
    unit_two, rstd_two, normed_two = norm_forward(middle_low, norm2_gain, norm2_bias)
    hidden_pre = jnp.dot(
        normed_two, w_hidden, preferred_element_type=jnp.float32
    ) + b_hidden.astype(jnp.float32)
    hidden_low = gelu_exact(hidden_pre).astype(jnp.bfloat16)
    mlp_terms = jnp.dot(hidden_low, w_mlp_out, preferred_element_type=jnp.float32)
    final_low = (middle_full + whole_sum(mlp_terms, b_mlp_out, model_index)).astype(jnp.bfloat16)
    decoded_own = (
        jnp.dot(final_low, w_decoder, preferred_element_type=jnp.float32)
        + b_decoder.astype(jnp.float32)
    ).astype(jnp.bfloat16)
    returning = jnp.where(live_flat, decoded_own[gather_rows], zero_low).reshape(
        data_size, pair_rows, dec_part
    )
    came_back = lax.all_to_all(returning, "dp", split_axis=0, concat_axis=0, tiled=True).reshape(
        -1, dec_part
    )
    decoded = (
        jnp.broadcast_to(mask_token[None, :], (grid_count, dec_part))
        .at[grid_place]
        .set(came_back[send_rows], mode="drop")
    )
    cot_rows = jnp.where(usable_rows, cotangent[grid_rows], zero_low)
    shown = jnp.zeros((grid_count,), jnp.bool_).at[grid_place].set(True, mode="drop")
    grad_mask_token = jnp.sum(jnp.where(shown[:, None], 0.0, cotangent.astype(jnp.float32)), axis=0)
    cot_sending = (
        jnp.zeros((data_size * pair_rows, dec_part), jnp.bfloat16).at[send_rows].set(cot_rows)
    )
    cot_arrived = lax.all_to_all(
        cot_sending.reshape(data_size, pair_rows, dec_part),
        "dp",
        split_axis=0,
        concat_axis=0,
        tiled=True,
    ).reshape(-1, dec_part)
    decoded_grad = (
        jnp.zeros((owner_rows, dec_part), jnp.bfloat16).at[place_rows].set(cot_arrived, mode="drop")
    )
    grad_w_decoder = jnp.dot(final_low.T, decoded_grad, preferred_element_type=jnp.float32)
    grad_b_decoder = jnp.sum(decoded_grad.astype(jnp.float32), axis=0)
    final_grad = narrow(jnp.dot(decoded_grad, w_decoder.T, preferred_element_type=jnp.float32))
    final_grad_low = final_grad.astype(jnp.bfloat16)
    grad_b_mlp_out = jnp.sum(final_grad_low.astype(jnp.float32), axis=0)
    final_grad_full = widen_grad(final_grad_low)
    grad_w_mlp_out = jnp.dot(hidden_low.T, final_grad_full, preferred_element_type=jnp.float32)
    hidden_grad = jnp.dot(final_grad_full, w_mlp_out.T, preferred_element_type=jnp.float32)
    unused_value, gelu_pull = jax.vjp(gelu_exact, hidden_pre)
    pre_grad = gelu_pull(hidden_grad)[0].astype(jnp.bfloat16)
    grad_b_hidden = jnp.sum(pre_grad.astype(jnp.float32), axis=0)
    grad_w_hidden = jnp.dot(normed_two.T, pre_grad, preferred_element_type=jnp.float32)
    two_grad = jnp.dot(pre_grad, w_hidden.T, preferred_element_type=jnp.float32)
    middle_term, gain_two_part, bias_two_part = norm_backward(
        two_grad, unit_two, rstd_two, norm2_gain
    )
    middle_grad = final_grad + narrow(middle_term)
    middle_grad_low = middle_grad.astype(jnp.bfloat16)
    grad_b_attn_out = jnp.sum(middle_grad_low.astype(jnp.float32), axis=0)
    attn_grad_full = widen_grad(middle_grad_low)
    grad_w_attn_out = jnp.dot(attended_low.T, attn_grad_full, preferred_element_type=jnp.float32)
    attended_grad = (
        jnp.dot(attn_grad_full, w_attn_out.T, preferred_element_type=jnp.float32)
        .astype(jnp.bfloat16)
        .reshape(head_shape)
    )
    query_grad, key_grad, value_grad = attend_back(
        query_heads, key_heads, value_heads, usable_own, log_totals, attended_grad, score_scale
    )
    query_grad = query_grad.reshape(owner_rows, part_width).astype(jnp.bfloat16)
    key_grad = key_grad.reshape(owner_rows, part_width).astype(jnp.bfloat16)
    value_grad = value_grad.reshape(owner_rows, part_width).astype(jnp.bfloat16)
    grad_b_query = jnp.sum(query_grad.astype(jnp.float32), axis=0)
    grad_b_value = jnp.sum(value_grad.astype(jnp.float32), axis=0)
    grad_w_query = jnp.dot(normed_one.T, query_grad, preferred_element_type=jnp.float32)
    grad_w_key = jnp.dot(normed_one.T, key_grad, preferred_element_type=jnp.float32)
    grad_w_value = jnp.dot(normed_one.T, value_grad, preferred_element_type=jnp.float32)
    one_grad = jnp.dot(query_grad, w_query.T, preferred_element_type=jnp.float32)
    one_grad = one_grad + jnp.dot(key_grad, w_key.T, preferred_element_type=jnp.float32)
    one_grad = one_grad + jnp.dot(value_grad, w_value.T, preferred_element_type=jnp.float32)
    start_term, gain_one_part, bias_one_part = norm_backward(
        one_grad, unit_one, rstd_one, norm1_gain
    )
    start_grad = (middle_grad + narrow(start_term)).astype(jnp.bfloat16)
    leaving = jnp.where(live_flat, start_grad[gather_rows], zero_low).reshape(
        data_size, pair_rows, part_width
    )
    embed_grad = lax.all_to_all(leaving, "dp", split_axis=0, concat_axis=0, tiled=True).reshape(
        -1, part_width
    )[send_rows]
    grad_b_embed = jnp.sum(embed_grad.astype(jnp.float32), axis=0)
    embed_grad_full = lax.all_gather(embed_grad, "mp", axis=1, tiled=True)
    grad_w_embed = jnp.dot(normed_low.T, embed_grad_full, preferred_element_type=jnp.float32)
    normed_grad = jnp.dot(embed_grad_full, w_embed.T, preferred_element_type=jnp.float32)
    sum_grad = jnp.sum(jnp.sum(normed_grad, axis=0).reshape(-1, BANDS), axis=0)
    sum_cross = jnp.sum(jnp.sum(normed_grad * centred_pix, axis=0).reshape(-1, BANDS), axis=0)
    gain_one, bias_one, gain_two, bias_two, grad_all, cross_all = lax.psum(
        (gain_one_part, bias_one_part, gain_two_part, bias_two_part, sum_grad, sum_cross),
        ("dp", "mp"),
    )
    grad_var = -0.5 * cross_all * band_rstd * band_rstd * band_rstd
    grad_mean = -band_rstd * grad_all - 2.0 * band_mean * grad_var
    patch_grad = jnp.tile(grad_mean / per_band, pixel_cols // BANDS) + 2.0 * pixels * jnp.tile(
        grad_var / per_band, pixel_cols // BANDS
    )
    patch_grad = patch_grad.at[grid_place].add(normed_grad * rstd_cols, mode="drop")
    summed = (
        lax.psum(grad_w_embed.astype(jnp.bfloat16), "dp").astype(jnp.float32),
        lax.psum(grad_b_embed.astype(jnp.bfloat16), "dp").astype(jnp.float32),
        lax.psum(grad_w_query.astype(jnp.bfloat16), "dp").astype(jnp.float32),
        lax.psum(grad_b_query.astype(jnp.bfloat16), "dp").astype(jnp.float32),
        lax.psum(grad_w_key.astype(jnp.bfloat16), "dp").astype(jnp.float32),
        lax.psum(grad_w_value.astype(jnp.bfloat16), "dp").astype(jnp.float32),
        lax.psum(grad_b_value.astype(jnp.bfloat16), "dp").astype(jnp.float32),
        lax.psum(grad_w_attn_out.astype(jnp.bfloat16), "dp").astype(jnp.float32),
        lax.psum(grad_b_attn_out.astype(jnp.bfloat16), "dp").astype(jnp.float32),
        lax.psum(grad_w_hidden.astype(jnp.bfloat16), "dp").astype(jnp.float32),
        lax.psum(grad_b_hidden.astype(jnp.bfloat16), "dp").astype(jnp.float32),
        lax.psum(grad_w_mlp_out.astype(jnp.bfloat16), "dp").astype(jnp.float32),
        lax.psum(grad_b_mlp_out.astype(jnp.bfloat16), "dp").astype(jnp.float32),
        lax.psum(grad_w_decoder.astype(jnp.bfloat16), "dp").astype(jnp.float32),
        lax.psum(grad_b_decoder.astype(jnp.bfloat16), "dp").astype(jnp.float32),
        lax.psum(grad_mask_token.astype(jnp.bfloat16), "dp").astype(jnp.float32),
    )
    return (
        decoded,
        patch_grad,
        summed[0],
        summed[1],
        gain_one,
        bias_one,
        summed[2],
        summed[3],
        summed[4],
        summed[5],
        summed[6],
        summed[7],
        summed[8],
        gain_two,
        bias_two,
        summed[9],
        summed[10],
        summed[11],
        summed[12],
        summed[13],
        summed[14],
        summed[15],
    )


def solution(mesh):
    in_specs = (
        P("dp", "mp"),
        P("dp"),
        P("dp", None),
        P("dp"),
        P("dp"),
        P("mp", None),
        P("mp"),
        P(),
        P(),
        P(None, "mp"),
        P("mp"),
        P(None, "mp"),
        P(None, "mp"),
        P("mp"),
        P("mp", None),
        P("mp"),
        P(),
        P(),
        P(None, "mp"),
        P("mp"),
        P("mp", None),
        P("mp"),
        P(None, "mp"),
        P("mp"),
        P("mp"),
        P("dp", "mp"),
    )
    out_specs = (
        P("dp", "mp"),
        P("dp", "mp"),
        P("mp", None),
        P("mp"),
        P(),
        P(),
        P(None, "mp"),
        P("mp"),
        P(None, "mp"),
        P(None, "mp"),
        P("mp"),
        P("mp", None),
        P("mp"),
        P(),
        P(),
        P(None, "mp"),
        P("mp"),
        P("mp", None),
        P("mp"),
        P(None, "mp"),
        P("mp"),
        P("mp"),
    )
    return jax.shard_map(shards, mesh=mesh, in_specs=in_specs, out_specs=out_specs, check_vma=False)
```

profile of v0, /device:TPU:0, one launch (start us, length us, event | category | flops | bytes accessed | tf_op | source)
XLA Modules:
  0.0 816.5 jit_solution(12842917659056257035)
XLA Ops:
  13.6 9.7 %gather_fusion = bf16[2048,384]{1,0:T(8,128)(2,1)S(1)} fusion(bf16[4704,384]{1,0:T(8,128)(2,1)} %param.28, s32[2048]{0:T(1024)S(1)} %broadcast_clamp_fusion.2), kind=kCustom, calls=%fused_computation | custom fusion | bytes 3153920 | tf_op jit(solution)/shard_map/gather | solution.py:196
  23.3 42.0 %all-reduce.2 = (f32[6]{0:T(128)S(1)}, f32[6]{0:T(128)S(1)}) all-reduce(f32[6]{0:T(128)S(1)} %reduce_sum.308, f32[6]{0:T(128)S(1)} %reduce_sum.306), channel_id=1, replica_groups=mesh['dp'=8,'mp'=4] {'dp','mp'}, use_global_device_ids=true, to_apply=%region_8.9 | all-reduce | flops 12 | bytes 96 | tf_op jit(solution)/shard_map/psum | solution.py:181
  112.5 9.9 %scatter_custom_fusion.1 = bf16[2048,192]{1,0:T(8,128)(2,1)S(1)} fusion(s32[2048]{0:T(1024)S(1)} %bitcast.170, bf16[2048,192]{1,0:T(8,128)(2,1)} %copy.214, bf16[]{:T(256)} %constant.213.clone.1), kind=kCustom, calls=%fused_computation.147 | custom fusion | bytes 786944 | tf_op jit(solution)/shard_map/scatter | solution.py:215
  130.0 19.4 %all-to-all-done.1 = bf16[8,256,192]{1,2,0:T(8,128)(2,1)S(1)} async-done(((bf16[8,256,192]{1,2,0:T(8,128)(2,1)}), bf16[8,256,192]{1,2,0:T(8,128)(2,1)S(1)}, u32[]{:S(2)}, u32[]{:S(2)}) %all-to-all-start.1) | async-done | bytes 786464 | tf_op jit(solution)/shard_map/all_to_all | solution.py:223
  150.7 9.9 %scatter_custom_fusion.2 = bf16[2048,192]{1,0:T(8,128)(2,1)S(1)} fusion(s32[2048]{0:T(1024)S(1)} %bitcast.174, bf16[2048,192]{1,0:T(8,128)(2,1)} %bitcast.160, bf16[]{:T(256)} %constant.213.clone.1), kind=kCustom, calls=%fused_computation.149 | custom fusion | bytes 786944 | tf_op jit(solution)/shard_map/scatter | solution.py:245
  162.0 13.2 %scatter_custom_fusion.5 = bf16[2048,128]{1,0:T(8,128)(2,1)S(1)} fusion(s32[2048]{0:T(1024)S(1)} %bitcast.171, pred[2048]{0:T(1024)(128)(4,1)S(1)} %lt.207, bf16[]{:T(256)} %constant.213.clone.1, bf16[4704,128]{1,0:T(8,128)(2,1)S(1)} %copy-done.25, s32[2048]{0:T(1024)S(1)} %broadcast_clamp_fusion.2), kind=kCustom, calls=%fused_computation.154 | custom fusion | flops 262144 | bytes 1739776 | tf_op jit(solution)/shard_map/scatter | solution.py:299
  175.2 18.2 %all_to_all.25 = bf16[8,256,128]{2,1,0:T(8,128)(2,1)S(1)} all-to-all(bf16[8,256,128]{2,1,0:T(8,128)(2,1)S(1)} %bitcast.159), channel_id=1, replica_groups=mesh['dp'=8,'mp'=4] {'dp'}, dimensions={0} | all-to-all | bytes 1048576 | tf_op jit(solution)/shard_map/all_to_all | solution.py:301
  229.9 9.4 %reduce-scatter.13.cloned.1.call-done = bf16[192,2048]{1,0:T(8,128)(2,1)} async-done(((bf16[768,2048]{1,0:T(8,128)(2,1)}), bf16[192,2048]{1,0:T(8,128)(2,1)}) %reduce-scatter.13.cloned.1.call-update) | async-done | bytes 786448
  239.5 71.1 %all-reduce.9.cloned.1.call-done = bf16[2048,768]{1,0:T(8,128)(2,1)} async-done(((bf16[2048,768]{1,0:T(8,128)(2,1)}), bf16[2048,768]{1,0:T(8,128)(2,1)}) %all-reduce.9.cloned.1.call-update) | async-done | bytes 3145744 | tf_op jit(solution)/shard_map/psum | solution.py:63
  321.2 19.4 %all-gather.8.cloned.1.call-done = bf16[2048,768]{0,1:T(8,128)(2,1)} async-done(((bf16[2048,192]{0,1:T(8,128)(2,1)}), bf16[2048,768]{0,1:T(8,128)(2,1)}) %all-gather.8.cloned.1.call-update) | async-done | bytes 3145744 | tf_op jit(solution)/shard_map/all_gather | solution.py:52
  340.7 20.1 %fusion.101 = (bf16[768]{0:T(1024)(128)(2,1)S(1)}, bf16[2048,768]{1,0:T(8,128)(2,1)S(1)}, f32[2048,768]{1,0:T(8,128)}) fusion(f32[2048,768]{1,0:T(8,128)} %fusion.98, f32[768]{0:T(1024)S(1)} %convert_element_type.327, bf16[2048,768]{0,1:T(8,128)(2,1)} %all-gather.8.cloned.1.call-done, bf16[768,768]{1,0:T(8,128)(2,1)S(1)} %copy-done), kind=kOutput, calls=%fused_computation.240 | convolution fusion | flops 2532310272 | bytes 20058624 | tf_op jit(solution)/shard_map/dot_general | solution.py:318
  373.7 37.5 %reduce-scatter.15.cloned.1.call-done = bf16[192,2048]{1,0:T(8,128)(2,1)} async-done(((bf16[768,2048]{1,0:T(8,128)(2,1)}), bf16[192,2048]{1,0:T(8,128)(2,1)}) %reduce-scatter.15.cloned.1.call-update) | async-done | bytes 786448
  416.6 28.4 %all-gather.10.cloned.1.call-done = bf16[2048,768]{0,1:T(8,128)(2,1)} async-done(((bf16[2048,192]{0,1:T(8,128)(2,1)}), bf16[2048,768]{0,1:T(8,128)(2,1)}) %all-gather.10.cloned.1.call-update) | async-done | bytes 3145744 | tf_op jit(solution)/shard_map/all_gather | solution.py:52
  488.7 26.6 %reduce-scatter.17.cloned.1.call-done = bf16[192,2048]{1,0:T(8,128)(2,1)} async-done(((bf16[768,2048]{1,0:T(8,128)(2,1)}), bf16[192,2048]{1,0:T(8,128)(2,1)}) %reduce-scatter.17.cloned.1.call-update) | async-done | bytes 786448
  519.7 9.1 %gather_fusion.2 = bf16[2048,192]{1,0:T(8,128)(2,1)} fusion(bf16[2048,192]{1,0:T(8,128)(2,1)S(1)} %add_convert_fusion.4, s32[2048]{0:T(1024)S(1)} %broadcast_clamp_fusion.1), kind=kCustom, calls=%fused_computation.4 | custom fusion | bytes 1581056 | tf_op jit(solution)/shard_map/gather | solution.py:355
  536.8 20.2 %all-to-all-done.4 = bf16[8,256,192]{1,2,0:T(8,128)(2,1)} async-done(((bf16[8,256,192]{1,2,0:T(8,128)(2,1)}), bf16[8,256,192]{1,2,0:T(8,128)(2,1)}, u32[]{:S(2)}, u32[]{:S(2)}) %all-to-all-start.4) | async-done | bytes 786464 | tf_op jit(solution)/shard_map/all_to_all | solution.py:358
  599.4 18.1 %all-gather.12.cloned.1.call-done = bf16[2048,768]{0,1:T(8,128)(2,1)} async-done(((bf16[2048,192]{0,1:T(8,128)(2,1)}), bf16[2048,768]{0,1:T(8,128)(2,1)}) %all-gather.12.cloned.1.call-update) | async-done | bytes 3145744 | tf_op jit(solution)/shard_map/all_gather | solution.py:362
  643.4 9.1 %scatter_custom_fusion.8 = pred[4704]{0:T(1024)(128)(4,1)S(1)} fusion(s32[2048]{0:T(1024)S(1)} %bitcast.176, pred[2048]{0:T(1024)(128)(4,1)S(1)} %broadcast.529, pred[]{:T(512)} %constant.263.clone.1), kind=kCustom, calls=%fused_computation.187 | custom fusion | bytes 4705 | tf_op jit(solution)/shard_map/scatter | solution.py:296
  657.8 14.5 %all-to-all-done.2 = bf16[8,256,128]{2,1,0:T(8,128)(2,1)S(1)} async-done(((bf16[8,256,128]{2,1,0:T(8,128)(2,1)}), bf16[8,256,128]{2,1,0:T(8,128)(2,1)S(1)}, u32[]{:S(2)}, u32[]{:S(2)}) %all-to-all-start.2) | async-done | bytes 524320 | tf_op jit(solution)/shard_map/all_to_all | solution.py:287
  673.5 14.3 %scatter_custom_fusion.4 = bf16[4704,128]{1,0:T(8,128)(2,1)} fusion(bf16[4704,128]{1,0:T(8,128)(2,1)} %broadcast_in_dim.92, s32[2048]{0:T(1024)S(1)} %bitcast.177, bf16[2048,128]{1,0:T(8,128)(2,1)S(1)} %bitcast.166, s32[2048]{0:T(1024)S(1)} %broadcast_clamp_fusion), kind=kCustom, calls=%fused_computation.151 | custom fusion | bytes 1204224 | tf_op jit(solution)/shard_map/scatter | solution.py:293
  688.2 19.9 %all-reduce.3 = (bf16[192]{0:T(256)(128)(2,1)S(1)}, bf16[192]{0:T(256)(128)(2,1)S(1)}, bf16[192]{0:T(256)(128)(2,1)S(1)}, bf16[192]{0:T(256)(128)(2,1)S(1)}, bf1...) all-reduce(bf16[192]{0:T(256)(128)(2,1)S(1)} %reduce_sum.323, ...), channel_id=1, replica_groups=mesh['dp'=8,'mp'=4] {'dp'}, use_global_device_ids=true, to_apply=%region_41.42 | all-reduce | flops 1984 | bytes 7936 | tf_op jit(solution)/shard_map/psum | solution.py:379
  719.1 38.2 %all-reduce.1 = (f32[6]{0:T(128)S(1)}, f32[6]{0:T(128)S(1)}, f32[768]{0:T(1024)}, f32[768]{0:T(1024)}, f32[768]{0:T(1024)}, /*index=5*/f32[768]{0:T(1024)}) all-reduce(f32[6]{0:T(128)S(1)} %reduce_sum.322, f32[6]{0:T(128)S(1)} %reduce_sum.320, f32[768]{0:T(1024)S(1)} %get-tuple-element.36, ...), channel_id=1, replica_groups=mesh['dp'=8,'mp'=4] {'dp','mp'}, use_global_device_ids=true, to_apply=%region_37.38 | all-reduce | flops 3084 | bytes 24672 | tf_op jit(solution)/shard_map/psum | solution.py:367
  763.4 19.4 %scatter_custom_fusion.7 = f32[4704,384]{1,0:T(8,128)} fusion(f32[4704,384]{1,0:T(8,128)} %fusion.13, s32[2048]{0:T(1024)S(1)} %bitcast.178, f32[2048,384]{1,0:T(8,128)} %get-tuple-element.108, f32[384]{0:T(512)S(1)} %copy-done.50), kind=kCustom, calls=%fused_computation.88 | custom fusion | flops 1572864 | bytes 10373120 | tf_op jit(solution)/shard_map/scatter-add | solution.py:376
  782.8 15.6 %all-reduce.13.cloned.1.call-done = (bf16[384,768]{1,0:T(8,128)(2,1)}, bf16[768,192]{0,1:T(8,128)(2,1)}, bf16[768,192]{0,1:T(8,128)(2,1)}, bf16[768,192]{0,1:T(8...) async-done(((bf16[384,768]{1,0:T(8,128)(2,1)}, bf16[768,192]{0,1:T(8,128)(2,1)}, ...) | async-done | bytes 4325392 | tf_op jit(solution)/shard_map/psum | solution.py:378
  (386 shorter events, 286.9 us)
Async XLA Ops:
  7.2 333.5 %copy-start = (bf16[768,768]{1,0:T(8,128)(2,1)S(1)}, bf16[768,768]{1,0:T(8,128)(2,1)}, u32[]{:S(2)}) copy-start(bf16[768,768]{1,0:T(8,128)(2,1)} %param.48) | copy-start | bytes 3538948
  7.2 102.1 %reduce-scatter.11.cloned.1.call-start = ((), (), s32[]{:S(2)}) async-start(), calls=%async_computation.9 | async-start | bytes 3932160 | tf_op jit(solution)/shard_map/reduce_scatter | solution.py:198
  74.5 49.2 %all-to-all-start = ((bf16[8,4,3]{1,2,0:T(4,128)(2,1)}), bf16[8,4,3]{1,2,0:T(4,128)(2,1)S(1)}, u32[]{:S(2)}, u32[]{:S(2)}) async-start(bf16[8,4,3]{1,2,0:T(4,128)(2,1)} %copy.209), calls=%async_computation | async-start | bytes 16384 | tf_op jit(solution)/shard_map/all_to_all | solution.py:230
  80.6 81.4 %copy-start.47 = (s32[2048,1]{0,1:T(1,128)}, s32[2048,1]{0,1:T(1,128)S(1)}, u32[]{:S(2)}) copy-start(s32[2048,1]{0,1:T(1,128)S(1)} %compare_select_fusion.2) | copy-start | bytes 24580
  111.2 50.8 %copy-start.25 = (bf16[4704,128]{1,0:T(8,128)(2,1)S(1)}, bf16[4704,128]{1,0:T(8,128)(2,1)}, u32[]{:S(2)}) copy-start(bf16[4704,128]{1,0:T(8,128)(2,1)} %param.53) | copy-start | bytes 3612676
  123.7 25.7 %all-to-all-start.1 = ((bf16[8,256,192]{1,2,0:T(8,128)(2,1)}), bf16[8,256,192]{1,2,0:T(8,128)(2,1)S(1)}, u32[]{:S(2)}, u32[]{:S(2)}) async-start(bf16[8,256,192]{1,2,0:T(8,128)(2,1)} %copy.215), calls=%async_computation.2 | async-start | bytes 1572864 | tf_op jit(solution)/shard_map/all_to_all | solution.py:223
  129.3 75.8 %all-gather.6.cloned.1.call-start = ((), (), s32[]{:S(2)}) async-start(), calls=%async_computation.10 | async-start | bytes 3932160 | tf_op jit(solution)/shard_map/all_gather | solution.py:42
  161.9 77.4 %reduce-scatter.13.cloned.1.call-start = ((), (), s32[]{:S(2)}) async-start(), calls=%async_computation.16 | async-start | bytes 3932160
  203.0 107.5 %all-reduce.9.cloned.1.call-start = ((), (), s32[]{:S(2)}) async-start(), calls=%async_computation.11 | async-start | bytes 6291456 | tf_op jit(solution)/shard_map/psum | solution.py:63
  229.9 110.8 %all-gather.8.cloned.1.call-start = ((), (), s32[]{:S(2)}) async-start(), calls=%async_computation.13 | async-start | bytes 3932160 | tf_op jit(solution)/shard_map/all_gather | solution.py:52
  239.4 171.9 %reduce-scatter.15.cloned.1.call-start = ((), (), s32[]{:S(2)}) async-start(), calls=%async_computation.17 | async-start | bytes 3932160
  239.5 76.6 %copy-start.68 = (bf16[768,768]{1,0:T(8,128)(2,1)S(1)}, bf16[768,768]{1,0:T(8,128)(2,1)}, u32[]{:S(2)}) copy-start(bf16[768,768]{1,0:T(8,128)(2,1)} %param.46) | copy-start | bytes 3538948
  373.1 71.9 %all-gather.10.cloned.1.call-start = ((), (), s32[]{:S(2)}) async-start(), calls=%async_computation.14 | async-start | bytes 3932160 | tf_op jit(solution)/shard_map/all_gather | solution.py:52
  373.7 74.4 %copy-start.14 = (bf16[2048,192]{1,0:T(8,128)(2,1)}, bf16[2048,192]{1,0:T(8,128)(2,1)S(1)}, u32[]{:S(2)}) copy-start(bf16[2048,192]{1,0:T(8,128)(2,1)S(1)} %copy.251) | copy-start | bytes 2359300
  416.3 98.9 %reduce-scatter.17.cloned.1.call-start = ((), (), s32[]{:S(2)}) async-start(), calls=%async_computation.18 | async-start | bytes 3932160
  477.1 109.6 %all-reduce.11.cloned.1.call-start = ((), (), s32[]{:S(2)}) async-start(), calls=%async_computation.12 | async-start | bytes 6291456 | tf_op jit(solution)/shard_map/psum | solution.py:63
  531.2 25.8 %all-to-all-start.4 = ((bf16[8,256,192]{1,2,0:T(8,128)(2,1)}), bf16[8,256,192]{1,2,0:T(8,128)(2,1)}, u32[]{:S(2)}, u32[]{:S(2)}) async-start(bf16[8,256,192]{1,2,0:T(8,128)(2,1)} %broadcast_select_fusion), calls=%async_computation.5 | async-start | bytes 1572864 | tf_op jit(solution)/shard_map/all_to_all | solution.py:358
  536.7 80.7 %all-gather.12.cloned.1.call-start = ((), (), s32[]{:S(2)}) async-start(), calls=%async_computation.15 | async-start | bytes 3932160 | tf_op jit(solution)/shard_map/all_gather | solution.py:362
  569.6 228.8 %all-reduce.13.cloned.1.call-start = ((), (), s32[]{:S(2)}) async-start(), calls=%async_computation.19 | async-start | bytes 8650752 | tf_op jit(solution)/shard_map/psum | solution.py:378
  627.5 60.2 %copy-start.63 = (bf16[3,64]{1,0:T(4,128)(2,1)S(1)}, bf16[3,64]{1,0:T(4,128)(2,1)}, u32[]{:S(2)}) copy-start(bf16[3,64]{1,0:T(4,128)(2,1)} %get-tuple-element.109) | copy-start | bytes 1156
  627.5 60.4 %copy-start.16 = (bf16[2048,192]{1,0:T(8,128)(2,1)S(1)}, bf16[2048,192]{1,0:T(8,128)(2,1)}, u32[]{:S(2)}) copy-start(bf16[2048,192]{1,0:T(8,128)(2,1)} %gather_fusion.3) | copy-start | bytes 2359300
  637.8 34.5 %all-to-all-start.2 = ((bf16[8,256,128]{2,1,0:T(8,128)(2,1)}), bf16[8,256,128]{2,1,0:T(8,128)(2,1)S(1)}, u32[]{:S(2)}, u32[]{:S(2)}) async-start(bf16[8,256,128]{2,1,0:T(8,128)(2,1)} %broadcast_select_fusion.3), calls=%async_computation.3 | async-start | bytes 1048576 | tf_op jit(solution)/shard_map/all_to_all | solution.py:287
  708.8 48.5 %copy-start.53 = (f32[6]{0:T(128)S(1)}, f32[6]{0:T(128)}, u32[]{:S(2)}) copy-start(f32[6]{0:T(128)} %copy-done.52) | copy-start | bytes 76
  708.8 48.5 %copy-start.62 = (f32[6]{0:T(128)S(1)}, f32[6]{0:T(128)}, u32[]{:S(2)}) copy-start(f32[6]{0:T(128)} %copy-done.61) | copy-start | bytes 76
  (69 other events, 695.2 us)
Sparse Core Ops, SparseCore 0:
  71.5 37.7 reduce-scatter.10
  162.0 26.5 all-gather.5
  203.2 36.1 reduce-scatter.12
  242.1 68.4 all-reduce.8
  312.0 28.6 all-gather.7
  373.3 37.9 reduce-scatter.14
  416.5 28.5 all-gather.9
  477.2 37.9 reduce-scatter.16
  518.2 68.4 all-reduce.10
  588.7 28.7 all-gather.11
  623.7 174.6 all-reduce.12
where the time goes:
time: 822 us; the launch traced here: 817 us
  waiting for transfers between devices  289 us (35%)
  local copies, waits for them, and re-layouts  131 us (16%)
  other arithmetic  129 us (16%)
  blocking collectives  118 us (14%)
  matrix products  110 us (13%)
  starting transfers between devices  23.1 us (3%)
  between operations  16.4 us (2%)
    psum x2, waiting for transfers between devices, whole_sum(): lax.psum((term_rows + bias_full).astype(jnp.bfloat16), 'mp')  77 us
    unnamed x14, waiting for transfers between devices  73.7 us
    all_gather x2, waiting for transfers between devices, widen_grad(): return lax.all_gather(part_rows, 'mp', axis=1, tiled=True)  47.9 us
    psum x1, blocking collectives, shards(): first_all, second_all = lax.psum((first_sum, second_sum), ('dp', 'mp'))  42 us
    psum x1, blocking collectives, shards(): lax.psum((gain_one_part, bias_one_part, gain_two_part, bias_two_part, sum...  38.2 us
    unnamed x6, other arithmetic  22.5 us
    unnamed x169, local copies, waits for them, and re-layouts  20.8 us
    all_to_all x1, waiting for transfers between devices, shards(): lax.all_to_all(leaving, 'dp', split_axis=0, concat_axis=0, tiled=True)  20.2 us
  transfers between devices with their start and end apart: 15, of which 13 were waited for; matrix products, arithmetic and copies ran while one was open for 30% of the time, Pallas kernels for 0%

commit v1 on v0

v1 whole, which is shorter than its diff:
```python
import functools

import jax
import jax.numpy as jnp
import numpy as np
from jax import lax
from jax.experimental import pallas as pl
from jax.experimental.pallas import tpu as pltpu
from jax.sharding import PartitionSpec as P

HEAD_DIM = 64
BANDS = 6
SIDE = 7
SAMP_OWN = 8
WINDOW = 176
VMEM_BYTES = 56 * 1024 * 1024

norm_eps = 1e-06
band_eps = 1e-06
big_negative = -1000000000.0
F32 = jnp.float32
BF16 = jnp.bfloat16


def params():
    return pltpu.CompilerParams(vmem_limit_bytes=VMEM_BYTES)


VM = pl.BlockSpec(memory_space=pltpu.VMEM)
SM = pl.BlockSpec(memory_space=pltpu.SMEM)


def swap(values, axis, bit):
    size = lax.axis_size(axis)
    return lax.ppermute(values, axis, [(i, i ^ bit) for i in range(size)])


def bits_of(axis):
    size = lax.axis_size(axis)
    return [1 << k for k in range(size.bit_length() - 1)]


def after(value, *before):
    return lax.optimization_barrier((value,) + before)[0]


def dot(left, right):
    return jnp.dot(left, right, preferred_element_type=F32)


def dot_t(left, right):
    return lax.dot_general(left, right, (((1,), (1,)), ((), ())), preferred_element_type=F32)


def dot_tl(left, right):
    return lax.dot_general(left, right, (((0,), (0,)), ((), ())), preferred_element_type=F32)


def window_of(tile, tile_tokens, total):
    base = tile * tile_tokens
    start = jnp.minimum((base // 16) * 16, total - WINDOW)
    return pl.multiple_of(start, 16), base - start


def hot_rows(pos_ref, count, tile, rem):
    lane = lax.broadcasted_iota(jnp.int32, (1, 128), 1)
    target = jnp.where(lane < count, pos_ref[pl.ds(tile, 1), :] + rem, -1)
    row = lax.broadcasted_iota(jnp.int32, (WINDOW, 128), 0)
    return row == target


def stats_kernel(patches, stats):
    def sum_step(i, carry):
        first, second = carry
        at = pl.multiple_of(i * 336, 16)
        x = patches[pl.ds(at, 336), :].astype(F32).reshape(42, 8, patches.shape[1])
        return first + jnp.sum(x, axis=0), second + jnp.sum(x * x, axis=0)

    blank = jnp.zeros((8, patches.shape[1]), F32)
    first, second = lax.fori_loop(0, patches.shape[0] // 336, sum_step, (blank, blank))
    stats[...] = band_sums(
        jnp.sum(first, axis=0, keepdims=True), jnp.sum(second, axis=0, keepdims=True)
    )


def pick_kernel(tile_tokens, order, count, pos, patches, cot, picked, cot_picked, mask_sum):
    total = patches.shape[0]
    slots = order.shape[0]
    visible = picked.shape[0] // slots
    mask_total = jnp.zeros((8, cot.shape[1]), F32)
    row = lax.broadcasted_iota(jnp.int32, (WINDOW, 128), 0)
    lane = lax.broadcasted_iota(jnp.int32, (WINDOW, 128), 1)
    for slot in range(slots):
        tile = order[slot]
        start, rem = window_of(tile, tile_tokens, total)
        hot = hot_rows(pos, count[tile], tile, rem).astype(F32)
        shown = jnp.sum(hot, axis=1, keepdims=True)
        inside = jnp.logical_and(row >= rem, row < rem + tile_tokens)
        hidden = jnp.where(inside, 1.0 - shown, 0.0)
        chooser = jnp.where(lane == visible, hidden, hot).astype(BF16)
        got = dot_tl(chooser, patches[pl.ds(start, WINDOW), :])
        got_cot = dot_tl(chooser, cot[pl.ds(start, WINDOW), :])
        here = slice(slot * visible, (slot + 1) * visible)
        picked[here, :] = got[:visible].astype(BF16)
        cot_picked[here, :] = got_cot[:visible].astype(BF16)
        mask_total = mask_total + got_cot[visible : visible + 8]
    mask_sum[...] = mask_total


def place_in(codes, tiles, visible, blocks):
    rows, cols = tiles.shape
    each = rows // blocks

    def kernel(code_ref, tile_ref, *refs):
        outs, held = refs[:-1], refs[-1]
        for k in range(rows // visible):
            at = pl.multiple_of(code_ref[k] * visible, 16)
            held[pl.ds(at, visible), :] = tile_ref[k * visible : (k + 1) * visible, :]
        at = 0
        for out in outs:
            out[...] = held[at : at + out.shape[0], :]
            at += out.shape[0]

    return call(
        kernel,
        [((each, cols), tiles.dtype)] * 2 + [((2 * each, cols), tiles.dtype)],
        [codes, tiles],
        "place_tiles",
        [pltpu.VMEM((rows, cols), tiles.dtype)],
        scalars=1,
    )


def place_out(codes, parts, visible):
    rows, cols = parts[0].shape
    total = 4 * rows

    def kernel(code_ref, own, near, far, out, held):
        for b, ref in enumerate(blocks_of((own, near, far))):
            held[b * rows : (b + 1) * rows, :] = ref[...]
        for k in range(total // visible):
            at = pl.multiple_of(code_ref[k] * visible, 16)
            out[k * visible : (k + 1) * visible, :] = held[pl.ds(at, visible), :]

    return call(
        kernel,
        [((total, cols), parts[0].dtype)],
        [codes] + parts,
        "return_tiles",
        [pltpu.VMEM((total, cols), parts[0].dtype)],
        scalars=1,
    )[0]


def blocks_of(crossed):
    own, near, far = crossed
    rows = own.shape[0]
    return [own, near.at[:rows], far.at[:rows], near.at[rows:]]


class Crossing:
    def __init__(self, own, near, far):
        self.own, self.near = own, near
        self.far = swap(far, "mp", 2)

    def relay(self, line):
        rows = self.own.shape[0]
        both = jnp.concatenate([self.near, line.wait(self.far)[rows:]], axis=0)
        line.mark(both)
        self.parts = [self.own, swap(both, "mp", 1), self.far]


def spread_kernel(tile_tokens, order, count, pos, mask_token, given, out):
    total = out.shape[0]
    slots = order.shape[0]
    visible = given.shape[0] // slots
    out[...] = jnp.broadcast_to(mask_token[...], out.shape)
    for slot in range(slots):
        tile = order[slot]
        start, rem = window_of(tile, tile_tokens, total)
        hot = hot_rows(pos, count[tile], tile, rem).astype(F32)
        shown = jnp.sum(hot, axis=1, keepdims=True) > 0.5
        rows = given[slot * visible : (slot + 1) * visible, :]
        new = dot(hot[:, :visible].astype(BF16), rows).astype(BF16)
        here = pl.ds(start, WINDOW)
        out[here, :] = jnp.where(shown, new, out[here, :])


def patch_kernel(tile_tokens, order, count, pos, cols, patches, given, out):
    total = out.shape[0]
    slots = order.shape[0]
    visible = given.shape[0] // slots

    def base_step(i, carry):
        at = pl.multiple_of(i * 336, 16)
        here = pl.ds(at, 336)
        out[here, :] = cols[0:1, :] + patches[here, :].astype(F32) * cols[1:2, :]
        return carry

    lax.fori_loop(0, total // 336, base_step, 0)
    for slot in range(slots):
        tile = order[slot]
        start, rem = window_of(tile, tile_tokens, total)
        hot = hot_rows(pos, count[tile], tile, rem).astype(F32)
        rows = given[slot * visible : (slot + 1) * visible, :]
        new = dot(hot[:, :visible].astype(BF16), rows)
        here = pl.ds(start, WINDOW)
        out[here, :] = out[here, :] + new * cols[2:3, :]


def sincos_table(limit, full_width):
    half_width = full_width // 2
    frequency = 1.0 / 10000.0 ** (np.arange(half_width, dtype=np.float32) / half_width)
    angles = np.arange(limit, dtype=np.float32)[:, None] * frequency.astype(np.float32)
    return np.concatenate([np.sin(angles), np.cos(angles)], axis=-1).astype(np.float32)


def place_table(full_width, frames):
    part = full_width // 16 * 6
    lines = 2 * SIDE
    table = np.zeros((2 * lines + frames, full_width), np.float32)
    table[:lines, :part] = sincos_table(lines, part)
    table[lines : 2 * lines, part : 2 * part] = sincos_table(lines, part)
    table[2 * lines :, 2 * part :] = sincos_table(frames, full_width - 2 * part)
    return table


def norm_forward(full_rows, gain_vec, bias_vec):
    values = full_rows.astype(F32)
    centred = values - jnp.mean(values, axis=-1, keepdims=True)
    inverse_std = lax.rsqrt(jnp.mean(centred * centred, axis=-1, keepdims=True) + norm_eps)
    unit_rows = centred * inverse_std
    normed_low = (unit_rows * gain_vec + bias_vec).astype(BF16)
    return (unit_rows, inverse_std, normed_low)


def row_sum(values):
    return jnp.sum(values.astype(F32), axis=0, keepdims=True)


def norm_backward(out_grad, unit_rows, inverse_std, gain_vec):
    scaled = out_grad * gain_vec
    first_mean = jnp.mean(scaled, axis=-1, keepdims=True)
    cross_mean = jnp.mean(scaled * unit_rows, axis=-1, keepdims=True)
    input_grad = inverse_std * (scaled - first_mean - unit_rows * cross_mean)
    return (input_grad, row_sum(out_grad * unit_rows), row_sum(out_grad))


def prep_kernel(odd, q, k, v, attn, hid, out, dec, embed, *refs):
    biases, (first, second, first_cut, second_cut) = refs[:-4], refs[-4:]
    e, w, h = embed.shape[0], q.shape[0], hid.shape[1]
    first[:e, :] = embed[...]
    for i, ref in enumerate((q, k, v)):
        first[e + i * w : e + (i + 1) * w, :] = ref[...]
    first[e + 3 * w : e + 4 * w, :] = attn[...]
    base = e + 4 * w
    first[base:, :] = jnp.zeros((first.shape[0] - base, first.shape[1]), BF16)
    for i, ref in enumerate(biases):
        first[base + i : base + i + 1, : ref.shape[1]] = ref[...]
    second[:h, :] = hid[...].T
    second[h : 2 * h, :] = out[...]
    second[2 * h :, :] = dec[...].T
    for whole, part in ((first, first_cut), (second, second_cut)):
        half = part.shape[0]
        part[...] = whole[pl.ds(pl.multiple_of(odd[0] * half, 16), half), :]


def copy_rows(target, refs, start, count):
    for e, ref in enumerate(refs):
        target[e * count : (e + 1) * count, :] = ref[start : start + count, :]


def normed_pixels(pix, cols):
    centred = pix[...].astype(F32) - cols[0:1, :]
    return centred, (centred * cols[1:2, :]).astype(BF16)


def embed_kernel(sizes, chosen, table, cols, vecs, mask, *refs):
    n, part, rows_s = sizes
    pix, weights = blocks_of(refs[:3]), split_blocks(refs[3], refs[4], n)
    start_ref, q_ref, k_ref, v_ref, probs, att_ref, middle, full = refs[5:]
    e_rows = pix[0].shape[1]
    rows, width = start_ref.shape
    total = dot(chosen[...], table[...]) + vecs[0:1, :]
    for e in range(n):
        total = total + dot(normed_pixels(pix[e], cols)[1], weights[e][:e_rows, :])
    live = chosen[:, 127:128].astype(F32) > 0.5
    start = jnp.where(live, total, 0.0).astype(BF16)
    start_ref[...] = start
    normed = norm_forward(start, vecs[1:2, :], vecs[2:3, :])[2]
    copy_rows(full, weights, e_rows, part)
    q_ref[...] = (dot_t(normed, full[...]) + vecs[3:4, :]).astype(BF16)
    copy_rows(full, weights, e_rows + part, part)
    k_ref[...] = dot_t(normed, full[...]).astype(BF16)
    copy_rows(full, weights, e_rows + 2 * part, part)
    v_ref[...] = (dot_t(normed, full[...]) + vecs[4:5, :]).astype(BF16)
    scale = HEAD_DIM ** (-0.5)
    low = lax.broadcasted_iota(jnp.int32, (rows_s, 128), 1) < HEAD_DIM
    zero = jnp.zeros((rows_s, 128), BF16)

    def pair_step(i, carry):
        s, p = i // (width // 128), i % (width // 128)
        here = pl.ds(pl.multiple_of(s * rows_s, 16), rows_s)
        lanes = pl.ds(pl.multiple_of(p * 128, 128), 128)
        q2, k2, v2 = q_ref[here, lanes], k_ref[here, lanes], v_ref[here, lanes]
        extra = mask[pl.ds(s, 1), :]
        got = jnp.zeros((rows_s, 128), F32)
        for h in range(2):
            keep = low if h == 0 else jnp.logical_not(low)
            scores = dot_t(q2, jnp.where(keep, k2, zero)) * scale
            scores = jnp.where(extra > 0.5, scores, big_negative)
            shifted = jnp.exp(scores - jnp.max(scores, axis=-1, keepdims=True))
            share = (shifted / jnp.sum(shifted, axis=-1, keepdims=True)).astype(BF16)
            probs[i * 2 + h] = share
            got = got + dot(share, jnp.where(keep, v2, zero))
        att_ref[here, lanes] = got.astype(BF16)
        return carry

    lax.fori_loop(0, (rows // rows_s) * (width // 128), pair_step, 0)
    copy_rows(full, weights, e_rows + 3 * part, part)
    middle[...] = start_ref[...].astype(F32) + dot(att_ref[...], full[...]) + vecs[5:6, :]


def gelu_pair(x):
    cdf = 0.5 * (1.0 + lax.erf(x * (2.0**-0.5)))
    pdf = jnp.exp(-0.5 * x * x) * float(1.0 / np.sqrt(2.0 * np.pi))
    return x * cdf, cdf + x * pdf


def split_blocks(kept, sent, n):
    count = 2 * kept.shape[0] // n
    return [
        (kept if e % 2 == 0 else sent).at[e // 2 * count : (e // 2 + 1) * count] for e in range(n)
    ]


def mlp_kernel(n, middle, vecs, bias_hid, bias_dec, *refs):
    cot, weights = blocks_of(refs[:3]), split_blocks(refs[3], refs[4], n)
    rows = middle.shape[0]
    decoded = [refs[5], refs[6], refs[7].at[:rows], refs[7].at[rows:]]
    pre_refs = refs[8 : 8 + n]
    kept, sent, final_grad, sums, hidden, slope = refs[8 + n :]
    grads = split_blocks(kept, sent, n)
    h = pre_refs[0].shape[1]
    dec = decoded[0].shape[1]
    normed = norm_forward(middle[...].astype(BF16), vecs[6:7, :], vecs[7:8, :])[2]
    total = middle[...] + vecs[8:9, :]
    for e in range(n):
        pre = dot_t(normed, weights[e][:h, :]) + bias_hid[e : e + 1, :]
        value, grad = gelu_pair(pre)
        value = value.astype(BF16)
        hidden[e] = value
        slope[e] = grad.astype(BF16)
        total = total + dot(value, weights[e][h : 2 * h, :])
    final = total.astype(BF16)
    back = jnp.zeros(total.shape, F32)
    sums[...] = jnp.zeros(sums.shape, F32)
    for e in range(n):
        w_dec = weights[e][2 * h :, :]
        decoded[e][...] = (dot_t(final, w_dec) + bias_dec[e : e + 1, :]).astype(BF16)
        back = back + dot(cot[e][...], w_dec)
        grads[e][h:, :] = dot_tl(cot[e][...], final).astype(BF16)
        sums[n + 1 + e : n + 2 + e, :dec] = row_sum(cot[e][...])
    final_grad[...] = back
    low = back.astype(BF16)
    sums[n : n + 1, :] = row_sum(low)
    for e in range(n):
        grads[e][:h, :] = dot_tl(hidden[e], low).astype(BF16)
        pre_grad = (dot_t(low, weights[e][h : 2 * h, :]) * slope[e].astype(F32)).astype(BF16)
        pre_refs[e][...] = pre_grad
        sums[e : e + 1, :] = row_sum(pre_grad)


def hidden_kernel(n, middle, vecs, final_grad, *refs):
    pre, weights = refs[:n], split_blocks(refs[n], refs[n + 1], n)
    kept, sent, middle_grad, sums = refs[n + 2 :]
    grads = split_blocks(kept, sent, n)
    h = pre[0].shape[1]
    unit, rstd, normed = norm_forward(middle[...].astype(BF16), vecs[6:7, :], vecs[7:8, :])
    total = jnp.zeros(unit.shape, F32)
    for e in range(n):
        total = total + dot(pre[e][...], weights[e][:h, :])
        grads[e][...] = dot_tl(pre[e][...], normed).astype(BF16)
    term, gain, bias = norm_backward(total, unit, rstd, vecs[6:7, :])
    middle_grad[...] = final_grad[...] + term
    sums[0:1, :] = gain
    sums[1:2, :] = bias
    sums[2:8, :] = jnp.zeros((6, sums.shape[1]), F32)


def attn_back_kernel(sizes, middle_grad, start, q, k, v, probs, chosen, vecs, *refs):
    n, part, rows_s, e_rows = sizes
    weights = split_blocks(refs[0], refs[1], n)
    start_grad, dq, dk, dv, sums, full, ag = refs[2:]
    rows, width = start.shape
    copy_rows(full, weights, e_rows + 3 * part, part)
    low_grad = middle_grad[...].astype(BF16)
    ag[...] = dot_t(low_grad, full[...]).astype(BF16)
    scale = HEAD_DIM ** (-0.5)
    low = lax.broadcasted_iota(jnp.int32, (rows_s, 128), 1) < HEAD_DIM
    zero = jnp.zeros((rows_s, 128), BF16)

    def pair_step(i, carry):
        s, p = i // (width // 128), i % (width // 128)
        here = pl.ds(pl.multiple_of(s * rows_s, 16), rows_s)
        lanes = pl.ds(pl.multiple_of(p * 128, 128), 128)
        q2, k2, v2, g2 = q[here, lanes], k[here, lanes], v[here, lanes], ag[here, lanes]
        tq = jnp.zeros((rows_s, 128), F32)
        tk = jnp.zeros((rows_s, 128), F32)
        tv = jnp.zeros((rows_s, 128), F32)
        for h in range(2):
            keep = low if h == 0 else jnp.logical_not(low)
            share = probs[i * 2 + h]
            wide = share.astype(F32)
            prob_grad = dot_t(g2, jnp.where(keep, v2, zero))
            delta = jnp.sum(wide * prob_grad, axis=-1, keepdims=True)
            score_grad = (wide * (prob_grad - delta)).astype(BF16)
            tv = tv + dot_tl(share, jnp.where(keep, g2, zero))
            tq = tq + dot(score_grad, jnp.where(keep, k2, zero))
            tk = tk + dot_tl(score_grad, jnp.where(keep, q2, zero))
        dq[here, lanes] = (tq * scale).astype(BF16)
        dk[here, lanes] = (tk * scale).astype(BF16)
        dv[here, lanes] = tv.astype(BF16)
        return carry

    lax.fori_loop(0, (rows // rows_s) * (width // 128), pair_step, 0)
    copy_rows(full, weights, e_rows, part)
    total = dot(dq[...], full[...])
    copy_rows(full, weights, e_rows + part, part)
    total = total + dot(dk[...], full[...])
    copy_rows(full, weights, e_rows + 2 * part, part)
    total = total + dot(dv[...], full[...])
    unit, rstd, _ = norm_forward(start[...], vecs[1:2, :], vecs[2:3, :])
    term, gain, bias = norm_backward(total, unit, rstd, vecs[1:2, :])
    live = chosen[:, 127:128].astype(F32) > 0.5
    grad = jnp.where(live, middle_grad[...] + term, 0.0).astype(BF16)
    start_grad[...] = grad
    sums[0:1, :] = gain
    sums[1:2, :] = bias
    sums[2:3, :] = row_sum(grad)
    sums[3:4, :] = row_sum(low_grad)
    sums[4:5, :] = row_sum(dq[...])
    sums[5:6, :] = row_sum(dv[...])
    sums[6:8, :] = jnp.zeros((2, width), F32)


def pixel_grad_kernel(n, start_grad, cols, *refs):
    pix, weights = blocks_of(refs[:3]), split_blocks(refs[3], refs[4], n)
    rows = start_grad.shape[0]
    grads, bands = [refs[5], refs[6], refs[7].at[:rows], refs[7].at[rows:]], refs[8]
    e_rows = pix[0].shape[1]
    first = jnp.zeros((1, e_rows), F32)
    second = jnp.zeros((1, e_rows), F32)
    for e in range(n):
        got = dot_t(start_grad[...], weights[e][:e_rows, :])
        grads[e][...] = got.astype(BF16)
        first = first + row_sum(got)
        second = second + row_sum(got * (pix[e][...].astype(F32) - cols[0:1, :]))
    bands[...] = band_sums(first, second)


def weight_grads(n, part, base, pairs, kept, sent):
    grads = split_blocks(kept, sent, n)
    for i, (left, right) in enumerate(pairs):
        whole = dot_tl(left[...], right).astype(BF16)
        for e in range(n):
            at = base + i * part
            grads[e][at : at + part, :] = whole[e * part : (e + 1) * part, :]


def weight_kernel(sizes, start_grad, middle_grad, start, att, dq, dk, dv, cols, vecs, *refs):
    n, part = sizes
    pix, (kept, sent) = blocks_of(refs[:3]), refs[3:]
    e_rows = pix[0].shape[1]
    normed = norm_forward(start[...], vecs[1:2, :], vecs[2:3, :])[2]
    low_grad = middle_grad[...].astype(BF16)
    pairs = ((dq, normed), (dk, normed), (dv, normed), (att, low_grad))
    weight_grads(n, part, e_rows, pairs, kept, sent)
    grads = split_blocks(kept, sent, n)
    for e in range(n):
        got = dot_tl(normed_pixels(pix[e], cols)[1], start_grad[...])
        grads[e][:e_rows, :] = got.astype(BF16)


def join_kernel(half, flag, own, direct, handed, out):
    rows = own.shape[0]
    out[:rows, :] = own[...]
    at = pl.multiple_of(rows + flag[0] * half, 16)
    out[pl.ds(at, half), :] = direct[...]
    at = pl.multiple_of(rows + (1 - flag[0]) * half, 16)
    out[pl.ds(at, half), :] = handed[...]


def pack_kernel(sizes, place, mlp_sums, hid_sums, attn_sums, bands, mask_rows, out):
    n, part = sizes
    me = place[0]
    dec, width = mask_rows.shape[1], out.shape[1]
    base = 5 * n
    row = lax.broadcasted_iota(jnp.int32, (base, width), 0)
    total = jnp.zeros((base, width), F32)

    def widened(values):
        return jnp.concatenate([values, jnp.zeros((1, width - values.shape[1]), F32)], axis=1)

    for e in range(n):
        at = e ^ me
        lanes = slice(e * part, (e + 1) * part)
        total = jnp.where(row == at, mlp_sums[e : e + 1, :], total)
        total = jnp.where(row == n + at, widened(attn_sums[4:5, lanes]), total)
        total = jnp.where(row == 2 * n + at, widened(attn_sums[5:6, lanes]), total)
        total = jnp.where(row == 3 * n + at, mlp_sums[n + 1 + e : n + 2 + e, :], total)
    total = jnp.where(row == 4 * n + me, widened(mask_rows[0:1, :]), total)
    out[:base, :] = total
    out[base : base + 4, :] = attn_sums[:4, :]
    out[base + 4 : base + 6, :] = hid_sums[:2, :]
    out[base + 6 : base + 7, :] = mlp_sums[n : n + 1, :]
    out[base + 7 :, :] = jnp.zeros((out.shape[0] - base - 7, width), F32)
    out[base + 7 : base + 9, :128] = bands[:2, :]


def write_out(plan, values, outs):
    at = 0
    for out, turned in zip(outs, plan):
        if turned:
            count = out.shape[1]
            out[...] = values[at : at + count, :].T.astype(F32)
        else:
            count = out.shape[0]
            out[...] = values[at : at + count, :].astype(F32)
        at += count


def finish_kernel(half, plan, flag, own, came, *refs):
    outs, held = refs[:-1], refs[-1]
    first = flag[0] == 0

    @pl.when(first)
    def _():
        held[:half, :] = own[...]
        held[half:, :] = came[...]

    @pl.when(jnp.logical_not(first))
    def _():
        held[:half, :] = came[...]
        held[half:, :] = own[...]

    write_out(plan, held, outs)


def band_sums(first, second):
    columns = first.shape[1]
    band = lax.broadcasted_iota(jnp.int32, (columns, 128), 0) % BANDS
    pick_band = (band == lax.broadcasted_iota(jnp.int32, band.shape, 1)).astype(F32)
    rows = jnp.concatenate([first, second, jnp.zeros((6, columns), F32)], axis=0)
    return jnp.dot(rows, pick_band, precision=lax.Precision.HIGHEST, preferred_element_type=F32)


def call(kernel, outs, args, name, scratch=(), us=2.0, scalars=0):
    run = pl.pallas_call(
        kernel,
        out_shape=[jax.ShapeDtypeStruct(shape, kind) for shape, kind in outs],
        in_specs=[SM] * scalars + [VM] * (len(args) - scalars),
        out_specs=[VM] * len(outs),
        scratch_shapes=list(scratch),
        compiler_params=params(),
        cost_estimate=pl.CostEstimate(
            flops=0, bytes_accessed=int(us * 3.3e6), transcendentals=0
        ),
        name=name,
    )
    return list(run(*args))


class Weights:
    def __init__(self, own, part, data_index):
        self.own, self.half = own, part.shape[0]
        self.flag = (data_index & 1).astype(jnp.int32)[None]
        self.direct = swap(part, "mp", 2)

    def hand_on(self):
        self.handed = swap(self.direct, "dp", 1)

    def join(self, line):
        rows, width = self.own.shape
        [both] = call(
            functools.partial(join_kernel, self.half),
            [((2 * rows, width), BF16)],
            [self.flag, self.own, self.direct, line.wait(self.handed)],
            "join_weights",
            us=3.0,
            scalars=1,
        )
        line.mark(both)
        self.pair = [both, swap(both, "mp", 1)]


def to_absolute(blocks, model_index):
    size = blocks.shape[0]
    for bit in bits_of("mp"):
        turned = jnp.stack([blocks[i ^ bit] for i in range(size)])
        blocks = jnp.where((model_index & bit) != 0, turned, blocks)
    return blocks


class Line:
    def __init__(self):
        self.last = None

    def wait(self, value):
        return value if self.last is None else after(value, self.last)

    def mark(self, value):
        self.last = value


class Reduction:
    def __init__(self, kept, sent, order, data_index, line, plan, shapes, name):
        self.kept, self.came = kept, swap(sent, "mp", 1)
        self.quarters, self.line, self.name = 2, line, name
        self.plan, self.shapes = plan, shapes
        self.flags = [((data_index >> k) & 1).astype(jnp.int32)[None] for k in range(len(bits_of("dp")))]
        self.order = list(order) + [k for k in range(len(self.flags)) if k not in order]
        self.done, self.own = [], None

    def step(self):
        if self.order or self.own is None:
            self.scatter()
        elif len(self.done) > 1:
            self.gather()
        else:
            self.finish()

    def scatter(self):
        came = self.line.wait(self.came)
        axis = self.order.pop(0) if self.order else None
        rows = self.kept.shape[0] // self.quarters
        if axis is None:
            [self.own] = self.stage(came, None, 0)
            self.line.mark(self.own)
            self.came = swap(self.own, "dp", 1 << self.done[-1])
        elif axis == "x":
            self.kept, sent = self.stage(came, None, rows)
            self.line.mark(self.kept)
            self.quarters = 1
            self.came = swap(sent, "mp", 2)
        else:
            self.kept, sent = self.stage(came, self.flags[axis], rows // 2)
            self.line.mark(self.kept)
            self.done.append(axis)
            self.came = swap(sent, "dp", 1 << axis)

    def stage(self, came, flag, half):
        total, width = self.kept.shape
        quarters, rows = self.quarters, total // self.quarters
        if flag is not None and half % 16:
            summed = (self.kept.astype(F32) + came.astype(F32)).astype(BF16)
            summed = summed.reshape(quarters, rows, width)
            own = lax.dynamic_slice_in_dim(summed, flag[0] * half, half, 1)
            other = lax.dynamic_slice_in_dim(summed, (1 - flag[0]) * half, half, 1)
            return own.reshape(-1, width), other.reshape(-1, width)

        def total_of(a, b, at, count):
            here = pl.ds(at, count)
            return (a[here, :].astype(F32) + b[here, :].astype(F32)).astype(BF16)

        if flag is None:

            def kernel(a, b, *outs):
                for k, out in enumerate(outs):
                    out[...] = total_of(a, b, k * out.shape[0], out.shape[0])

            count = 1 if half == 0 else 2
            return call(
                kernel, [((total // count, width), BF16)] * count, [self.kept, came], "reduce_" + self.name
            )

        def kernel(mine, a, b, own, other):
            for q in range(quarters):
                here = slice(q * half, (q + 1) * half)
                at = pl.multiple_of(q * rows + mine[0] * half, 16)
                own[here, :] = total_of(a, b, at, half)
                at = pl.multiple_of(q * rows + (1 - mine[0]) * half, 16)
                other[here, :] = total_of(a, b, at, half)

        return call(
            kernel,
            [((total // 2, width), BF16)] * 2,
            [flag, self.kept, came],
            "reduce_" + self.name,
            scalars=1,
        )

    def gather(self):
        axis = self.done.pop()
        came = self.line.wait(self.came)
        self.own = jnp.where(
            self.flags[axis][0] == 0,
            jnp.concatenate([self.own, came], axis=0),
            jnp.concatenate([came, self.own], axis=0),
        )
        self.line.mark(self.own)
        self.came = swap(self.own, "dp", 1 << self.done[-1])

    def finish(self):
        half, width = self.own.shape
        self.result = call(
            functools.partial(finish_kernel, half, self.plan),
            [(shape, F32) for shape in self.shapes],
            [self.flags[self.done[0]], self.own, self.line.wait(self.came)],
            "finish_" + self.name,
            [pltpu.VMEM((2 * half, width), BF16)],
            us=3.0,
            scalars=1,
        )
        self.line.mark(self.result[0])


class Sums:
    def __init__(self, values, line):
        self.values, self.line = values, line
        self.left = [(axis, bit) for axis in ("mp", "dp") for bit in bits_of(axis)]
        self.came = swap(values, *self.left[0])

    def step(self):
        self.values = self.values + self.line.wait(self.came)
        self.line.mark(self.values)
        self.left.pop(0)
        if self.left:
            self.came = swap(self.values, *self.left[0])


def exchange(tiles):
    size = lax.axis_size("dp")
    blocks = tiles.reshape(size, tiles.shape[0] // size, tiles.shape[1])
    return lax.all_to_all(blocks, "dp", split_axis=0, concat_axis=0, tiled=True).reshape(tiles.shape)


def shards(
    patches,
    vis_count,
    vis_pos,
    tile_sample,
    tile_quad,
    w_embed,
    b_embed,
    norm1_gain,
    norm1_bias,
    w_query,
    b_query,
    w_key,
    w_value,
    b_value,
    w_attn_out,
    b_attn_out,
    norm2_gain,
    norm2_bias,
    w_hidden,
    b_hidden,
    w_mlp_out,
    b_mlp_out,
    w_decoder,
    b_decoder,
    mask_token,
    cotangent,
):
    data_size = lax.axis_size("dp")
    model_size = lax.axis_size("mp")
    data_index = lax.axis_index("dp")
    model_index = lax.axis_index("mp")
    tile_count = vis_count.shape[0]
    visible = vis_pos.shape[1]
    grid_count, pixel_cols = patches.shape
    tile_tokens = grid_count // tile_count
    full_width = w_embed.shape[1]
    part_width = b_embed.shape[0]
    dec_part = b_decoder.shape[0]
    hid_part = b_hidden.shape[0]
    pair_tiles = tile_count // data_size
    own_samples = SAMP_OWN // model_size
    sample_rows = 4 * visible
    rows = own_samples * sample_rows
    my_tiles = own_samples * 4
    score_scale = HEAD_DIM ** (-0.5)

    tile_ids = jnp.arange(tile_count, dtype=jnp.int32)
    owners = tile_sample // SAMP_OWN
    earlier = (owners[:, None] == owners[None, :]) & (tile_ids[None, :] < tile_ids[:, None])
    tile_ranks = jnp.sum(earlier.astype(jnp.int32), axis=1)
    slot_of = owners * pair_tiles + tile_ranks
    at_slot = slot_of[None, :] == tile_ids[:, None]
    order = jnp.sum(jnp.where(at_slot, tile_ids[None, :], 0), axis=1)
    tile_code = (tile_sample % SAMP_OWN) * 4 + tile_quad
    pos_wide = jnp.pad(vis_pos, ((0, 0), (0, 128 - visible)), constant_values=-1000)

    line = Line()
    [stats] = call(stats_kernel, [((8, 128), F32)], [patches], "band_sums", us=4.0)
    stats = stats + swap(stats, "mp", 1)
    stats = stats + swap(stats, "mp", 2)

    small = [b_embed, b_query, b_value, b_attn_out, b_mlp_out, b_decoder, b_hidden]
    base = pixel_cols + 4 * part_width
    own_first, own_second, cut_first, cut_second = call(
        prep_kernel,
        [((base + 32, full_width), BF16), ((2 * hid_part + dec_part, full_width), BF16)]
        + [(((base + 32) // 2, full_width), BF16), (((2 * hid_part + dec_part) // 2, full_width), BF16)],
        [(data_index & 1).astype(jnp.int32)[None]]
        + [w_query.T, w_key.T, w_value.T, w_attn_out, w_hidden, w_mlp_out, w_decoder]
        + [after(w_embed, stats)]
        + [v[None, :] for v in small],
        "prep_weights",
        us=5.0,
        scalars=1,
    )
    line.mark(own_first)
    first_w = Weights(own_first, cut_first, data_index)
    by_slot = jnp.where(at_slot, 1.0, 0.0)
    codes_slot = jnp.sum(by_slot * tile_code.astype(F32)[None, :], axis=1)
    counts_slot = jnp.sum(by_slot * vis_count.astype(F32)[None, :], axis=1)
    pos_slot = jnp.sum(by_slot[:, :, None] * vis_pos.astype(F32)[None, :, :], axis=1)
    info = jnp.concatenate([codes_slot[None], counts_slot[None]], axis=0)
    info = jnp.pad(info, ((0, 6), (0, 128 - tile_count)))
    packet = jnp.concatenate([stats, info, pos_slot.reshape(-1, 128)], axis=0)[None]
    for k, bit in enumerate(bits_of("dp")):
        came = swap(packet, "dp", bit)
        if k == 0:
            picked, cot_picked, mask_rows = call(
                functools.partial(pick_kernel, tile_tokens),
                [
                    ((tile_count * visible, pixel_cols), BF16),
                    ((tile_count * visible, dec_part), BF16),
                    ((8, dec_part), F32),
                ],
                [line.wait(order), vis_count, pos_wide, patches, cotangent],
                "pick_rows",
                us=7.5,
                scalars=2,
            )
            came = after(came, picked)
        packet = jnp.where(
            (data_index >> k) & 1 == 0,
            jnp.concatenate([packet, came], axis=0),
            jnp.concatenate([came, packet], axis=0),
        )

    arrived = exchange(after(picked, packet))

    second_w = Weights(own_second, after(cut_second, first_w.direct), data_index)
    first_w.hand_on()
    second_w.hand_on()

    own_info = lax.dynamic_slice_in_dim(packet[:, 8:10], data_index * pair_tiles, pair_tiles, 2)
    own_info = own_info.transpose(1, 0, 2).reshape(2, tile_count).astype(jnp.int32)
    my_tiles_bit = model_index * my_tiles
    codes = own_info[0] ^ my_tiles_bit
    line = Line()
    line.mark(second_w.direct)
    first_w.join(line)
    own, near, far = place_in(codes, line.wait(arrived), visible, model_size)
    line.mark(far)
    pix = Crossing(own, near, far)
    arrived_cot = exchange(after(cot_picked, far))
    pix.relay(line)
    own, near, far = place_in(codes, line.wait(arrived_cot), visible, model_size)
    line.mark(far)
    cot = Crossing(own, near, far)
    second_w.join(line)

    bias_rel = [first_w.pair[e % 2][e // 2 * own_first.shape[0] + base :][:16] for e in range(4)]
    bias_rel = jnp.stack(bias_rel).astype(F32)
    bias_abs = to_absolute(bias_rel, model_index)

    def rel_vec(k):
        return bias_rel[:, k, : small[k].shape[0]].reshape(1, -1)

    def abs_vec(k):
        return bias_abs[:, k, : small[k].shape[0]].reshape(1, -1)

    gains = [norm1_gain, norm1_bias, norm2_gain, norm2_bias]
    gains = [v[None].astype(F32) for v in gains]
    vecs = jnp.concatenate(
        [abs_vec(0), gains[0], gains[1], rel_vec(1), rel_vec(2), abs_vec(3)]
        + [gains[2], gains[3], abs_vec(4), jnp.zeros((7, full_width), F32)]
    )
    bias_hid, bias_dec = bias_rel[:, 6, :hid_part], bias_rel[:, 5, :dec_part]

    total = jnp.sum(packet[:, :2, :BANDS], axis=0)
    per_band = float(grid_count * data_size * (pixel_cols // BANDS) * model_size)
    band_mean = total[0] / per_band
    band_var = total[1] / per_band - band_mean * band_mean
    band_rstd = lax.rsqrt(band_var + band_eps)
    mean_cols = jnp.tile(band_mean, pixel_cols // BANDS)
    rstd_cols = jnp.tile(band_rstd, pixel_cols // BANDS)

    own_pos = packet[:, 16:].reshape(data_size, tile_count, visible)
    own_pos = lax.dynamic_slice_in_dim(own_pos, data_index * pair_tiles, pair_tiles, 1)
    own_pos = own_pos.reshape(tile_count, visible)
    mine = (codes[None, :] == jnp.arange(my_tiles)[:, None]).astype(F32)
    my_counts = jnp.sum(mine * own_info[1].astype(F32)[None, :], axis=1)
    my_pos = jnp.sum(mine[:, :, None] * own_pos[None], axis=1)
    my_pos = my_pos.astype(jnp.int32)
    live = jnp.arange(visible)[None, :] < my_counts.astype(jnp.int32)[:, None]
    live_col = live.reshape(rows, 1)
    usable = live.reshape(own_samples, sample_rows)
    quadrant = (jnp.arange(my_tiles) % 4)[:, None]
    inner = my_pos % (SIDE * SIDE)
    frames = tile_tokens // (SIDE * SIDE)
    col_at = quadrant % 2 * SIDE + inner % SIDE
    row_at = quadrant // 2 * SIDE + inner // SIDE + 2 * SIDE
    frame_at = my_pos // (SIDE * SIDE) + 4 * SIDE
    table = place_table(full_width, frames)
    high = table.astype(jnp.bfloat16)
    low = (table - high.astype(np.float32)).astype(jnp.bfloat16)
    wide = np.zeros((128, full_width), jnp.bfloat16)
    wide[: table.shape[0]], wide[64 : 64 + table.shape[0]] = high, low
    lane = jnp.arange(128)[None, :]
    spots = jnp.where(lane < 127, lane % 64, -1)
    chosen = (
        (col_at.reshape(rows, 1) == spots)
        | (row_at.reshape(rows, 1) == spots)
        | (frame_at.reshape(rows, 1) == spots)
        | ((lane == 127) & live_col)
    ).astype(BF16)
    key_mask = jnp.pad(usable.astype(F32), ((0, 8 - own_samples), (0, 0)))
    cols = jnp.pad(jnp.stack([mean_cols, rstd_cols]), ((0, 6), (0, 0)))

    square = ((rows, full_width), BF16)
    wide_rows = ((rows, full_width), F32)
    heads = own_samples * full_width // HEAD_DIM
    weight_scratch = pltpu.VMEM((full_width, full_width), BF16)
    start, queries, key_rows, value_rows, probs, attended, middle = call(
        functools.partial(embed_kernel, (model_size, part_width, sample_rows)),
        [square] * 4 + [((heads, sample_rows, sample_rows), BF16), square, wide_rows],
        [chosen, jnp.asarray(wide), cols, vecs, line.wait(key_mask)] + pix.parts + first_w.pair,
        "embed_attend",
        [weight_scratch],
        us=19.0,
    )
    line.mark(middle)
    cot.relay(line)
    decoded_shape = ((rows, dec_part), BF16)
    hidden_shape = ((rows, hid_part), BF16)
    out = call(
        functools.partial(mlp_kernel, model_size),
        [decoded_shape] * 2
        + [((2 * rows, dec_part), BF16)]
        + [hidden_shape] * model_size
        + [((2 * (hid_part + dec_part), full_width), BF16)] * 2
        + [wide_rows, ((16, full_width), F32)],
        [middle, vecs, bias_hid, bias_dec] + cot.parts + second_w.pair,
        "mlp_decode",
        [pltpu.VMEM((model_size, rows, hid_part), BF16)] * 2,
        us=20.0,
    )
    decoded_rows, pre_grads = out[:3], out[3 : 3 + model_size]
    out_kept, out_sent, final_grad, mlp_sums = out[3 + model_size :]
    red_a = Reduction(
        out_kept,
        out_sent,
        ["x", 0, 1, 2],
        data_index,
        line,
        (False, True),
        [w_mlp_out.shape, w_decoder.shape],
        "out",
    )
    out = call(
        functools.partial(hidden_kernel, model_size),
        [((2 * hid_part, full_width), BF16)] * 2 + [wide_rows, ((8, full_width), F32)],
        [middle, vecs, final_grad] + pre_grads + second_w.pair,
        "hidden_back",
        us=13.0,
    )
    hid_kept, hid_sent, middle_grad, hid_sums = out
    line.mark(middle_grad)
    red_b = Reduction(
        hid_kept, hid_sent, ["x", 0, 1, 2], data_index, line, (True,), [w_hidden.shape], "hidden"
    )
    red_a.step()
    start_grad, dq, dk, dv, attn_sums = call(
        functools.partial(attn_back_kernel, (model_size, part_width, sample_rows, pixel_cols)),
        [square] * 4 + [((8, full_width), F32)],
        [line.wait(middle_grad), start, queries, key_rows, value_rows]
        + [probs, chosen, vecs]
        + first_w.pair,
        "attend_back",
        [weight_scratch, pltpu.VMEM((rows, full_width), BF16)],
        us=18.0,
    )
    line.mark(start_grad)
    out = call(
        functools.partial(pixel_grad_kernel, model_size),
        [((rows, pixel_cols), BF16)] * 2 + [((2 * rows, pixel_cols), BF16), ((8, 128), F32)],
        [line.wait(start_grad), cols] + pix.parts + first_w.pair,
        "pixel_grad",
        us=6.7,
    )
    normed_grad, bands = out[:3], out[3]
    line.mark(bands)
    grad_mp = Crossing(*normed_grad)
    red_a.step()
    first_kept, first_sent = call(
        functools.partial(weight_kernel, (model_size, part_width)),
        [((2 * base, full_width), BF16)] * 2,
        [line.wait(start_grad), middle_grad, start, attended, dq, dk, dv, cols, vecs] + pix.parts,
        "weight_grad",
        us=10.0,
    )
    line.mark(first_kept)
    grad_mp.relay(line)
    [sums] = call(
        functools.partial(pack_kernel, (model_size, part_width)),
        [((32, full_width), F32)],
        [model_index.astype(jnp.int32)[None], mlp_sums, hid_sums, attn_sums, line.wait(bands)]
        + [mask_rows],
        "pack_sums",
        us=1.5,
        scalars=1,
    )
    line.mark(sums)
    sums = Sums(sums, line)
    red_c = Reduction(
        first_kept,
        first_sent,
        ["x", 0, 1, 2],
        data_index,
        line,
        (False,) * 5,
        [w_embed.shape] + [w_attn_out.shape] * 4,
        "first",
    )

    def go_home(crossing):
        parts = crossing.parts
        tiles = place_out(codes, [parts[0], line.wait(parts[1]), parts[2]], visible)
        line.mark(tiles)
        return exchange(tiles)

    def patch_step():
        bands_all = sums.values[5 * model_size + 7 : 5 * model_size + 9, :BANDS]
        grad_all, cross_all = bands_all[0], bands_all[1]
        grad_var = -0.5 * cross_all * band_rstd * band_rstd * band_rstd
        grad_mean = -band_rstd * grad_all - 2.0 * band_mean * grad_var
        terms = jnp.stack([grad_mean / per_band, 2.0 * grad_var / per_band, band_rstd])
        terms = jnp.pad(jnp.tile(terms, (1, pixel_cols // BANDS)), ((0, 5), (0, 0)))
        out = call(
            functools.partial(patch_kernel, tile_tokens),
            [((grid_count, pixel_cols), F32)],
            [order, vis_count, pos_wide, terms, patches, line.wait(grad_dp)],
            "spread_patch_grad",
            us=8.0,
            scalars=2,
        )
        line.mark(out[0])
        return out

    def decoded_step():
        out = call(
            functools.partial(spread_kernel, tile_tokens),
            [((grid_count, dec_part), BF16)],
            [order, vis_count, pos_wide, mask_token[None, :], line.wait(decoded_dp)],
            "spread_decoded",
            us=3.5,
            scalars=2,
        )
        line.mark(out[0])
        return out

    def steps(*chains):
        for chain in chains:
            chain.step()

    steps(sums)
    grad_dp = go_home(grad_mp)
    steps(sums, red_c, red_a, red_b, sums, red_a, sums, red_a)
    while sums.left:
        sums.step()
    steps(red_c, red_a, red_a, red_c, red_b)
    [patch_grad] = patch_step()
    steps(red_c, red_b, red_a, red_c, red_b, red_c)
    decoded_mp = Crossing(decoded_rows[0], decoded_rows[1], line.wait(decoded_rows[2]))
    steps(red_b, red_c)
    decoded_mp.relay(line)
    steps(red_b)
    decoded_dp = go_home(decoded_mp)
    steps(red_b)
    while not all(hasattr(chain, "result") for chain in (red_a, red_b, red_c)):
        for chain in (red_a, red_c, red_b):
            if not hasattr(chain, "result"):
                chain.step()
    [decoded] = decoded_step()

    n = model_size
    sums = sums.values
    own_rows = [
        lax.dynamic_slice_in_dim(sums, model_index + k * n, 1, 0)[0] for k in range(5)
    ]
    sum_hidden = own_rows[0]
    sum_query, sum_value = own_rows[1][:part_width], own_rows[2][:part_width]
    sum_dec, grad_mask_token = own_rows[3][:dec_part], own_rows[4][:dec_part]
    gain_one, bias_one, embed_sum, attn_out_sum, gain_two, bias_two, mlp_out_sum = (
        sums[5 * n + k] for k in range(7)
    )

    def mine_of(vector):
        part = vector.shape[0] // model_size
        return lax.dynamic_slice_in_dim(vector, model_index * part, part, 0)

    (g_out, g_dec), [g_hid] = red_a.result, red_b.result
    g_embed, g_query, g_key, g_value, g_attn = red_c.result

    return (
        decoded,
        patch_grad,
        g_embed,
        mine_of(embed_sum),
        gain_one,
        bias_one,
        g_query.T,
        sum_query,
        g_key.T,
        g_value.T,
        sum_value,
        g_attn,
        mine_of(attn_out_sum),
        gain_two,
        bias_two,
        g_hid,
        sum_hidden,
        g_out,
        mine_of(mlp_out_sum),
        g_dec,
        sum_dec,
        grad_mask_token,
    )


def solution(mesh):
    in_specs = (
        P("dp", "mp"),
        P("dp"),
        P("dp", None),
        P("dp"),
        P("dp"),
        P("mp", None),
        P("mp"),
        P(),
        P(),
        P(None, "mp"),
        P("mp"),
        P(None, "mp"),
        P(None, "mp"),
        P("mp"),
        P("mp", None),
        P("mp"),
        P(),
        P(),
        P(None, "mp"),
        P("mp"),
        P("mp", None),
        P("mp"),
        P(None, "mp"),
        P("mp"),
        P("mp"),
        P("dp", "mp"),
    )
    out_specs = (
        P("dp", "mp"),
        P("dp", "mp"),
        P("mp", None),
        P("mp"),
        P(),
        P(),
        P(None, "mp"),
        P("mp"),
        P(None, "mp"),
        P(None, "mp"),
        P("mp"),
        P("mp", None),
        P("mp"),
        P(),
        P(),
        P(None, "mp"),
        P("mp"),
        P("mp", None),
        P("mp"),
        P(None, "mp"),
        P("mp"),
        P("mp"),
    )
    return jax.shard_map(shards, mesh=mesh, in_specs=in_specs, out_specs=out_specs, check_vma=False)
```

time: 822 us -> 518 us (0.63)
  Pallas kernels: 0 us -> 186 us
  other arithmetic: 129 us -> 9.11 us
  blocking collectives: 118 us -> 0 us
  matrix products: 110 us -> 0 us
  waiting for transfers between devices: 289 us -> 196 us
  local copies, waits for them, and re-layouts: 131 us -> 41.4 us
  starting transfers between devices: 23.1 us -> 77.5 us
  between operations: 16.4 us -> 1.73 us
    ppermute x0 -> x48, waiting for transfers between devices: none -> 191 us  [swap(): return lax.ppermute(values, axis, [(i, i ^ bit) for i in range(size)])]
    pallas_call x0 -> x36, Pallas kernels: none -> 186 us  [call(): return list(run(*args))]
    dot_general x30 -> x0, matrix products: 110 us -> none  [the longest x1 20.1 us: shards(): jnp.dot(final_grad_full, w_mlp_out.T, preferred_element_type=jnp.float32)]
    psum x3 -> x0, blocking collectives: 100 us -> none  [the longest x1 42 us: shards(): first_all, second_all = lax.psum((first_sum, second_sum), ('dp', 'mp'))]
    psum x3 -> x0, waiting for transfers between devices: 92.6 us -> none  [the longest x2 77 us: whole_sum(): lax.psum((term_rows + bias_full).astype(jnp.bfloat16), 'mp')]
    unnamed x14 -> x0, waiting for transfers between devices: 73.7 us -> none
    all_gather x4 -> x0, waiting for transfers between devices: 65.9 us -> none  [the longest x2 47.9 us: widen_grad(): return lax.all_gather(part_rows, 'mp', axis=1, tiled=True)]
    ppermute x0 -> x48, starting transfers between devices: none -> 57.6 us  [swap(): return lax.ppermute(values, axis, [(i, i ^ bit) for i in range(size)])]
  transfers between devices with their start and end apart: 15 -> 52, of which waited for: 13 -> 25; matrix products, arithmetic and copies ran while one was open for 30% -> 5% of each run, Pallas kernels for 0% -> 28%
where the time goes in v1:
time: 518 us; the launch traced here: 512 us
  waiting for transfers between devices  196 us (38%)
  Pallas kernels  186 us (36%)
  starting transfers between devices  77.5 us (15%)
  local copies, waits for them, and re-layouts  41.4 us (8%)
  other arithmetic  9.11 us (2%)
    ppermute x48, waiting for transfers between devices, swap(): return lax.ppermute(values, axis, [(i, i ^ bit) for i in range(size)])  191 us
    pallas_call x36, Pallas kernels, call(): return list(run(*args))  186 us
    ppermute x48, starting transfers between devices, swap(): return lax.ppermute(values, axis, [(i, i ^ bit) for i in range(size)])  57.6 us
    unnamed x119, local copies, waits for them, and re-layouts  23 us
    all_to_all x4, starting transfers between devices, exchange(): lax.all_to_all(blocks, 'dp', split_axis=0, concat_axis=0, tiled=True)  20 us
  transfers between devices with their start and end apart: 52, of which 25 were waited for; matrix products, arithmetic and copies ran while one was open for 5% of the time, Pallas kernels for 28%

profile of v1, /device:TPU:0, one launch (start us, length us, event | category | flops | bytes accessed | tf_op | source)
XLA Modules:
  0.0 512.1 jit_solution(1881886445299792102)
XLA Ops:
  23.7 7.3 %pick_rows.1 = (bf16[2048,384]{1,0:T(8,128)(2,1)}, bf16[2048,128]{1,0:T(8,128)(2,1)}, f32[8,128]{1,0:T(8,128)}) custom-call(s32[32]{0:T(128)} %select_reduce_fusion.order, s32[32]{0:T(128)} %count.5, s32[32,128]{1,0:T(8,128)} %pad.23.pos, bf16[4704,384]{1,0:T(8,128)(2,1)} %patches.5, bf16[4704,128]{1,0:T(8,128)(2,1)} %cot.1), custom_call_target="tpu_custom_call" | custom-call | bytes 24750000 | tf_op jit(solution)/shard_map/pick_rows/pallas_call | solution.py:571
  40.4 5.6 %all-to-all-start = ((bf16[8,256,384]{2,1,0:T(8,128)(2,1)}), bf16[8,256,384]{2,1,0:T(8,128)(2,1)S(1)}, u32[]{:S(2)}, u32[]{:S(2)}) async-start(bf16[8,256,384]{2,1,0:T(8,128)(2,1)} %bitcast.56), calls=%async_computation | async-start | bytes 3145728 | tf_op jit(solution)/shard_map/all_to_all | solution.py:735
  47.6 18.6 %collective-permute-done.5.direct = bf16[592,768]{1,0:T(8,128)(2,1)} collective-permute-done((bf16[592,768]{1,0:T(8,128)(2,1)S(1)}, bf16[592,768]{1,0:T(8,128)(2,1)}, u32[]{:S(2)}, u32[]{:S(2)}) %collective-permute-start.5) | collective-permute-done | bytes 909344 | tf_op jit(solution)/shard_map/ppermute | solution.py:35
  69.7 22.1 %collective-permute-done.7.direct = bf16[832,768]{1,0:T(8,128)(2,1)S(1)} collective-permute-done((bf16[832,768]{1,0:T(8,128)(2,1)}, bf16[832,768]{1,0:T(8,128)(2,1)S(1)}, u32[]{:S(2)}, u32[]{:S(2)}) %collective-permute-start.7) | collective-permute-done | bytes 1277984 | tf_op jit(solution)/shard_map/ppermute | solution.py:35
  108.5 7.1 %collective-permute-done.10.refs_2_ = bf16[1024,384]{1,0:T(8,128)(2,1)S(1)} collective-permute-done((bf16[1024,384]{1,0:T(8,128)(2,1)}, bf16[1024,384]{1,0:T(8,128)(2,1)S(1)}, u32[]{:S(2)}, u32[]{:S(2)}) %collective-permute-start.10) | collective-permute-done | bytes 786464 | tf_op jit(solution)/shard_map/ppermute | solution.py:35
  140.2 19.0 %embed_attend.1 = (bf16[512,768]{1,0:T(8,128)(2,1)}, bf16[512,768]{1,0:T(8,128)(2,1)}, bf16[512,768]{1,0:T(8,128)(2,1)}, bf16[512,768]{1,0:T(8,128)(2,1)}, bf16[...) custom-call(bf16[512,128]{1,0:T(8,128)(2,1)} %or_convert_fusion.chosen, ...), custom_call_target="tpu_custom_call" | custom-call | bytes 62700000 | tf_op jit(solution)/shard_map/embed_attend/pallas_call | solution.py:571
  161.5 19.0 %mlp_decode.1 = (bf16[512,128]{1,0:T(8,128)(2,1)}, bf16[512,128]{1,0:T(8,128)(2,1)}, bf16[1024,128]{1,0:T(8,128)(2,1)}, bf16[512,768]{1,0:T(8,128)(2,1)}, bf16[5...) custom-call(f32[512,768]{1,0:T(8,128)} %get-tuple-element.174.middle, ...), custom_call_target="tpu_custom_call" | custom-call | bytes 66000000 | tf_op jit(solution)/shard_map/mlp_decode/pallas_call | solution.py:571
  180.7 13.3 %hidden_back.1 = (bf16[1536,768]{1,0:T(8,128)(2,1)}, bf16[1536,768]{1,0:T(8,128)(2,1)}, f32[512,768]{1,0:T(8,128)}, f32[8,768]{1,0:T(8,128)}) custom-call(f32[512,768]{1,0:T(8,128)} %get-tuple-element.174.middle, f32[16,768]{1,0:T(8,128)} %concatenate.83.vecs, f32[512,768]{1,0:T(8,128)} %get-tuple-element.181.final_grad, ...), custom_call_target="tpu_custom_call" | custom-call | bytes 42900000 | tf_op jit(solution)/shard_map/hidden_back/pallas_call | solution.py:571
  201.5 18.1 %attend_back.1 = (bf16[512,768]{1,0:T(8,128)(2,1)}, bf16[512,768]{1,0:T(8,128)(2,1)}, bf16[512,768]{1,0:T(8,128)(2,1)}, bf16[512,768]{1,0:T(8,128)(2,1)}, f32[8,768]{1,0:T(8,128)}) custom-call(f32[512,768]{1,0:T(8,128)} %get-tuple-element.191.middle_grad, bf16[512,768]{1,0:T(8,128)(2,1)} %get-tuple-element.192.start, bf16[512,768]{1,0:T(8,128)(2,1)} %get-tuple-element.193.q, ...), custom_call_target="tpu_custom_call" | custom-call | bytes 59400000 | tf_op jit(solution)/shard_map/attend_back/pallas_call | solution.py:571
  219.7 6.7 %pixel_grad.1 = (bf16[512,384]{1,0:T(8,128)(2,1)}, bf16[512,384]{1,0:T(8,128)(2,1)}, bf16[1024,384]{1,0:T(8,128)(2,1)}, f32[8,128]{1,0:T(8,128)}) custom-call(bf16[512,768]{1,0:T(8,128)(2,1)} %get-tuple-element.203.start_grad, f32[8,384]{1,0:T(8,128)} %select_maximum_fusion.cols, bf16[512,384]{1,0:T(8,128)(2,1)} %get-tuple-element.173.refs_0_, ...), custom_call_target="tpu_custom_call" | custom-call | bytes 22110000 | tf_op jit(solution)/shard_map/pixel_grad/pallas_call | solution.py:571
  226.4 6.4 %collective-permute-done.16.b = bf16[896,768]{1,0:T(8,128)(2,1)S(1)} collective-permute-done((bf16[896,768]{1,0:T(8,128)(2,1)}, bf16[896,768]{1,0:T(8,128)(2,1)S(1)}, u32[]{:S(2)}, u32[]{:S(2)}) %collective-permute-start.16) | collective-permute-done | bytes 1376288 | tf_op jit(solution)/shard_map/ppermute | solution.py:35
  236.9 10.5 %weight_grad.1 = (bf16[2304,768]{1,0:T(8,128)(2,1)}, bf16[2304,768]{1,0:T(8,128)(2,1)}) custom-call(bf16[512,768]{1,0:T(8,128)(2,1)} %get-tuple-element.203.start_grad, f32[512,768]{1,0:T(8,128)} %get-tuple-element.191.middle_grad, bf16[512,768]{1,0:T(8,128)(2,1)} %get-tuple-element.192.start, bf16[512,768]{1,0:T(8,128)(2,1)} %get-tuple-element.204.att, ...), custom_call_target="tpu_custom_call" | custom-call | bytes 33000000 | tf_op jit(solution)/shard_map/weight_grad/pallas_call | solution.py:571
  249.1 18.3 %collective-permute-done.18.far = bf16[1024,384]{1,0:T(8,128)(2,1)S(1)} collective-permute-done((bf16[1024,384]{1,0:T(8,128)(2,1)S(1)}, bf16[1024,384]{1,0:T(8,128)(2,1)S(1)}, u32[]{:S(2)}, u32[]{:S(2)}) %collective-permute-start.18) | collective-permute-done | bytes 786464 | tf_op jit(solution)/shard_map/ppermute | solution.py:35
  285.5 5.8 %all-to-all-start.2 = ((bf16[8,256,384]{2,1,0:T(8,128)(2,1)}), bf16[8,256,384]{2,1,0:T(8,128)(2,1)S(1)}, u32[]{:S(2)}, u32[]{:S(2)}) async-start(bf16[8,256,384]{2,1,0:T(8,128)(2,1)} %bitcast.26), calls=%async_computation.2 | async-start | bytes 3145728 | tf_op jit(solution)/shard_map/all_to_all | solution.py:735
  293.4 31.2 %collective-permute-done.25.b = bf16[448,768]{1,0:T(8,128)(2,1)S(1)} collective-permute-done((bf16[448,768]{1,0:T(8,128)(2,1)}, bf16[448,768]{1,0:T(8,128)(2,1)S(1)}, u32[]{:S(2)}, u32[]{:S(2)}) %collective-permute-start.25) | collective-permute-done | bytes 688160 | tf_op jit(solution)/shard_map/ppermute | solution.py:35
  343.9 8.1 %collective-permute-done.29.b = bf16[112,768]{1,0:T(8,128)(2,1)S(1)} collective-permute-done((bf16[112,768]{1,0:T(8,128)(2,1)}, bf16[112,768]{1,0:T(8,128)(2,1)S(1)}, u32[]{:S(2)}, u32[]{:S(2)}) %collective-permute-start.29) | collective-permute-done | bytes 172064 | tf_op jit(solution)/shard_map/ppermute | solution.py:35
  360.1 9.1 %collective-permute-done.31 = bf16[112,768]{1,0:T(8,128)(2,1)S(1)} collective-permute-done((bf16[112,768]{1,0:T(8,128)(2,1)S(1)}, bf16[112,768]{1,0:T(8,128)(2,1)S(1)}, u32[]{:S(2)}, u32[]{:S(2)}) %collective-permute-start.31) | collective-permute-done | bytes 172064 | tf_op jit(solution)/shard_map/ppermute | solution.py:35
  369.3 8.6 %collective-permute-done.32 = bf16[224,768]{1,0:T(8,128)(2,1)S(1)} collective-permute-done((bf16[224,768]{1,0:T(8,128)(2,1)S(1)}, bf16[224,768]{1,0:T(8,128)(2,1)S(1)}, u32[]{:S(2)}, u32[]{:S(2)}) %collective-permute-start.32) | collective-permute-done | bytes 344096 | tf_op jit(solution)/shard_map/ppermute | solution.py:35
  392.3 8.0 %spread_patch_grad.1 = f32[4704,384]{1,0:T(8,128)} custom-call(s32[32]{0:T(128)} %select_reduce_fusion.order, s32[32]{0:T(128)} %count.5, s32[32,128]{1,0:T(8,128)} %pad.23.pos, f32[8,384]{1,0:T(8,128)} %pad.28.cols, bf16[4704,384]{1,0:T(8,128)(2,1)} %patches.5, bf16[2048,384]{1,0:T(8,128)(2,1)} %bitcast.51), custom_call_target="tpu_custom_call" | custom-call | bytes 26400000 | tf_op jit(solution)/shard_map/spread_patch_grad/pallas_call | solution.py:571
  424.0 5.7 %collective-permute-done.38 = bf16[144,768]{1,0:T(8,128)(2,1)S(1)} collective-permute-done((bf16[144,768]{1,0:T(8,128)(2,1)}, bf16[144,768]{1,0:T(8,128)(2,1)S(1)}, u32[]{:S(2)}, u32[]{:S(2)}) %collective-permute-start.38) | collective-permute-done | bytes 221216 | tf_op jit(solution)/shard_map/ppermute | solution.py:35
  433.9 9.6 %collective-permute-done.42.b = bf16[96,768]{1,0:T(8,128)(2,1)S(1)} collective-permute-done((bf16[96,768]{1,0:T(8,128)(2,1)}, bf16[96,768]{1,0:T(8,128)(2,1)S(1)}, u32[]{:S(2)}, u32[]{:S(2)}) %collective-permute-start.42) | collective-permute-done | bytes 147488 | tf_op jit(solution)/shard_map/ppermute | solution.py:35
  449.5 6.2 %collective-permute-done.44 = bf16[96,768]{1,0:T(8,128)(2,1)S(1)} collective-permute-done((bf16[96,768]{1,0:T(8,128)(2,1)}, bf16[96,768]{1,0:T(8,128)(2,1)S(1)}, u32[]{:S(2)}, u32[]{:S(2)}) %collective-permute-start.44) | collective-permute-done | bytes 147488 | tf_op jit(solution)/shard_map/ppermute | solution.py:35
  472.3 20.0 %collective-permute-done.47.came = bf16[576,768]{1,0:T(8,128)(2,1)S(1)} collective-permute-done((bf16[576,768]{1,0:T(8,128)(2,1)S(1)}, bf16[576,768]{1,0:T(8,128)(2,1)S(1)}, u32[]{:S(2)}, u32[]{:S(2)}) %collective-permute-start.47) | collective-permute-done | bytes 884768 | tf_op jit(solution)/shard_map/ppermute | solution.py:35
  496.6 7.2 %collective-permute-done.46.came = bf16[384,768]{1,0:T(8,128)(2,1)S(1)} collective-permute-done((bf16[384,768]{1,0:T(8,128)(2,1)S(1)}, bf16[384,768]{1,0:T(8,128)(2,1)S(1)}, u32[]{:S(2)}, u32[]{:S(2)}) %collective-permute-start.46) | collective-permute-done | bytes 589856 | tf_op jit(solution)/shard_map/ppermute | solution.py:35
  (353 shorter events, 218.9 us)
Async XLA Ops:
  11.5 19.6 %collective-permute-start.2 = (f32[1,32,128]{2,0,1:T(1,128)S(1)}, f32[1,32,128]{2,0,1:T(1,128)S(1)}, u32[]{:S(2)}, u32[]{:S(2)}) collective-permute-start(f32[1,32,128]{2,0,1:T(1,128)S(1)} %bitcast.61), channel_id=1, source_target_pairs={{0,4},{4,0},{8,12},{12,8},{16,20},{20,16},{24,28},{28,24},{1,5},{5... | collective-permute-start | bytes 49160 | tf_op jit(solution)/shard_map/ppermute | solution.py:35
  40.4 57.8 %all-to-all-start = ((bf16[8,256,384]{2,1,0:T(8,128)(2,1)}), bf16[8,256,384]{2,1,0:T(8,128)(2,1)S(1)}, u32[]{:S(2)}, u32[]{:S(2)}) async-start(bf16[8,256,384]{2,1,0:T(8,128)(2,1)} %bitcast.56), calls=%async_computation | async-start | bytes 3145728 | tf_op jit(solution)/shard_map/all_to_all | solution.py:735
  46.0 20.2 %collective-permute-start.5 = (bf16[592,768]{1,0:T(8,128)(2,1)S(1)}, bf16[592,768]{1,0:T(8,128)(2,1)}, u32[]{:S(2)}, u32[]{:S(2)}) collective-permute-start(bf16[592,768]{1,0:T(8,128)(2,1)S(1)} %copy-done.50), channel_id=1, source_target_pairs={{0,2},{1,3},{2,0},{3,1},{4,6},{5,7},{6,4},{7,5},{8,10},{9,11},{10,... | collective-permute-start | bytes 2727944 | tf_op jit(solution)/shard_map/ppermute | solution.py:35
  66.2 25.5 %collective-permute-start.7 = (bf16[832,768]{1,0:T(8,128)(2,1)}, bf16[832,768]{1,0:T(8,128)(2,1)S(1)}, u32[]{:S(2)}, u32[]{:S(2)}) collective-permute-start(bf16[832,768]{1,0:T(8,128)(2,1)} %get-tuple-element.159), channel_id=1, source_target_pairs={{0,2},{1,3},{2,0},{3,1},{4,6},{5,7},{6,4},{7,5},{8,10},{9,11},{10,... | collective-permute-start | bytes 3833864 | tf_op jit(solution)/shard_map/ppermute | solution.py:35
  67.7 26.4 %collective-permute-start.6 = (bf16[592,768]{1,0:T(8,128)(2,1)}, bf16[592,768]{1,0:T(8,128)(2,1)}, u32[]{:S(2)}, u32[]{:S(2)}) collective-permute-start(bf16[592,768]{1,0:T(8,128)(2,1)} %collective-permute-done.5.direct), channel_id=1, source_target_pairs={{0,4},{4,0},{8,12},{12,8},{16,20},{20,16},{24,28},{28,24},{1,5},{5... | collective-permute-start | bytes 2727944 | tf_op jit(solution)/shard_map/ppermute | solution.py:35
  91.7 32.7 %collective-permute-start.9 = (bf16[832,768]{1,0:T(8,128)(2,1)S(1)}, bf16[832,768]{1,0:T(8,128)(2,1)}, u32[]{:S(2)}, u32[]{:S(2)}) collective-permute-start(bf16[832,768]{1,0:T(8,128)(2,1)S(1)} %collective-permute-done.7.direct), channel_id=1, source_target_pairs={{0,4},{4,0},{8,12},{12,8},{16,20},{20,16},{24,28},{28,24},{1,5},{5... | collective-permute-start | bytes 3833864 | tf_op jit(solution)/shard_map/ppermute | solution.py:35
  108.4 28.2 %collective-permute-start.8 = (bf16[2368,768]{1,0:T(8,128)(2,1)}, bf16[2368,768]{1,0:T(8,128)(2,1)}, u32[]{:S(2)}, u32[]{:S(2)}) collective-permute-start(bf16[2368,768]{1,0:T(8,128)(2,1)} %join_weights.2.refs_3_.refs_0_), channel_id=1, source_target_pairs={{0,1},{1,0},{2,3},{3,2},{4,5},{5,4},{6,7},{7,6},{8,9},{9,8},{10,11... | collective-permute-start | bytes 10911752 | tf_op jit(solution)/shard_map/ppermute | solution.py:35
  129.7 31.2 %collective-permute-start.14 = (bf16[3328,768]{1,0:T(8,128)(2,1)}, bf16[3328,768]{1,0:T(8,128)(2,1)}, u32[]{:S(2)}, u32[]{:S(2)}) collective-permute-start(bf16[3328,768]{1,0:T(8,128)(2,1)} %join_weights.3.refs_3_.refs_4_), channel_id=1, source_target_pairs={{0,1},{1,0},{2,3},{3,2},{4,5},{5,4},{6,7},{7,6},{8,9},{9,8},{10,11... | collective-permute-start | bytes 15335432 | tf_op jit(solution)/shard_map/ppermute | solution.py:35
  135.2 24.0 %collective-permute-start.12 = (bf16[1024,128]{1,0:T(8,128)(2,1)S(1)}, bf16[1024,128]{1,0:T(8,128)(2,1)S(1)}, u32[]{:S(2)}, u32[]{:S(2)}) collective-permute-start(bf16[1024,128]{1,0:T(8,128)(2,1)S(1)} %copy-done.53), channel_id=1, source_target_pairs={{0,2},{1,3},{2,0},{3,1},{4,6},{5,7},{6,4},{7,5},{8,10},{9,11},{10,... | collective-permute-start | bytes 786440 | tf_op jit(solution)/shard_map/ppermute | solution.py:35
  200.1 32.6 %collective-permute-start.16 = (bf16[896,768]{1,0:T(8,128)(2,1)}, bf16[896,768]{1,0:T(8,128)(2,1)S(1)}, u32[]{:S(2)}, u32[]{:S(2)}) collective-permute-start(bf16[896,768]{1,0:T(8,128)(2,1)} %get-tuple-element.198), channel_id=1, source_target_pairs={{0,2},{1,3},{2,0},{3,1},{4,6},{5,7},{6,4},{7,5},{8,10},{9,11},{10,... | collective-permute-start | bytes 4128776 | tf_op jit(solution)/shard_map/ppermute | solution.py:35
  247.4 29.7 %collective-permute-start.17 = (bf16[2304,768]{1,0:T(8,128)(2,1)}, bf16[2304,768]{1,0:T(8,128)(2,1)S(1)}, u32[]{:S(2)}, u32[]{:S(2)}) collective-permute-start(bf16[2304,768]{1,0:T(8,128)(2,1)} %get-tuple-element.209), channel_id=1, source_target_pairs={{0,1},{1,0},{2,3},{3,2},{4,5},{5,4},{6,7},{7,6},{8,9},{9,8},{10,11... | collective-permute-start | bytes 10616840 | tf_op jit(solution)/shard_map/ppermute | solution.py:35
  247.4 20.0 %collective-permute-start.18 = (bf16[1024,384]{1,0:T(8,128)(2,1)S(1)}, bf16[1024,384]{1,0:T(8,128)(2,1)S(1)}, u32[]{:S(2)}, u32[]{:S(2)}) collective-permute-start(bf16[1024,384]{1,0:T(8,128)(2,1)S(1)} %copy-done.51), channel_id=1, source_target_pairs={{0,2},{1,3},{2,0},{3,1},{4,6},{5,7},{6,4},{7,5},{8,10},{9,11},{10,... | collective-permute-start | bytes 2359304 | tf_op jit(solution)/shard_map/ppermute | solution.py:35
  248.9 80.8 %collective-permute-start.24 = (bf16[1536,768]{1,0:T(8,128)(2,1)}, bf16[1536,768]{1,0:T(8,128)(2,1)}, u32[]{:S(2)}, u32[]{:S(2)}) collective-permute-start(bf16[1536,768]{1,0:T(8,128)(2,1)} %get-tuple-element.226), channel_id=1, source_target_pairs={{0,1},{1,0},{2,3},{3,2},{4,5},{5,4},{6,7},{7,6},{8,9},{9,8},{10,11... | collective-permute-start | bytes 7077896 | tf_op jit(solution)/shard_map/ppermute | solution.py:35
  284.3 70.1 %collective-permute-start.22 = (bf16[1152,768]{1,0:T(8,128)(2,1)}, bf16[1152,768]{1,0:T(8,128)(2,1)S(1)}, u32[]{:S(2)}, u32[]{:S(2)}) collective-permute-start(bf16[1152,768]{1,0:T(8,128)(2,1)} %get-tuple-element.224), channel_id=1, source_target_pairs={{0,2},{1,3},{2,0},{3,1},{4,6},{5,7},{6,4},{7,5},{8,10},{9,11},{10,... | collective-permute-start | bytes 5308424 | tf_op jit(solution)/shard_map/ppermute | solution.py:35
  285.5 105.7 %all-to-all-start.2 = ((bf16[8,256,384]{2,1,0:T(8,128)(2,1)}), bf16[8,256,384]{2,1,0:T(8,128)(2,1)S(1)}, u32[]{:S(2)}, u32[]{:S(2)}) async-start(bf16[8,256,384]{2,1,0:T(8,128)(2,1)} %bitcast.26), calls=%async_computation.2 | async-start | bytes 3145728 | tf_op jit(solution)/shard_map/all_to_all | solution.py:735
  291.3 33.3 %collective-permute-start.25 = (bf16[448,768]{1,0:T(8,128)(2,1)}, bf16[448,768]{1,0:T(8,128)(2,1)S(1)}, u32[]{:S(2)}, u32[]{:S(2)}) collective-permute-start(bf16[448,768]{1,0:T(8,128)(2,1)} %get-tuple-element.227), channel_id=1, source_target_pairs={{0,4},{4,0},{8,12},{12,8},{16,20},{20,16},{24,28},{28,24},{1,5},{5... | collective-permute-start | bytes 2064392 | tf_op jit(solution)/shard_map/ppermute | solution.py:35
  333.8 50.6 %collective-permute-start.34 = (bf16[768,768]{1,0:T(8,128)(2,1)}, bf16[768,768]{1,0:T(8,128)(2,1)S(1)}, u32[]{:S(2)}, u32[]{:S(2)}) collective-permute-start(bf16[768,768]{1,0:T(8,128)(2,1)} %get-tuple-element.248), channel_id=1, source_target_pairs={{0,2},{1,3},{2,0},{3,1},{4,6},{5,7},{6,4},{7,5},{8,10},{9,11},{10,... | collective-permute-start | bytes 3538952 | tf_op jit(solution)/shard_map/ppermute | solution.py:35
  359.1 21.9 %collective-permute-start.30 = (bf16[576,768]{1,0:T(8,128)(2,1)}, bf16[576,768]{1,0:T(8,128)(2,1)S(1)}, u32[]{:S(2)}, u32[]{:S(2)}) collective-permute-start(bf16[576,768]{1,0:T(8,128)(2,1)} %get-tuple-element.242), channel_id=1, source_target_pairs={{0,4},{4,0},{8,12},{12,8},{16,20},{20,16},{24,28},{28,24},{1,5},{5... | collective-permute-start | bytes 2654216 | tf_op jit(solution)/shard_map/ppermute | solution.py:35
  378.2 33.6 %collective-permute-start.36 = (bf16[448,768]{1,0:T(8,128)(2,1)S(1)}, bf16[448,768]{1,0:T(8,128)(2,1)S(1)}, u32[]{:S(2)}, u32[]{:S(2)}) collective-permute-start(bf16[448,768]{1,0:T(8,128)(2,1)S(1)} %maximum_select_fusion.1.own), channel_id=1, source_target_pairs={{0,4},{4,0},{8,12},{12,8},{16,20},{20,16},{24,28},{28,24},{1,5},{5... | collective-permute-start | bytes 2064392 | tf_op jit(solution)/shard_map/ppermute | solution.py:35
  388.5 19.6 %collective-permute-start.37 = (bf16[384,768]{1,0:T(8,128)(2,1)}, bf16[384,768]{1,0:T(8,128)(2,1)S(1)}, u32[]{:S(2)}, u32[]{:S(2)}) collective-permute-start(bf16[384,768]{1,0:T(8,128)(2,1)} %get-tuple-element.255), channel_id=1, source_target_pairs={{0,4},{4,0},{8,12},{12,8},{16,20},{20,16},{24,28},{28,24},{1,5},{5... | collective-permute-start | bytes 1769480 | tf_op jit(solution)/shard_map/ppermute | solution.py:35
  430.9 18.2 %collective-permute-start.41 = (bf16[288,768]{1,0:T(8,128)(2,1)S(1)}, bf16[288,768]{1,0:T(8,128)(2,1)S(1)}, u32[]{:S(2)}, u32[]{:S(2)}) collective-permute-start(bf16[288,768]{1,0:T(8,128)(2,1)S(1)} %maximum_select_fusion.3), channel_id=1, source_target_pairs={{0,8},{4,12},{8,0},{12,4},{16,24},{20,28},{24,16},{28,20},{1,9},{5... | collective-permute-start | bytes 1327112 | tf_op jit(solution)/shard_map/ppermute | solution.py:35
  460.2 47.5 %all-to-all-start.3 = ((bf16[8,256,128]{2,1,0:T(8,128)(2,1)}), bf16[8,256,128]{2,1,0:T(8,128)(2,1)S(1)}, u32[]{:S(2)}, u32[]{:S(2)}) async-start(bf16[8,256,128]{2,1,0:T(8,128)(2,1)} %bitcast.54), calls=%async_computation.3 | async-start | bytes 1048576 | tf_op jit(solution)/shard_map/all_to_all | solution.py:735
  464.0 28.3 %collective-permute-start.47 = (bf16[576,768]{1,0:T(8,128)(2,1)S(1)}, bf16[576,768]{1,0:T(8,128)(2,1)S(1)}, u32[]{:S(2)}, u32[]{:S(2)}) collective-permute-start(bf16[576,768]{1,0:T(8,128)(2,1)S(1)} %maximum_select_fusion.own), channel_id=1, source_target_pairs={{0,4},{4,0},{8,12},{12,8},{16,20},{20,16},{24,28},{28,24},{1,5},{5... | collective-permute-start | bytes 2654216 | tf_op jit(solution)/shard_map/ppermute | solution.py:35
  466.2 37.6 %collective-permute-start.46 = (bf16[384,768]{1,0:T(8,128)(2,1)S(1)}, bf16[384,768]{1,0:T(8,128)(2,1)S(1)}, u32[]{:S(2)}, u32[]{:S(2)}) collective-permute-start(bf16[384,768]{1,0:T(8,128)(2,1)S(1)} %maximum_select_fusion.2.own), channel_id=1, source_target_pairs={{0,4},{4,0},{8,12},{12,8},{16,20},{20,16},{24,28},{28,24},{1,5},{5... | collective-permute-start | bytes 1769480 | tf_op jit(solution)/shard_map/ppermute | solution.py:35
  (87 other events, 689.1 us)

commit v2 on v1

--- a/solution.py
+++ b/solution.py
@@ -277,8 +277,8 @@
 
 def embed_kernel(sizes, chosen, table, cols, vecs, mask, *refs):
     n, part, rows_s = sizes
-    pix, weights = blocks_of(refs[:3]), split_blocks(refs[3], refs[4], n)
-    start_ref, q_ref, k_ref, v_ref, probs, att_ref, middle, full = refs[5:]
+    pix, weights = blocks_of(refs[:3]), refs[3 : 3 + n]
+    start_ref, q_ref, k_ref, v_ref, probs, att_ref, middle, full = refs[3 + n :]
     e_rows = pix[0].shape[1]
     rows, width = start_ref.shape
     total = dot(chosen[...], table[...]) + vecs[0:1, :]
@@ -335,11 +335,11 @@
 
 
 def mlp_kernel(n, middle, vecs, bias_hid, bias_dec, *refs):
-    cot, weights = blocks_of(refs[:3]), split_blocks(refs[3], refs[4], n)
+    cot, weights, refs = blocks_of(refs[:3]), refs[3 : 3 + n], refs[3 + n :]
     rows = middle.shape[0]
-    decoded = [refs[5], refs[6], refs[7].at[:rows], refs[7].at[rows:]]
-    pre_refs = refs[8 : 8 + n]
-    kept, sent, final_grad, sums, hidden, slope = refs[8 + n :]
+    decoded = [refs[0], refs[1], refs[2].at[:rows], refs[2].at[rows:]]
+    pre_refs = refs[3 : 3 + n]
+    kept, sent, final_grad, sums, hidden, slope = refs[3 + n :]
     grads = split_blocks(kept, sent, n)
     h = pre_refs[0].shape[1]
     dec = decoded[0].shape[1]
@@ -371,18 +371,21 @@
         sums[e : e + 1, :] = row_sum(pre_grad)
 
 
-def hidden_kernel(n, middle, vecs, final_grad, *refs):
-    pre, weights = refs[:n], split_blocks(refs[n], refs[n + 1], n)
-    kept, sent, middle_grad, sums = refs[n + 2 :]
+def hidden_kernel(n, middle, vecs, final_grad, att, *refs):
+    pre, weights = refs[:n], refs[n : 2 * n]
+    kept, sent, middle_grad, sums = refs[2 * n :]
     grads = split_blocks(kept, sent, n)
     h = pre[0].shape[1]
     unit, rstd, normed = norm_forward(middle[...].astype(BF16), vecs[6:7, :], vecs[7:8, :])
     total = jnp.zeros(unit.shape, F32)
     for e in range(n):
         total = total + dot(pre[e][...], weights[e][:h, :])
-        grads[e][...] = dot_tl(pre[e][...], normed).astype(BF16)
+        grads[e][:h, :] = dot_tl(pre[e][...], normed).astype(BF16)
     term, gain, bias = norm_backward(total, unit, rstd, vecs[6:7, :])
     middle_grad[...] = final_grad[...] + term
+    part = kept.shape[0] // 2 - h
+    low_grad = middle_grad[...].astype(BF16)
+    weight_grads(n, part, h, ((att, low_grad),), kept, sent)
     sums[0:1, :] = gain
     sums[1:2, :] = bias
     sums[2:8, :] = jnp.zeros((6, sums.shape[1]), F32)
@@ -390,8 +393,8 @@
 
 def attn_back_kernel(sizes, middle_grad, start, q, k, v, probs, chosen, vecs, *refs):
     n, part, rows_s, e_rows = sizes
-    weights = split_blocks(refs[0], refs[1], n)
-    start_grad, dq, dk, dv, sums, full, ag = refs[2:]
+    weights = refs[:n]
+    start_grad, dq, dk, dv, sums, full, ag = refs[n:]
     rows, width = start.shape
     copy_rows(full, weights, e_rows + 3 * part, part)
     low_grad = middle_grad[...].astype(BF16)
@@ -445,9 +448,9 @@
 
 
 def pixel_grad_kernel(n, start_grad, cols, *refs):
-    pix, weights = blocks_of(refs[:3]), split_blocks(refs[3], refs[4], n)
+    pix, weights, refs = blocks_of(refs[:3]), refs[3 : 3 + n], refs[3 + n :]
     rows = start_grad.shape[0]
-    grads, bands = [refs[5], refs[6], refs[7].at[:rows], refs[7].at[rows:]], refs[8]
+    grads, bands = [refs[0], refs[1], refs[2].at[:rows], refs[2].at[rows:]], refs[3]
     e_rows = pix[0].shape[1]
     first = jnp.zeros((1, e_rows), F32)
     second = jnp.zeros((1, e_rows), F32)
@@ -468,13 +471,12 @@
             grads[e][at : at + part, :] = whole[e * part : (e + 1) * part, :]
 
 
-def weight_kernel(sizes, start_grad, middle_grad, start, att, dq, dk, dv, cols, vecs, *refs):
+def weight_kernel(sizes, start_grad, start, dq, dk, dv, cols, vecs, *refs):
     n, part = sizes
     pix, (kept, sent) = blocks_of(refs[:3]), refs[3:]
     e_rows = pix[0].shape[1]
     normed = norm_forward(start[...], vecs[1:2, :], vecs[2:3, :])[2]
-    low_grad = middle_grad[...].astype(BF16)
-    pairs = ((dq, normed), (dk, normed), (dv, normed), (att, low_grad))
+    pairs = ((dq, normed), (dk, normed), (dv, normed))
     weight_grads(n, part, e_rows, pairs, kept, sent)
     grads = split_blocks(kept, sent, n)
     for e in range(n):
@@ -482,12 +484,10 @@
         grads[e][:e_rows, :] = got.astype(BF16)
 
 
-def join_kernel(half, flag, own, direct, handed, out):
-    rows = own.shape[0]
-    out[:rows, :] = own[...]
-    at = pl.multiple_of(rows + flag[0] * half, 16)
+def join_kernel(half, flag, direct, handed, out):
+    at = pl.multiple_of(flag[0] * half, 16)
     out[pl.ds(at, half), :] = direct[...]
-    at = pl.multiple_of(rows + (1 - flag[0]) * half, 16)
+    at = pl.multiple_of((1 - flag[0]) * half, 16)
     out[pl.ds(at, half), :] = handed[...]
 
 
@@ -576,22 +576,23 @@
         self.own, self.half = own, part.shape[0]
         self.flag = (data_index & 1).astype(jnp.int32)[None]
         self.direct = swap(part, "mp", 2)
+        self.near = swap(own, "mp", 1)
 
     def hand_on(self):
         self.handed = swap(self.direct, "dp", 1)
 
     def join(self, line):
         rows, width = self.own.shape
-        [both] = call(
+        [far] = call(
             functools.partial(join_kernel, self.half),
-            [((2 * rows, width), BF16)],
-            [self.flag, self.own, self.direct, line.wait(self.handed)],
+            [((rows, width), BF16)],
+            [self.flag, self.direct, line.wait(self.handed)],
             "join_weights",
-            us=3.0,
+            us=2.0,
             scalars=1,
         )
-        line.mark(both)
-        self.pair = [both, swap(both, "mp", 1)]
+        line.mark(far)
+        self.blocks = [self.own, self.near, far, swap(far, "mp", 1)]
 
 
 def to_absolute(blocks, model_index):
@@ -620,7 +621,7 @@
         self.plan, self.shapes = plan, shapes
         self.flags = [((data_index >> k) & 1).astype(jnp.int32)[None] for k in range(len(bits_of("dp")))]
         self.order = list(order) + [k for k in range(len(self.flags)) if k not in order]
-        self.done, self.own = [], None
+        self.done, self.own, self.hold = [], None, False
 
     def step(self):
         if self.order or self.own is None:
@@ -637,21 +638,41 @@
         if axis is None:
             [self.own] = self.stage(came, None, 0)
             self.line.mark(self.own)
-            self.came = swap(self.own, "dp", 1 << self.done[-1])
+            self.came = swap(self.own, "dp", 1 << self.done[-1][0])
         elif axis == "x":
             self.kept, sent = self.stage(came, None, rows)
             self.line.mark(self.kept)
             self.quarters = 1
-            self.came = swap(sent, "mp", 2)
+            self.sent = sent
+            if not self.hold:
+                self.launch()
         else:
             self.kept, sent = self.stage(came, self.flags[axis], rows // 2)
             self.line.mark(self.kept)
-            self.done.append(axis)
+            self.done.append((axis, int(self.kept.shape[1] < came.shape[1])))
             self.came = swap(sent, "dp", 1 << axis)
+
+    def launch(self, *before):
+        self.came = swap(after(self.sent, *before) if before else self.sent, "mp", 2)
 
     def stage(self, came, flag, half):
         total, width = self.kept.shape
         quarters, rows = self.quarters, total // self.quarters
+        if flag is not None and half % 16 and width % 256 == 0:
+            part = width // 2
+
+            def kernel(mine, a, b, own, other):
+                for out, which in ((own, mine[0]), (other, 1 - mine[0])):
+                    here = pl.ds(pl.multiple_of(which * part, 128), part)
+                    out[...] = (a[:, here].astype(F32) + b[:, here].astype(F32)).astype(BF16)
+
+            return call(
+                kernel,
+                [((total, part), BF16)] * 2,
+                [flag, self.kept, came],
+                "reduce_" + self.name,
+                scalars=1,
+            )
         if flag is not None and half % 16:
             summed = (self.kept.astype(F32) + came.astype(F32)).astype(BF16)
             summed = summed.reshape(quarters, rows, width)
@@ -691,22 +712,22 @@
         )
 
     def gather(self):
-        axis = self.done.pop()
+        axis, dim = self.done.pop()
         came = self.line.wait(self.came)
         self.own = jnp.where(
             self.flags[axis][0] == 0,
-            jnp.concatenate([self.own, came], axis=0),
-            jnp.concatenate([came, self.own], axis=0),
+            jnp.concatenate([self.own, came], axis=dim),
+            jnp.concatenate([came, self.own], axis=dim),
         )
         self.line.mark(self.own)
-        self.came = swap(self.own, "dp", 1 << self.done[-1])
+        self.came = swap(self.own, "dp", 1 << self.done[-1][0])
 
     def finish(self):
         half, width = self.own.shape
         self.result = call(
             functools.partial(finish_kernel, half, self.plan),
             [(shape, F32) for shape in self.shapes],
-            [self.flags[self.done[0]], self.own, self.line.wait(self.came)],
+            [self.flags[self.done[0][0]], self.own, self.line.wait(self.came)],
             "finish_" + self.name,
             [pltpu.VMEM((2 * half, width), BF16)],
             us=3.0,
@@ -842,7 +863,7 @@
             jnp.concatenate([came, packet], axis=0),
         )
 
-    arrived = exchange(after(picked, packet))
+    arrived = exchange(after(picked, packet, first_w.direct))
 
     second_w = Weights(own_second, after(cut_second, first_w.direct), data_index)
     first_w.hand_on()
@@ -852,37 +873,6 @@
     own_info = own_info.transpose(1, 0, 2).reshape(2, tile_count).astype(jnp.int32)
     my_tiles_bit = model_index * my_tiles
     codes = own_info[0] ^ my_tiles_bit
-    line = Line()
-    line.mark(second_w.direct)
-    first_w.join(line)
-    own, near, far = place_in(codes, line.wait(arrived), visible, model_size)
-    line.mark(far)
-    pix = Crossing(own, near, far)
-    arrived_cot = exchange(after(cot_picked, far))
-    pix.relay(line)
-    own, near, far = place_in(codes, line.wait(arrived_cot), visible, model_size)
-    line.mark(far)
-    cot = Crossing(own, near, far)
-    second_w.join(line)
-
-    bias_rel = [first_w.pair[e % 2][e // 2 * own_first.shape[0] + base :][:16] for e in range(4)]
-    bias_rel = jnp.stack(bias_rel).astype(F32)
-    bias_abs = to_absolute(bias_rel, model_index)
-
-    def rel_vec(k):
-        return bias_rel[:, k, : small[k].shape[0]].reshape(1, -1)
-
-    def abs_vec(k):
-        return bias_abs[:, k, : small[k].shape[0]].reshape(1, -1)
-
-    gains = [norm1_gain, norm1_bias, norm2_gain, norm2_bias]
-    gains = [v[None].astype(F32) for v in gains]
-    vecs = jnp.concatenate(
-        [abs_vec(0), gains[0], gains[1], rel_vec(1), rel_vec(2), abs_vec(3)]
-        + [gains[2], gains[3], abs_vec(4), jnp.zeros((7, full_width), F32)]
-    )
-    bias_hid, bias_dec = bias_rel[:, 6, :hid_part], bias_rel[:, 5, :dec_part]
-
     total = jnp.sum(packet[:, :2, :BANDS], axis=0)
     per_band = float(grid_count * data_size * (pixel_cols // BANDS) * model_size)
     band_mean = total[0] / per_band
@@ -923,6 +913,33 @@
     key_mask = jnp.pad(usable.astype(F32), ((0, 8 - own_samples), (0, 0)))
     cols = jnp.pad(jnp.stack([mean_cols, rstd_cols]), ((0, 6), (0, 0)))
 
+    line = Line()
+    held = after(arrived, second_w.direct, chosen, key_mask, cols)
+    own, near, far = place_in(codes, held, visible, model_size)
+    line.mark(far)
+    pix = Crossing(own, near, far)
+    arrived_cot = exchange(after(cot_picked, far))
+    first_w.join(line)
+    pix.relay(line)
+    line.mark(pix.parts[1])
+    bias_rel = [first_w.blocks[e][base : base + 16] for e in range(4)]
+    bias_rel = jnp.stack(bias_rel).astype(F32)
+    bias_abs = to_absolute(bias_rel, model_index)
+
+    def rel_vec(k):
+        return bias_rel[:, k, : small[k].shape[0]].reshape(1, -1)
+
+    def abs_vec(k):
+        return bias_abs[:, k, : small[k].shape[0]].reshape(1, -1)
+
+    gains = [norm1_gain, norm1_bias, norm2_gain, norm2_bias]
+    gains = [v[None].astype(F32) for v in gains]
+    vecs = jnp.concatenate(
+        [abs_vec(0), gains[0], gains[1], rel_vec(1), rel_vec(2), abs_vec(3)]
+        + [gains[2], gains[3], abs_vec(4), jnp.zeros((7, full_width), F32)]
+    )
+    bias_hid, bias_dec = bias_rel[:, 6, :hid_part], bias_rel[:, 5, :dec_part]
+
     square = ((rows, full_width), BF16)
     wide_rows = ((rows, full_width), F32)
     heads = own_samples * full_width // HEAD_DIM
@@ -930,12 +947,16 @@
     start, queries, key_rows, value_rows, probs, attended, middle = call(
         functools.partial(embed_kernel, (model_size, part_width, sample_rows)),
         [square] * 4 + [((heads, sample_rows, sample_rows), BF16), square, wide_rows],
-        [chosen, jnp.asarray(wide), cols, vecs, line.wait(key_mask)] + pix.parts + first_w.pair,
+        [chosen, jnp.asarray(wide), cols, vecs, line.wait(key_mask)] + pix.parts + first_w.blocks,
         "embed_attend",
         [weight_scratch],
         us=19.0,
     )
     line.mark(middle)
+    own, near, far = place_in(codes, line.wait(arrived_cot), visible, model_size)
+    line.mark(far)
+    cot = Crossing(own, near, far)
+    second_w.join(line)
     cot.relay(line)
     decoded_shape = ((rows, dec_part), BF16)
     hidden_shape = ((rows, hid_part), BF16)
@@ -946,13 +967,14 @@
         + [hidden_shape] * model_size
         + [((2 * (hid_part + dec_part), full_width), BF16)] * 2
         + [wide_rows, ((16, full_width), F32)],
-        [middle, vecs, bias_hid, bias_dec] + cot.parts + second_w.pair,
+        [middle, vecs, bias_hid, bias_dec] + cot.parts + second_w.blocks,
         "mlp_decode",
         [pltpu.VMEM((model_size, rows, hid_part), BF16)] * 2,
         us=20.0,
     )
     decoded_rows, pre_grads = out[:3], out[3 : 3 + model_size]
     out_kept, out_sent, final_grad, mlp_sums = out[3 + model_size :]
+    decoded_mp = Crossing(*decoded_rows)
     red_a = Reduction(
         out_kept,
         out_sent,
@@ -963,50 +985,60 @@
         [w_mlp_out.shape, w_decoder.shape],
         "out",
     )
+    def decoded_step(decoded_dp):
+        out = call(
+            functools.partial(spread_kernel, tile_tokens),
+            [((grid_count, dec_part), BF16)],
+            [order, vis_count, pos_wide, mask_token[None, :], line.wait(decoded_dp)],
+            "spread_decoded",
+            us=3.5,
+            scalars=2,
+        )
+        line.mark(out[0])
+        return out
+
+    def go_home(crossing):
+        parts = crossing.parts
+        tiles = place_out(codes, [parts[0], line.wait(parts[1]), parts[2]], visible)
+        line.mark(tiles)
+        return exchange(tiles)
+
     out = call(
         functools.partial(hidden_kernel, model_size),
-        [((2 * hid_part, full_width), BF16)] * 2 + [wide_rows, ((8, full_width), F32)],
-        [middle, vecs, final_grad] + pre_grads + second_w.pair,
+        [((2 * (hid_part + part_width), full_width), BF16)] * 2 + [wide_rows, ((8, full_width), F32)],
+        [middle, vecs, final_grad, attended] + pre_grads + second_w.blocks,
         "hidden_back",
         us=13.0,
     )
     hid_kept, hid_sent, middle_grad, hid_sums = out
     line.mark(middle_grad)
     red_b = Reduction(
-        hid_kept, hid_sent, ["x", 0, 1, 2], data_index, line, (True,), [w_hidden.shape], "hidden"
-    )
+        hid_kept, hid_sent, ["x", 0, 1, 2], data_index, line, (True, False), [w_hidden.shape, w_attn_out.shape], "hidden"
+    )
+    decoded_mp.relay(line)
     red_a.step()
     start_grad, dq, dk, dv, attn_sums = call(
         functools.partial(attn_back_kernel, (model_size, part_width, sample_rows, pixel_cols)),
         [square] * 4 + [((8, full_width), F32)],
         [line.wait(middle_grad), start, queries, key_rows, value_rows]
         + [probs, chosen, vecs]
-        + first_w.pair,
+        + first_w.blocks,
         "attend_back",
         [weight_scratch, pltpu.VMEM((rows, full_width), BF16)],
         us=18.0,
     )
     line.mark(start_grad)
+    decoded_dp = go_home(decoded_mp)
     out = call(
         functools.partial(pixel_grad_kernel, model_size),
         [((rows, pixel_cols), BF16)] * 2 + [((2 * rows, pixel_cols), BF16), ((8, 128), F32)],
-        [line.wait(start_grad), cols] + pix.parts + first_w.pair,
+        [line.wait(start_grad), cols] + pix.parts + first_w.blocks,
         "pixel_grad",
         us=6.7,
     )
     normed_grad, bands = out[:3], out[3]
     line.mark(bands)
     grad_mp = Crossing(*normed_grad)
-    red_a.step()
-    first_kept, first_sent = call(
-        functools.partial(weight_kernel, (model_size, part_width)),
-        [((2 * base, full_width), BF16)] * 2,
-        [line.wait(start_grad), middle_grad, start, attended, dq, dk, dv, cols, vecs] + pix.parts,
-        "weight_grad",
-        us=10.0,
-    )
-    line.mark(first_kept)
-    grad_mp.relay(line)
     [sums] = call(
         functools.partial(pack_kernel, (model_size, part_width)),
         [((32, full_width), F32)],
@@ -1018,24 +1050,34 @@
     )
     line.mark(sums)
     sums = Sums(sums, line)
+    sums.step()
+    red_b.hold = True
+    red_b.step()
+    red_a.step()
+    spread = decoded_step(decoded_dp)
+    first_kept, first_sent = call(
+        functools.partial(weight_kernel, (model_size, part_width)),
+        [((2 * (base - part_width), full_width), BF16)] * 2,
+        [line.wait(start_grad), start, dq, dk, dv, cols, vecs] + pix.parts,
+        "weight_grad",
+        us=10.0,
+    )
+    line.mark(first_kept)
+    grad_mp.relay(line)
+    sums.step()
+    red_b.launch(sums.values)
     red_c = Reduction(
         first_kept,
-        first_sent,
+        line.wait(first_sent),
         ["x", 0, 1, 2],
         data_index,
         line,
-        (False,) * 5,
-        [w_embed.shape] + [w_attn_out.shape] * 4,
+        (False,) * 4,
+        [w_embed.shape] + [w_attn_out.shape] * 3,
         "first",
     )
 
-    def go_home(crossing):
-        parts = crossing.parts
-        tiles = place_out(codes, [parts[0], line.wait(parts[1]), parts[2]], visible)
-        line.mark(tiles)
-        return exchange(tiles)
-
-    def patch_step():
+    def patch_step(grad_dp):
         bands_all = sums.values[5 * model_size + 7 : 5 * model_size + 9, :BANDS]
         grad_all, cross_all = bands_all[0], bands_all[1]
         grad_var = -0.5 * cross_all * band_rstd * band_rstd * band_rstd
@@ -1053,41 +1095,31 @@
         line.mark(out[0])
         return out
 
-    def decoded_step():
-        out = call(
-            functools.partial(spread_kernel, tile_tokens),
-            [((grid_count, dec_part), BF16)],
-            [order, vis_count, pos_wide, mask_token[None, :], line.wait(decoded_dp)],
-            "spread_decoded",
-            us=3.5,
-            scalars=2,
-        )
-        line.mark(out[0])
-        return out
-
     def steps(*chains):
         for chain in chains:
             chain.step()
 
-    steps(sums)
-    grad_dp = go_home(grad_mp)
-    steps(sums, red_c, red_a, red_b, sums, red_a, sums, red_a)
+    kept = {}
+
+    def go(name):
+        if name in chains:
+            chains[name].step()
+        elif name == "H":
+            kept["grad"] = go_home(grad_mp)
+        elif name == "P":
+            while sums.left:
+                sums.step()
+            kept["patch"] = patch_step(kept["grad"])
+    chains = {"a": red_a, "b": red_b, "c": red_c, "s": sums}
+    for name in "HcasbasbascaPbacbbccabcbcc":
+        go(name)
     while sums.left:
         sums.step()
-    steps(red_c, red_a, red_a, red_c, red_b)
-    [patch_grad] = patch_step()
-    steps(red_c, red_b, red_a, red_c, red_b, red_c)
-    decoded_mp = Crossing(decoded_rows[0], decoded_rows[1], line.wait(decoded_rows[2]))
-    steps(red_b, red_c)
-    decoded_mp.relay(line)
-    steps(red_b)
-    decoded_dp = go_home(decoded_mp)
-    steps(red_b)
     while not all(hasattr(chain, "result") for chain in (red_a, red_b, red_c)):
-        for chain in (red_a, red_c, red_b):
+        for chain in (red_a, red_b, red_c):
             if not hasattr(chain, "result"):
                 chain.step()
-    [decoded] = decoded_step()
+    [patch_grad], [decoded] = kept["patch"], spread
 
     n = model_size
     sums = sums.values
@@ -1105,8 +1137,8 @@
         part = vector.shape[0] // model_size
         return lax.dynamic_slice_in_dim(vector, model_index * part, part, 0)
 
-    (g_out, g_dec), [g_hid] = red_a.result, red_b.result
-    g_embed, g_query, g_key, g_value, g_attn = red_c.result
+    (g_out, g_dec), (g_hid, g_attn) = red_a.result, red_b.result
+    g_embed, g_query, g_key, g_value = red_c.result
 
     return (
         decoded,

time: 518 us -> 486 us (0.938)
  waiting for transfers between devices: 196 us -> 171 us
  starting transfers between devices: 77.5 us -> 63.9 us
  local copies, waits for them, and re-layouts: 41.4 us -> 47 us
    ppermute x48 -> x50, waiting for transfers between devices: 191 us -> 161 us  [swap(): return lax.ppermute(values, axis, [(i, i ^ bit) for i in range(size)])]
    ppermute x48 -> x50, starting transfers between devices: 57.6 us -> 44.5 us  [swap(): return lax.ppermute(values, axis, [(i, i ^ bit) for i in range(size)])]
    all_to_all x4, waiting for transfers between devices: 5.04 us -> 10.4 us  [exchange(): lax.all_to_all(blocks, 'dp', split_axis=0, concat_axis=0, tiled=True)]
    unnamed x119 -> x121, local copies, waits for them, and re-layouts: 23 us -> 24.6 us
  transfers between devices with their start and end apart: 52 -> 54, of which waited for: 25 -> 24; matrix products, arithmetic and copies ran while one was open for 5% -> 7% of each run, Pallas kernels for 28% -> 32%
where the time goes in v2:
time: 486 us; the launch traced here: 478 us
  Pallas kernels  183 us (38%)
  waiting for transfers between devices  171 us (35%)
  starting transfers between devices  63.9 us (13%)
  local copies, waits for them, and re-layouts  47 us (10%)
  other arithmetic  11.8 us (2%)
    pallas_call x36, Pallas kernels, call(): return list(run(*args))  183 us
    ppermute x50, waiting for transfers between devices, swap(): return lax.ppermute(values, axis, [(i, i ^ bit) for i in range(size)])  161 us
    ppermute x50, starting transfers between devices, swap(): return lax.ppermute(values, axis, [(i, i ^ bit) for i in range(size)])  44.5 us
    unnamed x121, local copies, waits for them, and re-layouts  24.6 us
    all_to_all x4, starting transfers between devices, exchange(): lax.all_to_all(blocks, 'dp', split_axis=0, concat_axis=0, tiled=True)  19.4 us
    all_to_all x4, waiting for transfers between devices, exchange(): lax.all_to_all(blocks, 'dp', split_axis=0, concat_axis=0, tiled=True)  10.4 us
  transfers between devices with their start and end apart: 54, of which 24 were waited for; matrix products, arithmetic and copies ran while one was open for 7% of the time, Pallas kernels for 32%

profile of v2, /device:TPU:0, one launch (start us, length us, event | category | flops | bytes accessed | tf_op | source)
XLA Modules:
  0.0 478.4 jit_solution(14915974276084752151)
XLA Ops:
  13.6 5.5 %prep_weights.1 = (bf16[1184,768]{1,0:T(8,128)(2,1)}, bf16[1664,768]{1,0:T(8,128)(2,1)}, bf16[592,768]{1,0:T(8,128)(2,1)}, bf16[832,768]{1,0:T(8,128)(2,1)}) custom-call(s32[1]{0:T(128)} %bitcast.4.odd.flag, bf16[192,768]{1,0:T(8,128)(2,1)} %bitcast.59, bf16[192,768]{1,0:T(8,128)(2,1)} %bitcast.60, bf16[192,768]{1,0:T(8,128)(2,1)} %bitcast.61, ...), custom_call_target="tpu_custom_call" | custom-call | bytes 16500000 | tf_op jit(solution)/shard_map/prep_weights/pallas_call | solution.py:571
  22.4 7.5 %pick_rows.1 = (bf16[2048,384]{1,0:T(8,128)(2,1)}, bf16[2048,128]{1,0:T(8,128)(2,1)}, f32[8,128]{1,0:T(8,128)}) custom-call(s32[32]{0:T(128)} %select_reduce_fusion.order, s32[32]{0:T(128)} %count.5, s32[32,128]{1,0:T(8,128)} %pad.23.pos, bf16[4704,384]{1,0:T(8,128)(2,1)} %patches.5, bf16[4704,128]{1,0:T(8,128)(2,1)} %cot.1), custom_call_target="tpu_custom_call" | custom-call | bytes 24750000 | tf_op jit(solution)/shard_map/pick_rows/pallas_call | solution.py:571
  42.1 5.8 %all-to-all-start = ((bf16[8,256,384]{2,1,0:T(8,128)(2,1)}), bf16[8,256,384]{2,1,0:T(8,128)(2,1)S(1)}, u32[]{:S(2)}, u32[]{:S(2)}) async-start(bf16[8,256,384]{2,1,0:T(8,128)(2,1)} %bitcast.57), calls=%async_computation | async-start | bytes 3145728 | tf_op jit(solution)/shard_map/all_to_all | solution.py:756
  59.4 22.6 %collective-permute-done.8.direct = bf16[832,768]{1,0:T(8,128)(2,1)} collective-permute-done((bf16[832,768]{1,0:T(8,128)(2,1)}, bf16[832,768]{1,0:T(8,128)(2,1)}, u32[]{:S(2)}, u32[]{:S(2)}) %collective-permute-start.8) | collective-permute-done | bytes 1277984 | tf_op jit(solution)/shard_map/ppermute | solution.py:35
  91.7 19.3 %collective-permute-done.10.refs_2_ = bf16[1024,384]{1,0:T(8,128)(2,1)S(1)} collective-permute-done((bf16[1024,384]{1,0:T(8,128)(2,1)S(1)}, bf16[1024,384]{1,0:T(8,128)(2,1)S(1)}, u32[]{:S(2)}, u32[]{:S(2)}) %collective-permute-start.10) | collective-permute-done | bytes 786464 | tf_op jit(solution)/shard_map/ppermute | solution.py:35
  122.1 18.9 %embed_attend.1 = (bf16[512,768]{1,0:T(8,128)(2,1)}, bf16[512,768]{1,0:T(8,128)(2,1)}, bf16[512,768]{1,0:T(8,128)(2,1)}, bf16[512,768]{1,0:T(8,128)(2,1)}, bf16[...) custom-call(bf16[512,128]{1,0:T(8,128)(2,1)} %or_convert_fusion.chosen, ...), custom_call_target="tpu_custom_call" | custom-call | bytes 62700000 | tf_op jit(solution)/shard_map/embed_attend/pallas_call | solution.py:571
  141.1 8.3 %all-to-all-done.1 = bf16[8,256,128]{2,1,0:T(8,128)(2,1)S(1)} async-done(((bf16[8,256,128]{2,1,0:T(8,128)(2,1)}), bf16[8,256,128]{2,1,0:T(8,128)(2,1)S(1)}, u32[]{:S(2)}, u32[]{:S(2)}) %all-to-all-start.1) | async-done | bytes 524320 | tf_op jit(solution)/shard_map/all_to_all | solution.py:756
  157.1 8.2 %collective-permute-done.12.refs_2_ = bf16[1024,128]{1,0:T(8,128)(2,1)S(1)} collective-permute-done((bf16[1024,128]{1,0:T(8,128)(2,1)S(1)}, bf16[1024,128]{1,0:T(8,128)(2,1)S(1)}, u32[]{:S(2)}, u32[]{:S(2)}) %collective-permute-start.12) | collective-permute-done | bytes 262176 | tf_op jit(solution)/shard_map/ppermute | solution.py:35
  168.5 18.9 %mlp_decode.1 = (bf16[512,128]{1,0:T(8,128)(2,1)}, bf16[512,128]{1,0:T(8,128)(2,1)}, bf16[1024,128]{1,0:T(8,128)(2,1)}, bf16[512,768]{1,0:T(8,128)(2,1)}, bf16[5...) custom-call(f32[512,768]{1,0:T(8,128)} %get-tuple-element.169.middle, ...), custom_call_target="tpu_custom_call" | custom-call | bytes 66000000 | tf_op jit(solution)/shard_map/mlp_decode/pallas_call | solution.py:571
  187.6 15.7 %hidden_back.1 = (bf16[1920,768]{1,0:T(8,128)(2,1)}, bf16[1920,768]{1,0:T(8,128)(2,1)}, f32[512,768]{1,0:T(8,128)}, f32[8,768]{1,0:T(8,128)}) custom-call(f32[512,768]{1,0:T(8,128)} %get-tuple-element.169.middle, f32[16,768]{1,0:T(8,128)} %concatenate.83.vecs, f32[512,768]{1,0:T(8,128)} %get-tuple-element.182.final_grad, ...), custom_call_target="tpu_custom_call" | custom-call | bytes 42900000 | tf_op jit(solution)/shard_map/hidden_back/pallas_call | solution.py:571
  204.2 7.8 %collective-permute-done.17.far = bf16[1024,128]{1,0:T(8,128)(2,1)S(1)} collective-permute-done((bf16[1024,128]{1,0:T(8,128)(2,1)S(1)}, bf16[1024,128]{1,0:T(8,128)(2,1)S(1)}, u32[]{:S(2)}, u32[]{:S(2)}) %collective-permute-start.17) | collective-permute-done | bytes 262176 | tf_op jit(solution)/shard_map/ppermute | solution.py:35
  218.7 18.1 %attend_back.1 = (bf16[512,768]{1,0:T(8,128)(2,1)}, bf16[512,768]{1,0:T(8,128)(2,1)}, bf16[512,768]{1,0:T(8,128)(2,1)}, bf16[512,768]{1,0:T(8,128)(2,1)}, f32[8,768]{1,0:T(8,128)}) custom-call(f32[512,768]{1,0:T(8,128)} %get-tuple-element.194.middle_grad, bf16[512,768]{1,0:T(8,128)(2,1)} %get-tuple-element.195.start, bf16[512,768]{1,0:T(8,128)(2,1)} %get-tuple-element.196.q, ...), custom_call_target="tpu_custom_call" | custom-call | bytes 59400000 | tf_op jit(solution)/shard_map/attend_back/pallas_call | solution.py:571
  243.0 6.7 %pixel_grad.1 = (bf16[512,384]{1,0:T(8,128)(2,1)}, bf16[512,384]{1,0:T(8,128)(2,1)}, bf16[1024,384]{1,0:T(8,128)(2,1)}, f32[8,128]{1,0:T(8,128)}) custom-call(bf16[512,768]{1,0:T(8,128)(2,1)} %get-tuple-element.219.start_grad, f32[8,384]{1,0:T(8,128)} %select_maximum_fusion.cols, bf16[512,384]{1,0:T(8,128)(2,1)} %get-tuple-element.168.refs_0_, ...), custom_call_target="tpu_custom_call" | custom-call | bytes 22110000 | tf_op jit(solution)/shard_map/pixel_grad/pallas_call | solution.py:571
  269.9 8.7 %weight_grad.1 = (bf16[1920,768]{1,0:T(8,128)(2,1)}, bf16[1920,768]{1,0:T(8,128)(2,1)}) custom-call(bf16[512,768]{1,0:T(8,128)(2,1)} %get-tuple-element.219.start_grad, bf16[512,768]{1,0:T(8,128)(2,1)} %get-tuple-element.195.start, bf16[512,768]{1,0:T(8,128)(2,1)} %get-tuple-element.220.dq, bf16[512,768]{1,0:T(8,128)(2,1)} %get-tuple-element.221.dk, ...), custom_call_target="tpu_custom_call" | custom-call | bytes 33000000 | tf_op jit(solution)/shard_map/weight_grad/pallas_call | solution.py:571
  290.7 6.3 %all-to-all-start.3 = ((bf16[8,256,384]{2,1,0:T(8,128)(2,1)}), bf16[8,256,384]{2,1,0:T(8,128)(2,1)S(1)}, u32[]{:S(2)}, u32[]{:S(2)}) async-start(bf16[8,256,384]{2,1,0:T(8,128)(2,1)} %bitcast.53), calls=%async_computation.3 | async-start | bytes 3145728 | tf_op jit(solution)/shard_map/all_to_all | solution.py:756
  305.3 27.0 %collective-permute-done.26.b = bf16[448,768]{1,0:T(8,128)(2,1)S(1)} collective-permute-done((bf16[448,768]{1,0:T(8,128)(2,1)}, bf16[448,768]{1,0:T(8,128)(2,1)S(1)}, u32[]{:S(2)}, u32[]{:S(2)}) %collective-permute-start.26) | collective-permute-done | bytes 688160 | tf_op jit(solution)/shard_map/ppermute | solution.py:35
  341.8 6.3 %collective-permute-done.30.b = bf16[224,768]{1,0:T(8,128)(2,1)S(1)} collective-permute-done((bf16[224,768]{1,0:T(8,128)(2,1)S(1)}, bf16[224,768]{1,0:T(8,128)(2,1)S(1)}, u32[]{:S(2)}, u32[]{:S(2)}) %collective-permute-start.30) | collective-permute-done | bytes 344096 | tf_op jit(solution)/shard_map/ppermute | solution.py:35
  379.2 8.0 %spread_patch_grad.1 = f32[4704,384]{1,0:T(8,128)} custom-call(s32[32]{0:T(128)} %select_reduce_fusion.order, s32[32]{0:T(128)} %count.5, s32[32,128]{1,0:T(8,128)} %pad.23.pos, f32[8,384]{1,0:T(8,128)} %pad.28.cols, bf16[4704,384]{1,0:T(8,128)(2,1)} %patches.5, bf16[2048,384]{1,0:T(8,128)(2,1)} %bitcast.51), custom_call_target="tpu_custom_call" | custom-call | bytes 26400000 | tf_op jit(solution)/shard_map/spread_patch_grad/pallas_call | solution.py:571
  403.9 6.7 %collective-permute-done.42 = bf16[240,384]{1,0:T(8,128)(2,1)S(1)} collective-permute-done((bf16[240,384]{1,0:T(8,128)(2,1)}, bf16[240,384]{1,0:T(8,128)(2,1)S(1)}, u32[]{:S(2)}, u32[]{:S(2)}) %collective-permute-start.42) | collective-permute-done | bytes 184352 | tf_op jit(solution)/shard_map/ppermute | solution.py:35
  411.8 6.1 %collective-permute-done.40.b = bf16[240,768]{1,0:T(8,128)(2,1)S(1)} collective-permute-done((bf16[240,768]{1,0:T(8,128)(2,1)}, bf16[240,768]{1,0:T(8,128)(2,1)S(1)}, u32[]{:S(2)}, u32[]{:S(2)}) %collective-permute-start.40) | collective-permute-done | bytes 368672 | tf_op jit(solution)/shard_map/ppermute | solution.py:35
  420.6 12.2 %collective-permute-done.43.b = bf16[240,384]{1,0:T(8,128)(2,1)S(1)} collective-permute-done((bf16[240,384]{1,0:T(8,128)(2,1)}, bf16[240,384]{1,0:T(8,128)(2,1)S(1)}, u32[]{:S(2)}, u32[]{:S(2)}) %collective-permute-start.43) | collective-permute-done | bytes 184352 | tf_op jit(solution)/shard_map/ppermute | solution.py:35
  440.0 7.9 %collective-permute-done.44 = bf16[240,384]{1,0:T(8,128)(2,1)S(1)} collective-permute-done((bf16[240,384]{1,0:T(8,128)(2,1)S(1)}, bf16[240,384]{1,0:T(8,128)(2,1)S(1)}, u32[]{:S(2)}, u32[]{:S(2)}) %collective-permute-start.44) | collective-permute-done | bytes 184352 | tf_op jit(solution)/shard_map/ppermute | solution.py:35
  448.1 10.1 %collective-permute-done.48.came = bf16[480,768]{1,0:T(8,128)(2,1)S(1)} collective-permute-done((bf16[480,768]{1,0:T(8,128)(2,1)S(1)}, bf16[480,768]{1,0:T(8,128)(2,1)S(1)}, u32[]{:S(2)}, u32[]{:S(2)}) %collective-permute-start.48) | collective-permute-done | bytes 737312 | tf_op jit(solution)/shard_map/ppermute | solution.py:35
  469.3 5.0 %collective-permute-done.49.came = bf16[480,768]{1,0:T(8,128)(2,1)S(1)} collective-permute-done((bf16[480,768]{1,0:T(8,128)(2,1)S(1)}, bf16[480,768]{1,0:T(8,128)(2,1)S(1)}, u32[]{:S(2)}, u32[]{:S(2)}) %collective-permute-start.49) | collective-permute-done | bytes 737312 | tf_op jit(solution)/shard_map/ppermute | solution.py:35
  (361 shorter events, 209.1 us)
Async XLA Ops:
  19.0 22.2 %collective-permute-start.6 = (bf16[592,768]{1,0:T(8,128)(2,1)}, bf16[592,768]{1,0:T(8,128)(2,1)S(1)}, u32[]{:S(2)}, u32[]{:S(2)}) collective-permute-start(bf16[592,768]{1,0:T(8,128)(2,1)} %get-tuple-element.158), channel_id=1, source_target_pairs={{0,2},{1,3},{2,0},{3,1},{4,6},{5,7},{6,4},{7,5},{8,10},{9,11},{10,... | collective-permute-start | bytes 2727944 | tf_op jit(solution)/shard_map/ppermute | solution.py:35
  37.1 75.7 %collective-permute-start.5 = (bf16[1184,768]{1,0:T(8,128)(2,1)S(1)}, bf16[1184,768]{1,0:T(8,128)(2,1)}, u32[]{:S(2)}, u32[]{:S(2)}) collective-permute-start(bf16[1184,768]{1,0:T(8,128)(2,1)S(1)} %copy-done), channel_id=1, source_target_pairs={{0,1},{1,0},{2,3},{3,2},{4,5},{5,4},{6,7},{7,6},{8,9},{9,8},{10,11... | collective-permute-start | bytes 5455880 | tf_op jit(solution)/shard_map/ppermute | solution.py:35
  42.1 42.1 %all-to-all-start = ((bf16[8,256,384]{2,1,0:T(8,128)(2,1)}), bf16[8,256,384]{2,1,0:T(8,128)(2,1)S(1)}, u32[]{:S(2)}, u32[]{:S(2)}) async-start(bf16[8,256,384]{2,1,0:T(8,128)(2,1)} %bitcast.57), calls=%async_computation | async-start | bytes 3145728 | tf_op jit(solution)/shard_map/all_to_all | solution.py:756
  53.0 29.1 %collective-permute-start.8 = (bf16[832,768]{1,0:T(8,128)(2,1)}, bf16[832,768]{1,0:T(8,128)(2,1)}, u32[]{:S(2)}, u32[]{:S(2)}) collective-permute-start(bf16[832,768]{1,0:T(8,128)(2,1)} %get-tuple-element.161), channel_id=1, source_target_pairs={{0,2},{1,3},{2,0},{3,1},{4,6},{5,7},{6,4},{7,5},{8,10},{9,11},{10,... | collective-permute-start | bytes 3833864 | tf_op jit(solution)/shard_map/ppermute | solution.py:35
  53.6 34.5 %collective-permute-start.7 = (bf16[592,768]{1,0:T(8,128)(2,1)}, bf16[592,768]{1,0:T(8,128)(2,1)}, u32[]{:S(2)}, u32[]{:S(2)}) collective-permute-start(bf16[592,768]{1,0:T(8,128)(2,1)} %copy-done.16), channel_id=1, source_target_pairs={{0,4},{4,0},{8,12},{12,8},{16,20},{20,16},{24,28},{28,24},{1,5},{5... | collective-permute-start | bytes 2727944 | tf_op jit(solution)/shard_map/ppermute | solution.py:35
  91.0 28.4 %collective-permute-start.9 = (bf16[1184,768]{1,0:T(8,128)(2,1)}, bf16[1184,768]{1,0:T(8,128)(2,1)}, u32[]{:S(2)}, u32[]{:S(2)}) collective-permute-start(bf16[1184,768]{1,0:T(8,128)(2,1)} %join_weights.2.refs_5_.refs_2_), channel_id=1, source_target_pairs={{0,1},{1,0},{2,3},{3,2},{4,5},{5,4},{6,7},{7,6},{8,9},{9,8},{10,11... | collective-permute-start | bytes 5455880 | tf_op jit(solution)/shard_map/ppermute | solution.py:35
  112.2 54.4 %collective-permute-start.15 = (bf16[1664,768]{1,0:T(8,128)(2,1)}, bf16[1664,768]{1,0:T(8,128)(2,1)}, u32[]{:S(2)}, u32[]{:S(2)}) collective-permute-start(bf16[1664,768]{1,0:T(8,128)(2,1)} %get-tuple-element.178.refs_3_.refs_4_), channel_id=1, source_target_pairs={{0,1},{1,0},{2,3},{3,2},{4,5},{5,4},{6,7},{7,6},{8,9},{9,8},{10,11... | collective-permute-start | bytes 7667720 | tf_op jit(solution)/shard_map/ppermute | solution.py:35
  113.6 38.5 %collective-permute-start.13 = (bf16[832,768]{1,0:T(8,128)(2,1)}, bf16[832,768]{1,0:T(8,128)(2,1)S(1)}, u32[]{:S(2)}, u32[]{:S(2)}) collective-permute-start(bf16[832,768]{1,0:T(8,128)(2,1)} %collective-permute-done.8.direct), channel_id=1, source_target_pairs={{0,4},{4,0},{8,12},{12,8},{16,20},{20,16},{24,28},{28,24},{1,5},{5... | collective-permute-start | bytes 3833864 | tf_op jit(solution)/shard_map/ppermute | solution.py:35
  115.7 33.7 %all-to-all-start.1 = ((bf16[8,256,128]{2,1,0:T(8,128)(2,1)}), bf16[8,256,128]{2,1,0:T(8,128)(2,1)S(1)}, u32[]{:S(2)}, u32[]{:S(2)}) async-start(bf16[8,256,128]{2,1,0:T(8,128)(2,1)} %bitcast.58), calls=%async_computation.1 | async-start | bytes 1048576 | tf_op jit(solution)/shard_map/all_to_all | solution.py:756
  187.4 24.7 %collective-permute-start.19 = (bf16[1792,768]{1,0:T(8,128)(2,1)}, bf16[1792,768]{1,0:T(8,128)(2,1)S(1)}, u32[]{:S(2)}, u32[]{:S(2)}) collective-permute-start(bf16[1792,768]{1,0:T(8,128)(2,1)} %get-tuple-element.191), channel_id=1, source_target_pairs={{0,1},{1,0},{2,3},{3,2},{4,5},{5,4},{6,7},{7,6},{8,9},{9,8},{10,11... | collective-permute-start | bytes 8257544 | tf_op jit(solution)/shard_map/ppermute | solution.py:35
  203.3 53.0 %collective-permute-start.21 = (bf16[1920,768]{1,0:T(8,128)(2,1)}, bf16[1920,768]{1,0:T(8,128)(2,1)S(1)}, u32[]{:S(2)}, u32[]{:S(2)}) collective-permute-start(bf16[1920,768]{1,0:T(8,128)(2,1)} %get-tuple-element.204), channel_id=1, source_target_pairs={{0,1},{1,0},{2,3},{3,2},{4,5},{5,4},{6,7},{7,6},{8,9},{9,8},{10,11... | collective-permute-start | bytes 8847368 | tf_op jit(solution)/shard_map/ppermute | solution.py:35
  218.1 44.5 %collective-permute-start.20 = (bf16[896,768]{1,0:T(8,128)(2,1)}, bf16[896,768]{1,0:T(8,128)(2,1)}, u32[]{:S(2)}, u32[]{:S(2)}) collective-permute-start(bf16[896,768]{1,0:T(8,128)(2,1)} %get-tuple-element.202), channel_id=1, source_target_pairs={{0,2},{1,3},{2,0},{3,1},{4,6},{5,7},{6,4},{7,5},{8,10},{9,11},{10,... | collective-permute-start | bytes 4128776 | tf_op jit(solution)/shard_map/ppermute | solution.py:35
  239.4 26.4 %all-to-all-start.2 = ((bf16[8,256,128]{2,1,0:T(8,128)(2,1)}), bf16[8,256,128]{2,1,0:T(8,128)(2,1)S(1)}, u32[]{:S(2)}, u32[]{:S(2)}) async-start(bf16[8,256,128]{2,1,0:T(8,128)(2,1)} %bitcast.56), calls=%async_computation.2 | async-start | bytes 1048576 | tf_op jit(solution)/shard_map/all_to_all | solution.py:756
  249.7 29.0 %collective-permute-start.24 = (bf16[1024,384]{1,0:T(8,128)(2,1)}, bf16[1024,384]{1,0:T(8,128)(2,1)}, u32[]{:S(2)}, u32[]{:S(2)}) collective-permute-start(bf16[1024,384]{1,0:T(8,128)(2,1)} %get-tuple-element.218), channel_id=1, source_target_pairs={{0,2},{1,3},{2,0},{3,1},{4,6},{5,7},{6,4},{7,5},{8,10},{9,11},{10,... | collective-permute-start | bytes 2359304 | tf_op jit(solution)/shard_map/ppermute | solution.py:35
  255.8 24.0 %collective-permute-start.23 = (f32[32,768]{1,0:T(8,128)}, f32[32,768]{1,0:T(8,128)}, u32[]{:S(2)}, u32[]{:S(2)}) collective-permute-start(f32[32,768]{1,0:T(8,128)} %add.243), channel_id=1, source_target_pairs={{0,2},{1,3},{2,0},{3,1},{4,6},{5,7},{6,4},{7,5},{8,10},{9,11},{10,... | collective-permute-start | bytes 294920 | tf_op jit(solution)/shard_map/ppermute | solution.py:35
  281.3 54.1 %collective-permute-start.31 = (bf16[960,768]{1,0:T(8,128)(2,1)}, bf16[960,768]{1,0:T(8,128)(2,1)S(1)}, u32[]{:S(2)}, u32[]{:S(2)}) collective-permute-start(bf16[960,768]{1,0:T(8,128)(2,1)} %get-tuple-element.238), channel_id=1, source_target_pairs={{0,2},{1,3},{2,0},{3,1},{4,6},{5,7},{6,4},{7,5},{8,10},{9,11},{10,... | collective-permute-start | bytes 4423688 | tf_op jit(solution)/shard_map/ppermute | solution.py:35
  290.7 87.3 %all-to-all-start.3 = ((bf16[8,256,384]{2,1,0:T(8,128)(2,1)}), bf16[8,256,384]{2,1,0:T(8,128)(2,1)S(1)}, u32[]{:S(2)}, u32[]{:S(2)}) async-start(bf16[8,256,384]{2,1,0:T(8,128)(2,1)} %bitcast.53), calls=%async_computation.3 | async-start | bytes 3145728 | tf_op jit(solution)/shard_map/all_to_all | solution.py:756
  297.0 35.3 %collective-permute-start.26 = (bf16[448,768]{1,0:T(8,128)(2,1)}, bf16[448,768]{1,0:T(8,128)(2,1)S(1)}, u32[]{:S(2)}, u32[]{:S(2)}) collective-permute-start(bf16[448,768]{1,0:T(8,128)(2,1)} %get-tuple-element.226), channel_id=1, source_target_pairs={{0,4},{4,0},{8,12},{12,8},{16,20},{20,16},{24,28},{28,24},{1,5},{5... | collective-permute-start | bytes 2064392 | tf_op jit(solution)/shard_map/ppermute | solution.py:35
  303.8 63.3 %collective-permute-start.36 = (bf16[960,768]{1,0:T(8,128)(2,1)}, bf16[960,768]{1,0:T(8,128)(2,1)S(1)}, u32[]{:S(2)}, u32[]{:S(2)}) collective-permute-start(bf16[960,768]{1,0:T(8,128)(2,1)} %get-tuple-element.250), channel_id=1, source_target_pairs={{0,2},{1,3},{2,0},{3,1},{4,6},{5,7},{6,4},{7,5},{8,10},{9,11},{10,... | collective-permute-start | bytes 4423688 | tf_op jit(solution)/shard_map/ppermute | solution.py:35
  305.3 30.1 %collective-permute-start.25 = (f32[32,768]{1,0:T(8,128)S(1)}, f32[32,768]{1,0:T(8,128)S(1)}, u32[]{:S(2)}, u32[]{:S(2)}) collective-permute-start(f32[32,768]{1,0:T(8,128)S(1)} %add.244), channel_id=1, source_target_pairs={{0,4},{4,0},{8,12},{12,8},{16,20},{20,16},{24,28},{28,24},{1,5},{5... | collective-permute-start | bytes 294920 | tf_op jit(solution)/shard_map/ppermute | solution.py:35
  339.7 20.9 %collective-permute-start.34 = (bf16[480,768]{1,0:T(8,128)(2,1)}, bf16[480,768]{1,0:T(8,128)(2,1)S(1)}, u32[]{:S(2)}, u32[]{:S(2)}) collective-permute-start(bf16[480,768]{1,0:T(8,128)(2,1)} %get-tuple-element.245), channel_id=1, source_target_pairs={{0,4},{4,0},{8,12},{12,8},{16,20},{20,16},{24,28},{28,24},{1,5},{5... | collective-permute-start | bytes 2211848 | tf_op jit(solution)/shard_map/ppermute | solution.py:35
  371.4 22.2 %collective-permute-start.37 = (bf16[480,768]{1,0:T(8,128)(2,1)}, bf16[480,768]{1,0:T(8,128)(2,1)S(1)}, u32[]{:S(2)}, u32[]{:S(2)}) collective-permute-start(bf16[480,768]{1,0:T(8,128)(2,1)} %get-tuple-element.255), channel_id=1, source_target_pairs={{0,4},{4,0},{8,12},{12,8},{16,20},{20,16},{24,28},{28,24},{1,5},{5... | collective-permute-start | bytes 2211848 | tf_op jit(solution)/shard_map/ppermute | solution.py:35
  390.8 44.4 %collective-permute-start.46 = (bf16[448,768]{1,0:T(8,128)(2,1)S(1)}, bf16[448,768]{1,0:T(8,128)(2,1)S(1)}, u32[]{:S(2)}, u32[]{:S(2)}) collective-permute-start(bf16[448,768]{1,0:T(8,128)(2,1)S(1)} %maximum_select_fusion.2.own), channel_id=1, source_target_pairs={{0,4},{4,0},{8,12},{12,8},{16,20},{20,16},{24,28},{28,24},{1,5},{5... | collective-permute-start | bytes 2064392 | tf_op jit(solution)/shard_map/ppermute | solution.py:35
  411.7 27.4 %collective-permute-start.45 = (bf16[240,768]{1,0:T(8,128)(2,1)S(1)}, bf16[240,768]{1,0:T(8,128)(2,1)S(1)}, u32[]{:S(2)}, u32[]{:S(2)}) collective-permute-start(bf16[240,768]{1,0:T(8,128)(2,1)S(1)} %maximum_select_fusion.3), channel_id=1, source_target_pairs={{0,8},{4,12},{8,0},{12,4},{16,24},{20,28},{24,16},{28,20},{1,9},{5... | collective-permute-start | bytes 1105928 | tf_op jit(solution)/shard_map/ppermute | solution.py:35
  (90 other events, 736.6 us)

commit v3 on v2

--- a/solution.py
+++ b/solution.py
@@ -922,6 +922,9 @@
     first_w.join(line)
     pix.relay(line)
     line.mark(pix.parts[1])
+    own, near, far = place_in(codes, line.wait(arrived_cot), visible, model_size)
+    line.mark(far)
+    cot = Crossing(own, near, far)
     bias_rel = [first_w.blocks[e][base : base + 16] for e in range(4)]
     bias_rel = jnp.stack(bias_rel).astype(F32)
     bias_abs = to_absolute(bias_rel, model_index)
@@ -953,11 +956,8 @@
         us=19.0,
     )
     line.mark(middle)
-    own, near, far = place_in(codes, line.wait(arrived_cot), visible, model_size)
-    line.mark(far)
-    cot = Crossing(own, near, far)
+    cot.relay(line)
     second_w.join(line)
-    cot.relay(line)
     decoded_shape = ((rows, dec_part), BF16)
     hidden_shape = ((rows, hid_part), BF16)
     out = call(
@@ -1012,11 +1012,11 @@
     )
     hid_kept, hid_sent, middle_grad, hid_sums = out
     line.mark(middle_grad)
-    red_b = Reduction(
-        hid_kept, hid_sent, ["x", 0, 1, 2], data_index, line, (True, False), [w_hidden.shape, w_attn_out.shape], "hidden"
-    )
     decoded_mp.relay(line)
     red_a.step()
+    red_b = Reduction(
+        hid_kept, line.wait(hid_sent), ["x", 0, 1, 2], data_index, line, (True, False), [w_hidden.shape, w_attn_out.shape], "hidden"
+    )
     start_grad, dq, dk, dv, attn_sums = call(
         functools.partial(attn_back_kernel, (model_size, part_width, sample_rows, pixel_cols)),
         [square] * 4 + [((8, full_width), F32)],
@@ -1063,6 +1063,7 @@
         us=10.0,
     )
     line.mark(first_kept)
+    red_a.step()
     grad_mp.relay(line)
     sums.step()
     red_b.launch(sums.values)
@@ -1111,7 +1112,7 @@
                 sums.step()
             kept["patch"] = patch_step(kept["grad"])
     chains = {"a": red_a, "b": red_b, "c": red_c, "s": sums}
-    for name in "HcasbasbascaPbacbbccabcbcc":
+    for name in "cssHasbabacPbacbbcbaccbcc":
         go(name)
     while sums.left:
         sums.step()

time: 486 us -> 477 us (0.981)
  waiting for transfers between devices: 171 us -> 161 us
    all_to_all x4, waiting for transfers between devices: 10.4 us -> 2.14 us  [exchange(): lax.all_to_all(blocks, 'dp', split_axis=0, concat_axis=0, tiled=True)]
    unnamed x121 -> x111, local copies, waits for them, and re-layouts: 24.6 us -> 25.2 us
  transfers between devices with their start and end apart: 54 -> 54, of which waited for: 24 -> 27; matrix products, arithmetic and copies ran while one was open for 7% -> 7% of each run, Pallas kernels for 32% -> 31%
where the time goes in v3:
time: 477 us; the launch traced here: 470 us
  Pallas kernels  183 us (38%)
  waiting for transfers between devices  161 us (34%)
  starting transfers between devices  63.3 us (13%)
  local copies, waits for them, and re-layouts  48.5 us (10%)
  other arithmetic  12.7 us (3%)
    pallas_call x36, Pallas kernels, call(): return list(run(*args))  183 us
    ppermute x50, waiting for transfers between devices, swap(): return lax.ppermute(values, axis, [(i, i ^ bit) for i in range(size)])  159 us
    ppermute x50, starting transfers between devices, swap(): return lax.ppermute(values, axis, [(i, i ^ bit) for i in range(size)])  43.2 us
    unnamed x111, local copies, waits for them, and re-layouts  25.2 us
    all_to_all x4, starting transfers between devices, exchange(): lax.all_to_all(blocks, 'dp', split_axis=0, concat_axis=0, tiled=True)  20.1 us
  transfers between devices with their start and end apart: 54, of which 27 were waited for; matrix products, arithmetic and copies ran while one was open for 7% of the time, Pallas kernels for 31%

profile of v3, /device:TPU:0, one launch (start us, length us, event | category | flops | bytes accessed | tf_op | source)
XLA Modules:
  0.0 470.2 jit_solution(1633740213607754229)
XLA Ops:
  13.6 5.5 %prep_weights.1 = (bf16[1184,768]{1,0:T(8,128)(2,1)}, bf16[1664,768]{1,0:T(8,128)(2,1)}, bf16[592,768]{1,0:T(8,128)(2,1)}, bf16[832,768]{1,0:T(8,128)(2,1)}) custom-call(s32[1]{0:T(128)} %bitcast.4.odd.flag, bf16[192,768]{1,0:T(8,128)(2,1)} %bitcast.57, bf16[192,768]{1,0:T(8,128)(2,1)} %bitcast.58, bf16[192,768]{1,0:T(8,128)(2,1)} %bitcast.59, ...), custom_call_target="tpu_custom_call" | custom-call | bytes 16500000 | tf_op jit(solution)/shard_map/prep_weights/pallas_call | solution.py:571
  22.4 7.4 %pick_rows.1 = (bf16[2048,384]{1,0:T(8,128)(2,1)}, bf16[2048,128]{1,0:T(8,128)(2,1)}, f32[8,128]{1,0:T(8,128)}) custom-call(s32[32]{0:T(128)} %select_reduce_fusion.order, s32[32]{0:T(128)} %count.5, s32[32,128]{1,0:T(8,128)} %pad.23.pos, bf16[4704,384]{1,0:T(8,128)(2,1)} %patches.5, bf16[4704,128]{1,0:T(8,128)(2,1)} %cot.1), custom_call_target="tpu_custom_call" | custom-call | bytes 24750000 | tf_op jit(solution)/shard_map/pick_rows/pallas_call | solution.py:571
  42.1 5.8 %all-to-all-start = ((bf16[8,256,384]{2,1,0:T(8,128)(2,1)}), bf16[8,256,384]{2,1,0:T(8,128)(2,1)S(1)}, u32[]{:S(2)}, u32[]{:S(2)}) async-start(bf16[8,256,384]{2,1,0:T(8,128)(2,1)} %bitcast.56), calls=%async_computation | async-start | bytes 3145728 | tf_op jit(solution)/shard_map/all_to_all | solution.py:756
  59.4 22.7 %collective-permute-done.8.direct = bf16[832,768]{1,0:T(8,128)(2,1)} collective-permute-done((bf16[832,768]{1,0:T(8,128)(2,1)}, bf16[832,768]{1,0:T(8,128)(2,1)}, u32[]{:S(2)}, u32[]{:S(2)}) %collective-permute-start.8) | collective-permute-done | bytes 1277984 | tf_op jit(solution)/shard_map/ppermute | solution.py:35
  95.9 15.1 %collective-permute-done.10.refs_2_ = bf16[1024,384]{1,0:T(8,128)(2,1)S(1)} collective-permute-done((bf16[1024,384]{1,0:T(8,128)(2,1)}, bf16[1024,384]{1,0:T(8,128)(2,1)S(1)}, u32[]{:S(2)}, u32[]{:S(2)}) %collective-permute-start.10) | collective-permute-done | bytes 786464 | tf_op jit(solution)/shard_map/ppermute | solution.py:35
  121.1 19.0 %embed_attend.1 = (bf16[512,768]{1,0:T(8,128)(2,1)}, bf16[512,768]{1,0:T(8,128)(2,1)}, bf16[512,768]{1,0:T(8,128)(2,1)}, bf16[512,768]{1,0:T(8,128)(2,1)}, bf16[...) custom-call(bf16[512,128]{1,0:T(8,128)(2,1)} %or_convert_fusion.chosen, ...), custom_call_target="tpu_custom_call" | custom-call | bytes 62700000 | tf_op jit(solution)/shard_map/embed_attend/pallas_call | solution.py:571
  155.1 18.9 %mlp_decode.1 = (bf16[512,128]{1,0:T(8,128)(2,1)}, bf16[512,128]{1,0:T(8,128)(2,1)}, bf16[1024,128]{1,0:T(8,128)(2,1)}, bf16[512,768]{1,0:T(8,128)(2,1)}, bf16[5...) custom-call(f32[512,768]{1,0:T(8,128)} %get-tuple-element.174.middle, ...), custom_call_target="tpu_custom_call" | custom-call | bytes 66000000 | tf_op jit(solution)/shard_map/mlp_decode/pallas_call | solution.py:571
  174.7 15.6 %hidden_back.1 = (bf16[1920,768]{1,0:T(8,128)(2,1)}, bf16[1920,768]{1,0:T(8,128)(2,1)}, f32[512,768]{1,0:T(8,128)}, f32[8,768]{1,0:T(8,128)}) custom-call(f32[512,768]{1,0:T(8,128)} %get-tuple-element.174.middle, f32[16,768]{1,0:T(8,128)} %concatenate.83.vecs, f32[512,768]{1,0:T(8,128)} %get-tuple-element.183.final_grad, ...), custom_call_target="tpu_custom_call" | custom-call | bytes 42900000 | tf_op jit(solution)/shard_map/hidden_back/pallas_call | solution.py:571
  198.2 17.9 %attend_back.1 = (bf16[512,768]{1,0:T(8,128)(2,1)}, bf16[512,768]{1,0:T(8,128)(2,1)}, bf16[512,768]{1,0:T(8,128)(2,1)}, bf16[512,768]{1,0:T(8,128)(2,1)}, f32[8,768]{1,0:T(8,128)}) custom-call(f32[512,768]{1,0:T(8,128)} %get-tuple-element.195.middle_grad, bf16[512,768]{1,0:T(8,128)(2,1)} %get-tuple-element.196.start, bf16[512,768]{1,0:T(8,128)(2,1)} %get-tuple-element.197.q, ...), custom_call_target="tpu_custom_call" | custom-call | bytes 59400000 | tf_op jit(solution)/shard_map/attend_back/pallas_call | solution.py:571
  222.5 6.7 %pixel_grad.1 = (bf16[512,384]{1,0:T(8,128)(2,1)}, bf16[512,384]{1,0:T(8,128)(2,1)}, bf16[1024,384]{1,0:T(8,128)(2,1)}, f32[8,128]{1,0:T(8,128)}) custom-call(bf16[512,768]{1,0:T(8,128)(2,1)} %get-tuple-element.222.start_grad, f32[8,384]{1,0:T(8,128)} %select_maximum_fusion.cols, bf16[512,384]{1,0:T(8,128)(2,1)} %get-tuple-element.173.refs_0_, ...), custom_call_target="tpu_custom_call" | custom-call | bytes 22110000 | tf_op jit(solution)/shard_map/pixel_grad/pallas_call | solution.py:571
  235.4 4.7 reduce_hidden.5
  249.8 8.7 %weight_grad.1 = (bf16[1920,768]{1,0:T(8,128)(2,1)}, bf16[1920,768]{1,0:T(8,128)(2,1)}) custom-call(bf16[512,768]{1,0:T(8,128)(2,1)} %get-tuple-element.222.start_grad, bf16[512,768]{1,0:T(8,128)(2,1)} %get-tuple-element.196.start, bf16[512,768]{1,0:T(8,128)(2,1)} %get-tuple-element.223.dq, bf16[512,768]{1,0:T(8,128)(2,1)} %get-tuple-element.224.dk, ...), custom_call_target="tpu_custom_call" | custom-call | bytes 33000000 | tf_op jit(solution)/shard_map/weight_grad/pallas_call | solution.py:571
  274.6 4.8 %reduce_first.5 = (bf16[960,768]{1,0:T(8,128)(2,1)}, bf16[960,768]{1,0:T(8,128)(2,1)}) custom-call(bf16[1920,768]{1,0:T(8,128)(2,1)} %get-tuple-element.226.a, bf16[1920,768]{1,0:T(8,128)(2,1)} %copy-done.7), custom_call_target="tpu_custom_call" | custom-call | bytes 6600000 | tf_op jit(solution)/shard_map/reduce_first/pallas_call | solution.py:571
  288.2 6.0 %all-to-all-start.3 = ((bf16[8,256,384]{2,1,0:T(8,128)(2,1)}), bf16[8,256,384]{2,1,0:T(8,128)(2,1)S(1)}, u32[]{:S(2)}, u32[]{:S(2)}) async-start(bf16[8,256,384]{2,1,0:T(8,128)(2,1)} %bitcast.53), calls=%async_computation.3 | async-start | bytes 3145728 | tf_op jit(solution)/shard_map/all_to_all | solution.py:756
  299.2 28.4 %collective-permute-done.30.b = bf16[224,768]{1,0:T(8,128)(2,1)S(1)} collective-permute-done((bf16[224,768]{1,0:T(8,128)(2,1)}, bf16[224,768]{1,0:T(8,128)(2,1)S(1)}, u32[]{:S(2)}, u32[]{:S(2)}) %collective-permute-start.30) | collective-permute-done | bytes 344096 | tf_op jit(solution)/shard_map/ppermute | solution.py:35
  330.2 4.6 collective-permute-done.29
  340.6 9.5 %collective-permute-done.33.b = bf16[112,768]{1,0:T(8,128)(2,1)S(1)} collective-permute-done((bf16[112,768]{1,0:T(8,128)(2,1)S(1)}, bf16[112,768]{1,0:T(8,128)(2,1)S(1)}, u32[]{:S(2)}, u32[]{:S(2)}) %collective-permute-start.33) | collective-permute-done | bytes 172064 | tf_op jit(solution)/shard_map/ppermute | solution.py:35
  370.7 8.0 %spread_patch_grad.1 = f32[4704,384]{1,0:T(8,128)} custom-call(s32[32]{0:T(128)} %select_reduce_fusion.order, s32[32]{0:T(128)} %count.5, s32[32,128]{1,0:T(8,128)} %pad.23.pos, f32[8,384]{1,0:T(8,128)} %pad.28.cols, bf16[4704,384]{1,0:T(8,128)(2,1)} %patches.5, bf16[2048,384]{1,0:T(8,128)(2,1)} %bitcast.51), custom_call_target="tpu_custom_call" | custom-call | bytes 26400000 | tf_op jit(solution)/shard_map/spread_patch_grad/pallas_call | solution.py:571
  399.5 6.1 %collective-permute-done.42 = bf16[240,384]{1,0:T(8,128)(2,1)S(1)} collective-permute-done((bf16[240,384]{1,0:T(8,128)(2,1)}, bf16[240,384]{1,0:T(8,128)(2,1)S(1)}, u32[]{:S(2)}, u32[]{:S(2)}) %collective-permute-start.42) | collective-permute-done | bytes 184352 | tf_op jit(solution)/shard_map/ppermute | solution.py:35
  406.8 5.6 %collective-permute-done.40.b = bf16[240,768]{1,0:T(8,128)(2,1)S(1)} collective-permute-done((bf16[240,768]{1,0:T(8,128)(2,1)}, bf16[240,768]{1,0:T(8,128)(2,1)S(1)}, u32[]{:S(2)}, u32[]{:S(2)}) %collective-permute-start.40) | collective-permute-done | bytes 368672 | tf_op jit(solution)/shard_map/ppermute | solution.py:35
  415.3 5.6 %collective-permute-done.45 = bf16[240,768]{1,0:T(8,128)(2,1)S(1)} collective-permute-done((bf16[240,768]{1,0:T(8,128)(2,1)S(1)}, bf16[240,768]{1,0:T(8,128)(2,1)S(1)}, u32[]{:S(2)}, u32[]{:S(2)}) %collective-permute-start.45) | collective-permute-done | bytes 368672 | tf_op jit(solution)/shard_map/ppermute | solution.py:35
  428.4 9.1 %collective-permute-done.46 = bf16[240,384]{1,0:T(8,128)(2,1)S(1)} collective-permute-done((bf16[240,384]{1,0:T(8,128)(2,1)}, bf16[240,384]{1,0:T(8,128)(2,1)S(1)}, u32[]{:S(2)}, u32[]{:S(2)}) %collective-permute-start.46) | collective-permute-done | bytes 184352 | tf_op jit(solution)/shard_map/ppermute | solution.py:35
  442.9 5.6 %collective-permute-done.47 = bf16[240,768]{1,0:T(8,128)(2,1)S(1)} collective-permute-done((bf16[240,768]{1,0:T(8,128)(2,1)S(1)}, bf16[240,768]{1,0:T(8,128)(2,1)S(1)}, u32[]{:S(2)}, u32[]{:S(2)}) %collective-permute-start.47) | collective-permute-done | bytes 368672 | tf_op jit(solution)/shard_map/ppermute | solution.py:35
  455.9 9.9 %collective-permute-done.49.came = bf16[480,768]{1,0:T(8,128)(2,1)S(1)} collective-permute-done((bf16[480,768]{1,0:T(8,128)(2,1)S(1)}, bf16[480,768]{1,0:T(8,128)(2,1)S(1)}, u32[]{:S(2)}, u32[]{:S(2)}) %collective-permute-start.49) | collective-permute-done | bytes 737312 | tf_op jit(solution)/shard_map/ppermute | solution.py:35
  (351 shorter events, 217.3 us)
Async XLA Ops:
  19.0 22.2 %collective-permute-start.6 = (bf16[592,768]{1,0:T(8,128)(2,1)}, bf16[592,768]{1,0:T(8,128)(2,1)S(1)}, u32[]{:S(2)}, u32[]{:S(2)}) collective-permute-start(bf16[592,768]{1,0:T(8,128)(2,1)} %get-tuple-element.159), channel_id=1, source_target_pairs={{0,2},{1,3},{2,0},{3,1},{4,6},{5,7},{6,4},{7,5},{8,10},{9,11},{10,... | collective-permute-start | bytes 2727944 | tf_op jit(solution)/shard_map/ppermute | solution.py:35
  37.1 75.7 %collective-permute-start.5 = (bf16[1184,768]{1,0:T(8,128)(2,1)S(1)}, bf16[1184,768]{1,0:T(8,128)(2,1)}, u32[]{:S(2)}, u32[]{:S(2)}) collective-permute-start(bf16[1184,768]{1,0:T(8,128)(2,1)S(1)} %copy-done), channel_id=1, source_target_pairs={{0,1},{1,0},{2,3},{3,2},{4,5},{5,4},{6,7},{7,6},{8,9},{9,8},{10,11... | collective-permute-start | bytes 5455880 | tf_op jit(solution)/shard_map/ppermute | solution.py:35
  42.1 42.1 %all-to-all-start = ((bf16[8,256,384]{2,1,0:T(8,128)(2,1)}), bf16[8,256,384]{2,1,0:T(8,128)(2,1)S(1)}, u32[]{:S(2)}, u32[]{:S(2)}) async-start(bf16[8,256,384]{2,1,0:T(8,128)(2,1)} %bitcast.56), calls=%async_computation | async-start | bytes 3145728 | tf_op jit(solution)/shard_map/all_to_all | solution.py:756
  53.0 29.1 %collective-permute-start.8 = (bf16[832,768]{1,0:T(8,128)(2,1)}, bf16[832,768]{1,0:T(8,128)(2,1)}, u32[]{:S(2)}, u32[]{:S(2)}) collective-permute-start(bf16[832,768]{1,0:T(8,128)(2,1)} %get-tuple-element.162), channel_id=1, source_target_pairs={{0,2},{1,3},{2,0},{3,1},{4,6},{5,7},{6,4},{7,5},{8,10},{9,11},{10,... | collective-permute-start | bytes 3833864 | tf_op jit(solution)/shard_map/ppermute | solution.py:35
  53.6 34.5 %collective-permute-start.7 = (bf16[592,768]{1,0:T(8,128)(2,1)}, bf16[592,768]{1,0:T(8,128)(2,1)}, u32[]{:S(2)}, u32[]{:S(2)}) collective-permute-start(bf16[592,768]{1,0:T(8,128)(2,1)} %copy-done.16), channel_id=1, source_target_pairs={{0,4},{4,0},{8,12},{12,8},{16,20},{20,16},{24,28},{28,24},{1,5},{5... | collective-permute-start | bytes 2727944 | tf_op jit(solution)/shard_map/ppermute | solution.py:35
  90.9 27.6 %collective-permute-start.9 = (bf16[1184,768]{1,0:T(8,128)(2,1)}, bf16[1184,768]{1,0:T(8,128)(2,1)}, u32[]{:S(2)}, u32[]{:S(2)}) collective-permute-start(bf16[1184,768]{1,0:T(8,128)(2,1)} %join_weights.2.refs_5_.refs_2_), channel_id=1, source_target_pairs={{0,1},{1,0},{2,3},{3,2},{4,5},{5,4},{6,7},{7,6},{8,9},{9,8},{10,11... | collective-permute-start | bytes 5455880 | tf_op jit(solution)/shard_map/ppermute | solution.py:35
  90.9 20.2 %collective-permute-start.10 = (bf16[1024,384]{1,0:T(8,128)(2,1)}, bf16[1024,384]{1,0:T(8,128)(2,1)S(1)}, u32[]{:S(2)}, u32[]{:S(2)}) collective-permute-start(bf16[1024,384]{1,0:T(8,128)(2,1)} %get-tuple-element.164), channel_id=1, source_target_pairs={{0,2},{1,3},{2,0},{3,1},{4,6},{5,7},{6,4},{7,5},{8,10},{9,11},{10,... | collective-permute-start | bytes 2359304 | tf_op jit(solution)/shard_map/ppermute | solution.py:35
  91.4 24.3 %all-to-all-start.1 = ((bf16[8,256,128]{2,1,0:T(8,128)(2,1)}), bf16[8,256,128]{2,1,0:T(8,128)(2,1)}, u32[]{:S(2)}, u32[]{:S(2)}) async-start(bf16[8,256,128]{2,1,0:T(8,128)(2,1)} %bitcast.19), calls=%async_computation.1 | async-start | bytes 1048576 | tf_op jit(solution)/shard_map/all_to_all | solution.py:756
  112.2 37.7 %collective-permute-start.14 = (bf16[1664,768]{1,0:T(8,128)(2,1)}, bf16[1664,768]{1,0:T(8,128)(2,1)}, u32[]{:S(2)}, u32[]{:S(2)}) collective-permute-start(bf16[1664,768]{1,0:T(8,128)(2,1)} %get-tuple-element.178.refs_3_.refs_4_), channel_id=1, source_target_pairs={{0,1},{1,0},{2,3},{3,2},{4,5},{5,4},{6,7},{7,6},{8,9},{9,8},{10,11... | collective-permute-start | bytes 7667720 | tf_op jit(solution)/shard_map/ppermute | solution.py:35
  113.6 30.2 %collective-permute-start.15 = (bf16[832,768]{1,0:T(8,128)(2,1)}, bf16[832,768]{1,0:T(8,128)(2,1)S(1)}, u32[]{:S(2)}, u32[]{:S(2)}) collective-permute-start(bf16[832,768]{1,0:T(8,128)(2,1)} %collective-permute-done.8.direct), channel_id=1, source_target_pairs={{0,4},{4,0},{8,12},{12,8},{16,20},{20,16},{24,28},{28,24},{1,5},{5... | collective-permute-start | bytes 3833864 | tf_op jit(solution)/shard_map/ppermute | solution.py:35
  117.9 22.2 %collective-permute-start.12 = (bf16[1024,128]{1,0:T(8,128)(2,1)}, bf16[1024,128]{1,0:T(8,128)(2,1)}, u32[]{:S(2)}, u32[]{:S(2)}) collective-permute-start(bf16[1024,128]{1,0:T(8,128)(2,1)} %get-tuple-element.171), channel_id=1, source_target_pairs={{0,2},{1,3},{2,0},{3,1},{4,6},{5,7},{6,4},{7,5},{8,10},{9,11},{10,... | collective-permute-start | bytes 786440 | tf_op jit(solution)/shard_map/ppermute | solution.py:35
  196.4 37.4 %collective-permute-start.21 = (bf16[1920,768]{1,0:T(8,128)(2,1)}, bf16[1920,768]{1,0:T(8,128)(2,1)S(1)}, u32[]{:S(2)}, u32[]{:S(2)}) collective-permute-start(bf16[1920,768]{1,0:T(8,128)(2,1)} %get-tuple-element.206), channel_id=1, source_target_pairs={{0,1},{1,0},{2,3},{3,2},{4,5},{5,4},{6,7},{7,6},{8,9},{9,8},{10,11... | collective-permute-start | bytes 8847368 | tf_op jit(solution)/shard_map/ppermute | solution.py:35
  196.5 43.6 %collective-permute-start.20 = (bf16[896,768]{1,0:T(8,128)(2,1)}, bf16[896,768]{1,0:T(8,128)(2,1)}, u32[]{:S(2)}, u32[]{:S(2)}) collective-permute-start(bf16[896,768]{1,0:T(8,128)(2,1)} %get-tuple-element.203), channel_id=1, source_target_pairs={{0,2},{1,3},{2,0},{3,1},{4,6},{5,7},{6,4},{7,5},{8,10},{9,11},{10,... | collective-permute-start | bytes 4128776 | tf_op jit(solution)/shard_map/ppermute | solution.py:35
  218.7 27.0 %all-to-all-start.2 = ((bf16[8,256,128]{2,1,0:T(8,128)(2,1)}), bf16[8,256,128]{2,1,0:T(8,128)(2,1)S(1)}, u32[]{:S(2)}, u32[]{:S(2)}) async-start(bf16[8,256,128]{2,1,0:T(8,128)(2,1)} %bitcast.55), calls=%async_computation.2 | async-start | bytes 1048576 | tf_op jit(solution)/shard_map/all_to_all | solution.py:756
  231.0 33.2 %collective-permute-start.24 = (bf16[1024,384]{1,0:T(8,128)(2,1)}, bf16[1024,384]{1,0:T(8,128)(2,1)}, u32[]{:S(2)}, u32[]{:S(2)}) collective-permute-start(bf16[1024,384]{1,0:T(8,128)(2,1)} %get-tuple-element.220), channel_id=1, source_target_pairs={{0,2},{1,3},{2,0},{3,1},{4,6},{5,7},{6,4},{7,5},{8,10},{9,11},{10,... | collective-permute-start | bytes 2359304 | tf_op jit(solution)/shard_map/ppermute | solution.py:35
  245.2 20.2 %collective-permute-start.23 = (f32[32,768]{1,0:T(8,128)}, f32[32,768]{1,0:T(8,128)S(1)}, u32[]{:S(2)}, u32[]{:S(2)}) collective-permute-start(f32[32,768]{1,0:T(8,128)} %add.243), channel_id=1, source_target_pairs={{0,2},{1,3},{2,0},{3,1},{4,6},{5,7},{6,4},{7,5},{8,10},{9,11},{10,... | collective-permute-start | bytes 294920 | tf_op jit(solution)/shard_map/ppermute | solution.py:35
  268.6 66.2 %collective-permute-start.34 = (bf16[960,768]{1,0:T(8,128)(2,1)}, bf16[960,768]{1,0:T(8,128)(2,1)S(1)}, u32[]{:S(2)}, u32[]{:S(2)}) collective-permute-start(bf16[960,768]{1,0:T(8,128)(2,1)} %get-tuple-element.246), channel_id=1, source_target_pairs={{0,2},{1,3},{2,0},{3,1},{4,6},{5,7},{6,4},{7,5},{8,10},{9,11},{10,... | collective-permute-start | bytes 4423688 | tf_op jit(solution)/shard_map/ppermute | solution.py:35
  288.2 81.4 %all-to-all-start.3 = ((bf16[8,256,384]{2,1,0:T(8,128)(2,1)}), bf16[8,256,384]{2,1,0:T(8,128)(2,1)S(1)}, u32[]{:S(2)}, u32[]{:S(2)}) async-start(bf16[8,256,384]{2,1,0:T(8,128)(2,1)} %bitcast.53), calls=%async_computation.3 | async-start | bytes 3145728 | tf_op jit(solution)/shard_map/all_to_all | solution.py:756
  294.2 68.2 %collective-permute-start.32 = (bf16[960,768]{1,0:T(8,128)(2,1)}, bf16[960,768]{1,0:T(8,128)(2,1)S(1)}, u32[]{:S(2)}, u32[]{:S(2)}) collective-permute-start(bf16[960,768]{1,0:T(8,128)(2,1)} %get-tuple-element.243), channel_id=1, source_target_pairs={{0,2},{1,3},{2,0},{3,1},{4,6},{5,7},{6,4},{7,5},{8,10},{9,11},{10,... | collective-permute-start | bytes 4423688 | tf_op jit(solution)/shard_map/ppermute | solution.py:35
  294.8 32.8 %collective-permute-start.30 = (bf16[224,768]{1,0:T(8,128)(2,1)}, bf16[224,768]{1,0:T(8,128)(2,1)S(1)}, u32[]{:S(2)}, u32[]{:S(2)}) collective-permute-start(bf16[224,768]{1,0:T(8,128)(2,1)} %get-tuple-element.237), channel_id=1, source_target_pairs={{0,8},{4,12},{8,0},{12,4},{16,24},{20,28},{24,16},{28,20},{1,9},{5... | collective-permute-start | bytes 1032200 | tf_op jit(solution)/shard_map/ppermute | solution.py:35
  296.9 38.0 %collective-permute-start.29 = (f32[32,768]{1,0:T(8,128)S(1)}, f32[32,768]{1,0:T(8,128)S(1)}, u32[]{:S(2)}, u32[]{:S(2)}) collective-permute-start(f32[32,768]{1,0:T(8,128)S(1)} %add.246), channel_id=1, source_target_pairs={{0,16},{4,20},{8,24},{12,28},{16,0},{20,4},{24,8},{28,12},{1,17},{... | collective-permute-start | bytes 294920 | tf_op jit(solution)/shard_map/ppermute | solution.py:35
  366.7 19.1 %collective-permute-start.37 = (bf16[480,768]{1,0:T(8,128)(2,1)}, bf16[480,768]{1,0:T(8,128)(2,1)S(1)}, u32[]{:S(2)}, u32[]{:S(2)}) collective-permute-start(bf16[480,768]{1,0:T(8,128)(2,1)} %get-tuple-element.257), channel_id=1, source_target_pairs={{0,4},{4,0},{8,12},{12,8},{16,20},{20,16},{24,28},{28,24},{1,5},{5... | collective-permute-start | bytes 2211848 | tf_op jit(solution)/shard_map/ppermute | solution.py:35
  366.7 18.8 %collective-permute-start.38 = (bf16[224,768]{1,0:T(8,128)(2,1)S(1)}, bf16[224,768]{1,0:T(8,128)(2,1)S(1)}, u32[]{:S(2)}, u32[]{:S(2)}) collective-permute-start(bf16[224,768]{1,0:T(8,128)(2,1)S(1)} %maximum_select_fusion.5), channel_id=1, source_target_pairs={{0,8},{4,12},{8,0},{12,4},{16,24},{20,28},{24,16},{28,20},{1,9},{5... | collective-permute-start | bytes 1032200 | tf_op jit(solution)/shard_map/ppermute | solution.py:35
  394.8 27.3 %collective-permute-start.44 = (bf16[448,768]{1,0:T(8,128)(2,1)S(1)}, bf16[448,768]{1,0:T(8,128)(2,1)S(1)}, u32[]{:S(2)}, u32[]{:S(2)}) collective-permute-start(bf16[448,768]{1,0:T(8,128)(2,1)S(1)} %maximum_select_fusion.2.own), channel_id=1, source_target_pairs={{0,4},{4,0},{8,12},{12,8},{16,20},{20,16},{24,28},{28,24},{1,5},{5... | collective-permute-start | bytes 2064392 | tf_op jit(solution)/shard_map/ppermute | solution.py:35
  (85 other events, 756.8 us)

commit v4 on v3

--- a/solution.py
+++ b/solution.py
@@ -1112,7 +1112,7 @@
                 sums.step()
             kept["patch"] = patch_step(kept["grad"])
     chains = {"a": red_a, "b": red_b, "c": red_c, "s": sums}
-    for name in "cssHasbabacPbacbbcbaccbcc":
+    for name in "cassasabHabcabcbPcbcbcbcc":
         go(name)
     while sums.left:
         sums.step()

time: 477 us -> 470 us (0.985)
  waiting for transfers between devices: 161 us -> 145 us
  starting transfers between devices: 63.3 us -> 75.2 us
    ppermute x50, waiting for transfers between devices: 159 us -> 143 us  [swap(): return lax.ppermute(values, axis, [(i, i ^ bit) for i in range(size)])]
    ppermute x50, starting transfers between devices: 43.2 us -> 57 us  [swap(): return lax.ppermute(values, axis, [(i, i ^ bit) for i in range(size)])]
    unnamed x111 -> x115, local copies, waits for them, and re-layouts: 25.2 us -> 25.2 us
  transfers between devices with their start and end apart: 54 -> 54, of which waited for: 27 -> 23; matrix products, arithmetic and copies ran while one was open for 7% -> 7% of each run, Pallas kernels for 31% -> 31%
where the time goes in v4:
time: 470 us; the launch traced here: 463 us
  Pallas kernels  183 us (39%)
  waiting for transfers between devices  145 us (31%)
  starting transfers between devices  75.2 us (16%)
  local copies, waits for them, and re-layouts  46.2 us (10%)
  other arithmetic  11.8 us (3%)
    pallas_call x36, Pallas kernels, call(): return list(run(*args))  183 us
    ppermute x50, waiting for transfers between devices, swap(): return lax.ppermute(values, axis, [(i, i ^ bit) for i in range(size)])  143 us
    ppermute x50, starting transfers between devices, swap(): return lax.ppermute(values, axis, [(i, i ^ bit) for i in range(size)])  57 us
    unnamed x115, local copies, waits for them, and re-layouts  25.2 us
    all_to_all x4, starting transfers between devices, exchange(): lax.all_to_all(blocks, 'dp', split_axis=0, concat_axis=0, tiled=True)  18.2 us
  transfers between devices with their start and end apart: 54, of which 23 were waited for; matrix products, arithmetic and copies ran while one was open for 7% of the time, Pallas kernels for 31%

profile of v4, /device:TPU:0, one launch (start us, length us, event | category | flops | bytes accessed | tf_op | source)
XLA Modules:
  0.0 463.0 jit_solution(3818481213122184846)
XLA Ops:
  13.6 5.5 %prep_weights.1 = (bf16[1184,768]{1,0:T(8,128)(2,1)}, bf16[1664,768]{1,0:T(8,128)(2,1)}, bf16[592,768]{1,0:T(8,128)(2,1)}, bf16[832,768]{1,0:T(8,128)(2,1)}) custom-call(s32[1]{0:T(128)} %bitcast.4.odd.flag, bf16[192,768]{1,0:T(8,128)(2,1)} %bitcast.57, bf16[192,768]{1,0:T(8,128)(2,1)} %bitcast.58, bf16[192,768]{1,0:T(8,128)(2,1)} %bitcast.59, ...), custom_call_target="tpu_custom_call" | custom-call | bytes 16500000 | tf_op jit(solution)/shard_map/prep_weights/pallas_call | solution.py:571
  22.4 7.5 %pick_rows.1 = (bf16[2048,384]{1,0:T(8,128)(2,1)}, bf16[2048,128]{1,0:T(8,128)(2,1)}, f32[8,128]{1,0:T(8,128)}) custom-call(s32[32]{0:T(128)} %select_reduce_fusion.order, s32[32]{0:T(128)} %count.5, s32[32,128]{1,0:T(8,128)} %pad.23.pos, bf16[4704,384]{1,0:T(8,128)(2,1)} %patches.5, bf16[4704,128]{1,0:T(8,128)(2,1)} %cot.1), custom_call_target="tpu_custom_call" | custom-call | bytes 24750000 | tf_op jit(solution)/shard_map/pick_rows/pallas_call | solution.py:571
  42.1 5.8 %all-to-all-start = ((bf16[8,256,384]{2,1,0:T(8,128)(2,1)}), bf16[8,256,384]{2,1,0:T(8,128)(2,1)S(1)}, u32[]{:S(2)}, u32[]{:S(2)}) async-start(bf16[8,256,384]{2,1,0:T(8,128)(2,1)} %bitcast.56), calls=%async_computation | async-start | bytes 3145728 | tf_op jit(solution)/shard_map/all_to_all | solution.py:756
  59.4 22.6 %collective-permute-done.8.direct = bf16[832,768]{1,0:T(8,128)(2,1)} collective-permute-done((bf16[832,768]{1,0:T(8,128)(2,1)}, bf16[832,768]{1,0:T(8,128)(2,1)}, u32[]{:S(2)}, u32[]{:S(2)}) %collective-permute-start.8) | collective-permute-done | bytes 1277984 | tf_op jit(solution)/shard_map/ppermute | solution.py:35
  91.4 4.5 all-to-all-start.1
  95.9 15.1 %collective-permute-done.10.refs_2_ = bf16[1024,384]{1,0:T(8,128)(2,1)S(1)} collective-permute-done((bf16[1024,384]{1,0:T(8,128)(2,1)}, bf16[1024,384]{1,0:T(8,128)(2,1)S(1)}, u32[]{:S(2)}, u32[]{:S(2)}) %collective-permute-start.10) | collective-permute-done | bytes 786464 | tf_op jit(solution)/shard_map/ppermute | solution.py:35
  121.1 18.8 %embed_attend.1 = (bf16[512,768]{1,0:T(8,128)(2,1)}, bf16[512,768]{1,0:T(8,128)(2,1)}, bf16[512,768]{1,0:T(8,128)(2,1)}, bf16[512,768]{1,0:T(8,128)(2,1)}, bf16[...) custom-call(bf16[512,128]{1,0:T(8,128)(2,1)} %or_convert_fusion.chosen, ...), custom_call_target="tpu_custom_call" | custom-call | bytes 62700000 | tf_op jit(solution)/shard_map/embed_attend/pallas_call | solution.py:571
  155.0 18.9 %mlp_decode.1 = (bf16[512,128]{1,0:T(8,128)(2,1)}, bf16[512,128]{1,0:T(8,128)(2,1)}, bf16[1024,128]{1,0:T(8,128)(2,1)}, bf16[512,768]{1,0:T(8,128)(2,1)}, bf16[5...) custom-call(f32[512,768]{1,0:T(8,128)} %get-tuple-element.174.middle, ...), custom_call_target="tpu_custom_call" | custom-call | bytes 66000000 | tf_op jit(solution)/shard_map/mlp_decode/pallas_call | solution.py:571
  174.7 15.7 %hidden_back.1 = (bf16[1920,768]{1,0:T(8,128)(2,1)}, bf16[1920,768]{1,0:T(8,128)(2,1)}, f32[512,768]{1,0:T(8,128)}, f32[8,768]{1,0:T(8,128)}) custom-call(f32[512,768]{1,0:T(8,128)} %get-tuple-element.174.middle, f32[16,768]{1,0:T(8,128)} %concatenate.83.vecs, f32[512,768]{1,0:T(8,128)} %get-tuple-element.183.final_grad, ...), custom_call_target="tpu_custom_call" | custom-call | bytes 42900000 | tf_op jit(solution)/shard_map/hidden_back/pallas_call | solution.py:571
  192.0 4.4 reduce_out.5
  198.2 17.9 %attend_back.1 = (bf16[512,768]{1,0:T(8,128)(2,1)}, bf16[512,768]{1,0:T(8,128)(2,1)}, bf16[512,768]{1,0:T(8,128)(2,1)}, bf16[512,768]{1,0:T(8,128)(2,1)}, f32[8,768]{1,0:T(8,128)}) custom-call(f32[512,768]{1,0:T(8,128)} %get-tuple-element.195.middle_grad, bf16[512,768]{1,0:T(8,128)(2,1)} %get-tuple-element.196.start, bf16[512,768]{1,0:T(8,128)(2,1)} %get-tuple-element.197.q, ...), custom_call_target="tpu_custom_call" | custom-call | bytes 59400000 | tf_op jit(solution)/shard_map/attend_back/pallas_call | solution.py:571
  222.5 6.7 %pixel_grad.1 = (bf16[512,384]{1,0:T(8,128)(2,1)}, bf16[512,384]{1,0:T(8,128)(2,1)}, bf16[1024,384]{1,0:T(8,128)(2,1)}, f32[8,128]{1,0:T(8,128)}) custom-call(bf16[512,768]{1,0:T(8,128)(2,1)} %get-tuple-element.222.start_grad, f32[8,384]{1,0:T(8,128)} %select_maximum_fusion.cols, bf16[512,384]{1,0:T(8,128)(2,1)} %get-tuple-element.173.refs_0_, ...), custom_call_target="tpu_custom_call" | custom-call | bytes 22110000 | tf_op jit(solution)/shard_map/pixel_grad/pallas_call | solution.py:571
  235.5 4.7 %reduce_hidden.5 = (bf16[960,768]{1,0:T(8,128)(2,1)}, bf16[960,768]{1,0:T(8,128)(2,1)}) custom-call(bf16[1920,768]{1,0:T(8,128)(2,1)} %get-tuple-element.204.a, bf16[1920,768]{1,0:T(8,128)(2,1)} %copy-done.6), custom_call_target="tpu_custom_call" | custom-call | bytes 6600000 | tf_op jit(solution)/shard_map/reduce_hidden/pallas_call | solution.py:571
  249.9 8.7 %weight_grad.1 = (bf16[1920,768]{1,0:T(8,128)(2,1)}, bf16[1920,768]{1,0:T(8,128)(2,1)}) custom-call(bf16[512,768]{1,0:T(8,128)(2,1)} %get-tuple-element.222.start_grad, bf16[512,768]{1,0:T(8,128)(2,1)} %get-tuple-element.196.start, bf16[512,768]{1,0:T(8,128)(2,1)} %get-tuple-element.223.dq, bf16[512,768]{1,0:T(8,128)(2,1)} %get-tuple-element.224.dk, ...), custom_call_target="tpu_custom_call" | custom-call | bytes 33000000 | tf_op jit(solution)/shard_map/weight_grad/pallas_call | solution.py:571
  273.7 4.7 %reduce_first.5 = (bf16[960,768]{1,0:T(8,128)(2,1)}, bf16[960,768]{1,0:T(8,128)(2,1)}) custom-call(bf16[1920,768]{1,0:T(8,128)(2,1)} %get-tuple-element.226.a, bf16[1920,768]{1,0:T(8,128)(2,1)} %copy-done.7), custom_call_target="tpu_custom_call" | custom-call | bytes 6600000 | tf_op jit(solution)/shard_map/reduce_first/pallas_call | solution.py:571
  285.1 4.7 %collective-permute-done.29 = f32[32,768]{1,0:T(8,128)S(1)} collective-permute-done((f32[32,768]{1,0:T(8,128)S(1)}, f32[32,768]{1,0:T(8,128)S(1)}, u32[]{:S(2)}, u32[]{:S(2)}) %collective-permute-start.29) | collective-permute-done | bytes 98336 | tf_op jit(solution)/shard_map/ppermute | solution.py:35
  297.4 11.7 %collective-permute-done.30 = f32[32,768]{1,0:T(8,128)S(1)} collective-permute-done((f32[32,768]{1,0:T(8,128)S(1)}, f32[32,768]{1,0:T(8,128)S(1)}, u32[]{:S(2)}, u32[]{:S(2)}) %collective-permute-start.30) | collective-permute-done | bytes 98336 | tf_op jit(solution)/shard_map/ppermute | solution.py:35
  326.6 29.9 %collective-permute-done.36 = bf16[224,768]{1,0:T(8,128)(2,1)S(1)} collective-permute-done((bf16[224,768]{1,0:T(8,128)(2,1)S(1)}, bf16[224,768]{1,0:T(8,128)(2,1)S(1)}, u32[]{:S(2)}, u32[]{:S(2)}) %collective-permute-start.36) | collective-permute-done | bytes 344096 | tf_op jit(solution)/shard_map/ppermute | solution.py:35
  368.7 6.4 %collective-permute-done.38.came = bf16[448,768]{1,0:T(8,128)(2,1)S(1)} collective-permute-done((bf16[448,768]{1,0:T(8,128)(2,1)S(1)}, bf16[448,768]{1,0:T(8,128)(2,1)S(1)}, u32[]{:S(2)}, u32[]{:S(2)}) %collective-permute-start.38) | collective-permute-done | bytes 688160 | tf_op jit(solution)/shard_map/ppermute | solution.py:35
  400.0 8.0 %spread_patch_grad.1 = f32[4704,384]{1,0:T(8,128)} custom-call(s32[32]{0:T(128)} %select_reduce_fusion.order, s32[32]{0:T(128)} %count.5, s32[32,128]{1,0:T(8,128)} %pad.23.pos, f32[8,384]{1,0:T(8,128)} %pad.28.cols, bf16[4704,384]{1,0:T(8,128)(2,1)} %patches.5, bf16[2048,384]{1,0:T(8,128)(2,1)} %bitcast.51), custom_call_target="tpu_custom_call" | custom-call | bytes 26400000 | tf_op jit(solution)/shard_map/spread_patch_grad/pallas_call | solution.py:571
  412.9 9.5 %collective-permute-done.43.b = bf16[240,384]{1,0:T(8,128)(2,1)S(1)} collective-permute-done((bf16[240,384]{1,0:T(8,128)(2,1)}, bf16[240,384]{1,0:T(8,128)(2,1)S(1)}, u32[]{:S(2)}, u32[]{:S(2)}) %collective-permute-start.43) | collective-permute-done | bytes 184352 | tf_op jit(solution)/shard_map/ppermute | solution.py:35
  429.8 5.8 %collective-permute-done.45 = bf16[240,384]{1,0:T(8,128)(2,1)S(1)} collective-permute-done((bf16[240,384]{1,0:T(8,128)(2,1)}, bf16[240,384]{1,0:T(8,128)(2,1)S(1)}, u32[]{:S(2)}, u32[]{:S(2)}) %collective-permute-start.45) | collective-permute-done | bytes 184352 | tf_op jit(solution)/shard_map/ppermute | solution.py:35
  435.8 4.2 collective-permute-done.48.came
  449.7 8.9 %collective-permute-done.49.came = bf16[480,768]{1,0:T(8,128)(2,1)S(1)} collective-permute-done((bf16[480,768]{1,0:T(8,128)(2,1)S(1)}, bf16[480,768]{1,0:T(8,128)(2,1)S(1)}, u32[]{:S(2)}, u32[]{:S(2)}) %collective-permute-start.49) | collective-permute-done | bytes 737312 | tf_op jit(solution)/shard_map/ppermute | solution.py:35
  (355 shorter events, 210.7 us)
Async XLA Ops:
  19.0 22.2 %collective-permute-start.6 = (bf16[592,768]{1,0:T(8,128)(2,1)}, bf16[592,768]{1,0:T(8,128)(2,1)S(1)}, u32[]{:S(2)}, u32[]{:S(2)}) collective-permute-start(bf16[592,768]{1,0:T(8,128)(2,1)} %get-tuple-element.159), channel_id=1, source_target_pairs={{0,2},{1,3},{2,0},{3,1},{4,6},{5,7},{6,4},{7,5},{8,10},{9,11},{10,... | collective-permute-start | bytes 2727944 | tf_op jit(solution)/shard_map/ppermute | solution.py:35
  37.1 75.7 %collective-permute-start.5 = (bf16[1184,768]{1,0:T(8,128)(2,1)S(1)}, bf16[1184,768]{1,0:T(8,128)(2,1)}, u32[]{:S(2)}, u32[]{:S(2)}) collective-permute-start(bf16[1184,768]{1,0:T(8,128)(2,1)S(1)} %copy-done), channel_id=1, source_target_pairs={{0,1},{1,0},{2,3},{3,2},{4,5},{5,4},{6,7},{7,6},{8,9},{9,8},{10,11... | collective-permute-start | bytes 5455880 | tf_op jit(solution)/shard_map/ppermute | solution.py:35
  42.1 42.1 %all-to-all-start = ((bf16[8,256,384]{2,1,0:T(8,128)(2,1)}), bf16[8,256,384]{2,1,0:T(8,128)(2,1)S(1)}, u32[]{:S(2)}, u32[]{:S(2)}) async-start(bf16[8,256,384]{2,1,0:T(8,128)(2,1)} %bitcast.56), calls=%async_computation | async-start | bytes 3145728 | tf_op jit(solution)/shard_map/all_to_all | solution.py:756
  53.0 29.1 %collective-permute-start.8 = (bf16[832,768]{1,0:T(8,128)(2,1)}, bf16[832,768]{1,0:T(8,128)(2,1)}, u32[]{:S(2)}, u32[]{:S(2)}) collective-permute-start(bf16[832,768]{1,0:T(8,128)(2,1)} %get-tuple-element.162), channel_id=1, source_target_pairs={{0,2},{1,3},{2,0},{3,1},{4,6},{5,7},{6,4},{7,5},{8,10},{9,11},{10,... | collective-permute-start | bytes 3833864 | tf_op jit(solution)/shard_map/ppermute | solution.py:35
  53.6 34.5 %collective-permute-start.7 = (bf16[592,768]{1,0:T(8,128)(2,1)}, bf16[592,768]{1,0:T(8,128)(2,1)}, u32[]{:S(2)}, u32[]{:S(2)}) collective-permute-start(bf16[592,768]{1,0:T(8,128)(2,1)} %copy-done.16), channel_id=1, source_target_pairs={{0,4},{4,0},{8,12},{12,8},{16,20},{20,16},{24,28},{28,24},{1,5},{5... | collective-permute-start | bytes 2727944 | tf_op jit(solution)/shard_map/ppermute | solution.py:35
  90.9 27.6 %collective-permute-start.9 = (bf16[1184,768]{1,0:T(8,128)(2,1)}, bf16[1184,768]{1,0:T(8,128)(2,1)}, u32[]{:S(2)}, u32[]{:S(2)}) collective-permute-start(bf16[1184,768]{1,0:T(8,128)(2,1)} %join_weights.2.refs_5_.refs_2_), channel_id=1, source_target_pairs={{0,1},{1,0},{2,3},{3,2},{4,5},{5,4},{6,7},{7,6},{8,9},{9,8},{10,11... | collective-permute-start | bytes 5455880 | tf_op jit(solution)/shard_map/ppermute | solution.py:35
  90.9 20.2 %collective-permute-start.10 = (bf16[1024,384]{1,0:T(8,128)(2,1)}, bf16[1024,384]{1,0:T(8,128)(2,1)S(1)}, u32[]{:S(2)}, u32[]{:S(2)}) collective-permute-start(bf16[1024,384]{1,0:T(8,128)(2,1)} %get-tuple-element.164), channel_id=1, source_target_pairs={{0,2},{1,3},{2,0},{3,1},{4,6},{5,7},{6,4},{7,5},{8,10},{9,11},{10,... | collective-permute-start | bytes 2359304 | tf_op jit(solution)/shard_map/ppermute | solution.py:35
  91.4 24.3 %all-to-all-start.1 = ((bf16[8,256,128]{2,1,0:T(8,128)(2,1)}), bf16[8,256,128]{2,1,0:T(8,128)(2,1)}, u32[]{:S(2)}, u32[]{:S(2)}) async-start(bf16[8,256,128]{2,1,0:T(8,128)(2,1)} %bitcast.19), calls=%async_computation.1 | async-start | bytes 1048576 | tf_op jit(solution)/shard_map/all_to_all | solution.py:756
  112.2 37.6 %collective-permute-start.14 = (bf16[1664,768]{1,0:T(8,128)(2,1)}, bf16[1664,768]{1,0:T(8,128)(2,1)}, u32[]{:S(2)}, u32[]{:S(2)}) collective-permute-start(bf16[1664,768]{1,0:T(8,128)(2,1)} %get-tuple-element.178.refs_3_.refs_4_), channel_id=1, source_target_pairs={{0,1},{1,0},{2,3},{3,2},{4,5},{5,4},{6,7},{7,6},{8,9},{9,8},{10,11... | collective-permute-start | bytes 7667720 | tf_op jit(solution)/shard_map/ppermute | solution.py:35
  113.6 30.2 %collective-permute-start.15 = (bf16[832,768]{1,0:T(8,128)(2,1)}, bf16[832,768]{1,0:T(8,128)(2,1)S(1)}, u32[]{:S(2)}, u32[]{:S(2)}) collective-permute-start(bf16[832,768]{1,0:T(8,128)(2,1)} %collective-permute-done.8.direct), channel_id=1, source_target_pairs={{0,4},{4,0},{8,12},{12,8},{16,20},{20,16},{24,28},{28,24},{1,5},{5... | collective-permute-start | bytes 3833864 | tf_op jit(solution)/shard_map/ppermute | solution.py:35
  117.9 22.0 %collective-permute-start.12 = (bf16[1024,128]{1,0:T(8,128)(2,1)}, bf16[1024,128]{1,0:T(8,128)(2,1)}, u32[]{:S(2)}, u32[]{:S(2)}) collective-permute-start(bf16[1024,128]{1,0:T(8,128)(2,1)} %get-tuple-element.171), channel_id=1, source_target_pairs={{0,2},{1,3},{2,0},{3,1},{4,6},{5,7},{6,4},{7,5},{8,10},{9,11},{10,... | collective-permute-start | bytes 786440 | tf_op jit(solution)/shard_map/ppermute | solution.py:35
  196.4 37.4 %collective-permute-start.21 = (bf16[1920,768]{1,0:T(8,128)(2,1)}, bf16[1920,768]{1,0:T(8,128)(2,1)S(1)}, u32[]{:S(2)}, u32[]{:S(2)}) collective-permute-start(bf16[1920,768]{1,0:T(8,128)(2,1)} %get-tuple-element.206), channel_id=1, source_target_pairs={{0,1},{1,0},{2,3},{3,2},{4,5},{5,4},{6,7},{7,6},{8,9},{9,8},{10,11... | collective-permute-start | bytes 8847368 | tf_op jit(solution)/shard_map/ppermute | solution.py:35
  196.5 43.7 %collective-permute-start.20 = (bf16[896,768]{1,0:T(8,128)(2,1)}, bf16[896,768]{1,0:T(8,128)(2,1)}, u32[]{:S(2)}, u32[]{:S(2)}) collective-permute-start(bf16[896,768]{1,0:T(8,128)(2,1)} %get-tuple-element.203), channel_id=1, source_target_pairs={{0,2},{1,3},{2,0},{3,1},{4,6},{5,7},{6,4},{7,5},{8,10},{9,11},{10,... | collective-permute-start | bytes 4128776 | tf_op jit(solution)/shard_map/ppermute | solution.py:35
  218.7 27.1 %all-to-all-start.2 = ((bf16[8,256,128]{2,1,0:T(8,128)(2,1)}), bf16[8,256,128]{2,1,0:T(8,128)(2,1)S(1)}, u32[]{:S(2)}, u32[]{:S(2)}) async-start(bf16[8,256,128]{2,1,0:T(8,128)(2,1)} %bitcast.55), calls=%async_computation.2 | async-start | bytes 1048576 | tf_op jit(solution)/shard_map/all_to_all | solution.py:756
  231.1 33.3 %collective-permute-start.24 = (bf16[1024,384]{1,0:T(8,128)(2,1)}, bf16[1024,384]{1,0:T(8,128)(2,1)}, u32[]{:S(2)}, u32[]{:S(2)}) collective-permute-start(bf16[1024,384]{1,0:T(8,128)(2,1)} %get-tuple-element.220), channel_id=1, source_target_pairs={{0,2},{1,3},{2,0},{3,1},{4,6},{5,7},{6,4},{7,5},{8,10},{9,11},{10,... | collective-permute-start | bytes 2359304 | tf_op jit(solution)/shard_map/ppermute | solution.py:35
  245.3 20.2 %collective-permute-start.23 = (f32[32,768]{1,0:T(8,128)}, f32[32,768]{1,0:T(8,128)S(1)}, u32[]{:S(2)}, u32[]{:S(2)}) collective-permute-start(f32[32,768]{1,0:T(8,128)} %add.243), channel_id=1, source_target_pairs={{0,2},{1,3},{2,0},{3,1},{4,6},{5,7},{6,4},{7,5},{8,10},{9,11},{10,... | collective-permute-start | bytes 294920 | tf_op jit(solution)/shard_map/ppermute | solution.py:35
  266.5 43.7 %collective-permute-start.33 = (bf16[960,768]{1,0:T(8,128)(2,1)}, bf16[960,768]{1,0:T(8,128)(2,1)S(1)}, u32[]{:S(2)}, u32[]{:S(2)}) collective-permute-start(bf16[960,768]{1,0:T(8,128)(2,1)} %get-tuple-element.245), channel_id=1, source_target_pairs={{0,2},{1,3},{2,0},{3,1},{4,6},{5,7},{6,4},{7,5},{8,10},{9,11},{10,... | collective-permute-start | bytes 4423688 | tf_op jit(solution)/shard_map/ppermute | solution.py:35
  268.9 45.6 %collective-permute-start.32 = (bf16[1024,384]{1,0:T(8,128)(2,1)S(1)}, bf16[1024,384]{1,0:T(8,128)(2,1)S(1)}, u32[]{:S(2)}, u32[]{:S(2)}) collective-permute-start(bf16[1024,384]{1,0:T(8,128)(2,1)S(1)} %pad_maximum_fusion.1), channel_id=1, source_target_pairs={{0,1},{1,0},{2,3},{3,2},{4,5},{5,4},{6,7},{7,6},{8,9},{9,8},{10,11... | collective-permute-start | bytes 2359304 | tf_op jit(solution)/shard_map/ppermute | solution.py:35
  318.4 80.5 %all-to-all-start.3 = ((bf16[8,256,384]{2,1,0:T(8,128)(2,1)}), bf16[8,256,384]{2,1,0:T(8,128)(2,1)S(1)}, u32[]{:S(2)}, u32[]{:S(2)}) async-start(bf16[8,256,384]{2,1,0:T(8,128)(2,1)} %bitcast.53), calls=%async_computation.3 | async-start | bytes 3145728 | tf_op jit(solution)/shard_map/all_to_all | solution.py:756
  322.4 38.4 %collective-permute-start.39 = (bf16[960,768]{1,0:T(8,128)(2,1)}, bf16[960,768]{1,0:T(8,128)(2,1)S(1)}, u32[]{:S(2)}, u32[]{:S(2)}) collective-permute-start(bf16[960,768]{1,0:T(8,128)(2,1)} %get-tuple-element.255), channel_id=1, source_target_pairs={{0,2},{1,3},{2,0},{3,1},{4,6},{5,7},{6,4},{7,5},{8,10},{9,11},{10,... | collective-permute-start | bytes 4423688 | tf_op jit(solution)/shard_map/ppermute | solution.py:35
  323.1 34.6 %collective-permute-start.35 = (bf16[480,768]{1,0:T(8,128)(2,1)S(1)}, bf16[480,768]{1,0:T(8,128)(2,1)S(1)}, u32[]{:S(2)}, u32[]{:S(2)}) collective-permute-start(bf16[480,768]{1,0:T(8,128)(2,1)S(1)} %copy-done.49), channel_id=1, source_target_pairs={{0,4},{4,0},{8,12},{12,8},{16,20},{20,16},{24,28},{28,24},{1,5},{5... | collective-permute-start | bytes 2211848 | tf_op jit(solution)/shard_map/ppermute | solution.py:35
  325.1 31.3 %collective-permute-start.36 = (bf16[224,768]{1,0:T(8,128)(2,1)S(1)}, bf16[224,768]{1,0:T(8,128)(2,1)S(1)}, u32[]{:S(2)}, u32[]{:S(2)}) collective-permute-start(bf16[224,768]{1,0:T(8,128)(2,1)S(1)} %maximum_select_fusion.5), channel_id=1, source_target_pairs={{0,8},{4,12},{8,0},{12,4},{16,24},{20,28},{24,16},{28,20},{1,9},{5... | collective-permute-start | bytes 1032200 | tf_op jit(solution)/shard_map/ppermute | solution.py:35
  356.7 18.4 %collective-permute-start.38 = (bf16[448,768]{1,0:T(8,128)(2,1)S(1)}, bf16[448,768]{1,0:T(8,128)(2,1)S(1)}, u32[]{:S(2)}, u32[]{:S(2)}) collective-permute-start(bf16[448,768]{1,0:T(8,128)(2,1)S(1)} %maximum_select_fusion.2.own), channel_id=1, source_target_pairs={{0,4},{4,0},{8,12},{12,8},{16,20},{20,16},{24,28},{28,24},{1,5},{5... | collective-permute-start | bytes 2064392 | tf_op jit(solution)/shard_map/ppermute | solution.py:35
  365.1 23.9 %collective-permute-start.41 = (bf16[480,768]{1,0:T(8,128)(2,1)}, bf16[480,768]{1,0:T(8,128)(2,1)S(1)}, u32[]{:S(2)}, u32[]{:S(2)}) collective-permute-start(bf16[480,768]{1,0:T(8,128)(2,1)} %get-tuple-element.263), channel_id=1, source_target_pairs={{0,4},{4,0},{8,12},{12,8},{16,20},{20,16},{24,28},{28,24},{1,5},{5... | collective-permute-start | bytes 2211848 | tf_op jit(solution)/shard_map/ppermute | solution.py:35
  (87 other events, 711.4 us)

commit v5 on v4

--- a/solution.py
+++ b/solution.py
@@ -1112,7 +1112,7 @@
                 sums.step()
             kept["patch"] = patch_step(kept["grad"])
     chains = {"a": red_a, "b": red_b, "c": red_c, "s": sums}
-    for name in "cassasabHabcabcbPcbcbcbcc":
+    for name in "cassabsabacbHabcbcPbccbcc":
         go(name)
     while sums.left:
         sums.step()

time: 470 us -> 487 us (1.036)
  waiting for transfers between devices: 145 us -> 167 us
  starting transfers between devices: 75.2 us -> 69.5 us
    ppermute x50, waiting for transfers between devices: 143 us -> 165 us  [swap(): return lax.ppermute(values, axis, [(i, i ^ bit) for i in range(size)])]
    ppermute x50, starting transfers between devices: 57 us -> 50.1 us  [swap(): return lax.ppermute(values, axis, [(i, i ^ bit) for i in range(size)])]
  transfers between devices with their start and end apart: 54 -> 54, of which waited for: 23 -> 28; matrix products, arithmetic and copies ran while one was open for 7% -> 7% of each run, Pallas kernels for 31% -> 30%
where the time goes in v5:
time: 487 us; the launch traced here: 480 us
  Pallas kernels  183 us (38%)
  waiting for transfers between devices  167 us (34%)
  starting transfers between devices  69.5 us (14%)
  local copies, waits for them, and re-layouts  46.3 us (10%)
  other arithmetic  11.7 us (2%)
    pallas_call x36, Pallas kernels, call(): return list(run(*args))  183 us
    ppermute x50, waiting for transfers between devices, swap(): return lax.ppermute(values, axis, [(i, i ^ bit) for i in range(size)])  165 us
    ppermute x50, starting transfers between devices, swap(): return lax.ppermute(values, axis, [(i, i ^ bit) for i in range(size)])  50.1 us
    unnamed x115, local copies, waits for them, and re-layouts  25.2 us
    all_to_all x4, starting transfers between devices, exchange(): lax.all_to_all(blocks, 'dp', split_axis=0, concat_axis=0, tiled=True)  19.4 us
  transfers between devices with their start and end apart: 54, of which 28 were waited for; matrix products, arithmetic and copies ran while one was open for 7% of the time, Pallas kernels for 30%

profile of v5, /device:TPU:0, one launch (start us, length us, event | category | flops | bytes accessed | tf_op | source)
XLA Modules:
  0.0 479.5 jit_solution(3854092402953448918)
XLA Ops:
  13.6 5.5 %prep_weights.1 = (bf16[1184,768]{1,0:T(8,128)(2,1)}, bf16[1664,768]{1,0:T(8,128)(2,1)}, bf16[592,768]{1,0:T(8,128)(2,1)}, bf16[832,768]{1,0:T(8,128)(2,1)}) custom-call(s32[1]{0:T(128)} %bitcast.4.odd.flag, bf16[192,768]{1,0:T(8,128)(2,1)} %bitcast.57, bf16[192,768]{1,0:T(8,128)(2,1)} %bitcast.58, bf16[192,768]{1,0:T(8,128)(2,1)} %bitcast.59, ...), custom_call_target="tpu_custom_call" | custom-call | bytes 16500000 | tf_op jit(solution)/shard_map/prep_weights/pallas_call | solution.py:571
  22.4 7.5 %pick_rows.1 = (bf16[2048,384]{1,0:T(8,128)(2,1)}, bf16[2048,128]{1,0:T(8,128)(2,1)}, f32[8,128]{1,0:T(8,128)}) custom-call(s32[32]{0:T(128)} %select_reduce_fusion.order, s32[32]{0:T(128)} %count.5, s32[32,128]{1,0:T(8,128)} %pad.23.pos, bf16[4704,384]{1,0:T(8,128)(2,1)} %patches.5, bf16[4704,128]{1,0:T(8,128)(2,1)} %cot.1), custom_call_target="tpu_custom_call" | custom-call | bytes 24750000 | tf_op jit(solution)/shard_map/pick_rows/pallas_call | solution.py:571
  42.1 5.8 %all-to-all-start = ((bf16[8,256,384]{2,1,0:T(8,128)(2,1)}), bf16[8,256,384]{2,1,0:T(8,128)(2,1)S(1)}, u32[]{:S(2)}, u32[]{:S(2)}) async-start(bf16[8,256,384]{2,1,0:T(8,128)(2,1)} %bitcast.56), calls=%async_computation | async-start | bytes 3145728 | tf_op jit(solution)/shard_map/all_to_all | solution.py:756
  59.4 22.6 %collective-permute-done.8.direct = bf16[832,768]{1,0:T(8,128)(2,1)} collective-permute-done((bf16[832,768]{1,0:T(8,128)(2,1)}, bf16[832,768]{1,0:T(8,128)(2,1)}, u32[]{:S(2)}, u32[]{:S(2)}) %collective-permute-start.8) | collective-permute-done | bytes 1277984 | tf_op jit(solution)/shard_map/ppermute | solution.py:35
  91.4 4.5 all-to-all-start.1
  95.9 15.1 %collective-permute-done.10.refs_2_ = bf16[1024,384]{1,0:T(8,128)(2,1)S(1)} collective-permute-done((bf16[1024,384]{1,0:T(8,128)(2,1)}, bf16[1024,384]{1,0:T(8,128)(2,1)S(1)}, u32[]{:S(2)}, u32[]{:S(2)}) %collective-permute-start.10) | collective-permute-done | bytes 786464 | tf_op jit(solution)/shard_map/ppermute | solution.py:35
  121.1 18.8 %embed_attend.1 = (bf16[512,768]{1,0:T(8,128)(2,1)}, bf16[512,768]{1,0:T(8,128)(2,1)}, bf16[512,768]{1,0:T(8,128)(2,1)}, bf16[512,768]{1,0:T(8,128)(2,1)}, bf16[...) custom-call(bf16[512,128]{1,0:T(8,128)(2,1)} %or_convert_fusion.chosen, ...), custom_call_target="tpu_custom_call" | custom-call | bytes 62700000 | tf_op jit(solution)/shard_map/embed_attend/pallas_call | solution.py:571
  155.0 18.9 %mlp_decode.1 = (bf16[512,128]{1,0:T(8,128)(2,1)}, bf16[512,128]{1,0:T(8,128)(2,1)}, bf16[1024,128]{1,0:T(8,128)(2,1)}, bf16[512,768]{1,0:T(8,128)(2,1)}, bf16[5...) custom-call(f32[512,768]{1,0:T(8,128)} %get-tuple-element.174.middle, ...), custom_call_target="tpu_custom_call" | custom-call | bytes 66000000 | tf_op jit(solution)/shard_map/mlp_decode/pallas_call | solution.py:571
  174.7 15.7 %hidden_back.1 = (bf16[1920,768]{1,0:T(8,128)(2,1)}, bf16[1920,768]{1,0:T(8,128)(2,1)}, f32[512,768]{1,0:T(8,128)}, f32[8,768]{1,0:T(8,128)}) custom-call(f32[512,768]{1,0:T(8,128)} %get-tuple-element.174.middle, f32[16,768]{1,0:T(8,128)} %concatenate.83.vecs, f32[512,768]{1,0:T(8,128)} %get-tuple-element.183.final_grad, ...), custom_call_target="tpu_custom_call" | custom-call | bytes 42900000 | tf_op jit(solution)/shard_map/hidden_back/pallas_call | solution.py:571
  198.2 17.9 %attend_back.1 = (bf16[512,768]{1,0:T(8,128)(2,1)}, bf16[512,768]{1,0:T(8,128)(2,1)}, bf16[512,768]{1,0:T(8,128)(2,1)}, bf16[512,768]{1,0:T(8,128)(2,1)}, f32[8,768]{1,0:T(8,128)}) custom-call(f32[512,768]{1,0:T(8,128)} %get-tuple-element.195.middle_grad, bf16[512,768]{1,0:T(8,128)(2,1)} %get-tuple-element.196.start, bf16[512,768]{1,0:T(8,128)(2,1)} %get-tuple-element.197.q, ...), custom_call_target="tpu_custom_call" | custom-call | bytes 59400000 | tf_op jit(solution)/shard_map/attend_back/pallas_call | solution.py:571
  222.5 6.7 %pixel_grad.1 = (bf16[512,384]{1,0:T(8,128)(2,1)}, bf16[512,384]{1,0:T(8,128)(2,1)}, bf16[1024,384]{1,0:T(8,128)(2,1)}, f32[8,128]{1,0:T(8,128)}) custom-call(bf16[512,768]{1,0:T(8,128)(2,1)} %get-tuple-element.222.start_grad, f32[8,384]{1,0:T(8,128)} %select_maximum_fusion.cols, bf16[512,384]{1,0:T(8,128)(2,1)} %get-tuple-element.173.refs_0_, ...), custom_call_target="tpu_custom_call" | custom-call | bytes 22110000 | tf_op jit(solution)/shard_map/pixel_grad/pallas_call | solution.py:571
  235.5 4.7 reduce_hidden.5
  249.9 8.7 %weight_grad.1 = (bf16[1920,768]{1,0:T(8,128)(2,1)}, bf16[1920,768]{1,0:T(8,128)(2,1)}) custom-call(bf16[512,768]{1,0:T(8,128)(2,1)} %get-tuple-element.222.start_grad, bf16[512,768]{1,0:T(8,128)(2,1)} %get-tuple-element.196.start, bf16[512,768]{1,0:T(8,128)(2,1)} %get-tuple-element.223.dq, bf16[512,768]{1,0:T(8,128)(2,1)} %get-tuple-element.224.dk, ...), custom_call_target="tpu_custom_call" | custom-call | bytes 33000000 | tf_op jit(solution)/shard_map/weight_grad/pallas_call | solution.py:571
  273.7 4.7 reduce_first.5
  296.3 5.4 %collective-permute-done.31.b = bf16[960,768]{1,0:T(8,128)(2,1)S(1)} collective-permute-done((bf16[960,768]{1,0:T(8,128)(2,1)S(1)}, bf16[960,768]{1,0:T(8,128)(2,1)S(1)}, u32[]{:S(2)}, u32[]{:S(2)}) %collective-permute-start.31) | collective-permute-done | bytes 1474592 | tf_op jit(solution)/shard_map/ppermute | solution.py:35
  310.7 12.7 %collective-permute-done.30 = f32[32,768]{1,0:T(8,128)S(1)} collective-permute-done((f32[32,768]{1,0:T(8,128)S(1)}, f32[32,768]{1,0:T(8,128)S(1)}, u32[]{:S(2)}, u32[]{:S(2)}) %collective-permute-start.30) | collective-permute-done | bytes 98336 | tf_op jit(solution)/shard_map/ppermute | solution.py:35
  328.7 5.8 %collective-permute-done.38 = bf16[224,768]{1,0:T(8,128)(2,1)S(1)} collective-permute-done((bf16[224,768]{1,0:T(8,128)(2,1)S(1)}, bf16[224,768]{1,0:T(8,128)(2,1)S(1)}, u32[]{:S(2)}, u32[]{:S(2)}) %collective-permute-start.38) | collective-permute-done | bytes 344096 | tf_op jit(solution)/shard_map/ppermute | solution.py:35
  347.5 5.3 %all-to-all-start.3 = ((bf16[8,256,384]{2,1,0:T(8,128)(2,1)}), bf16[8,256,384]{2,1,0:T(8,128)(2,1)S(1)}, u32[]{:S(2)}, u32[]{:S(2)}) async-start(bf16[8,256,384]{2,1,0:T(8,128)(2,1)} %bitcast.53), calls=%async_computation.3 | async-start | bytes 3145728 | tf_op jit(solution)/shard_map/all_to_all | solution.py:756
  357.9 30.2 %collective-permute-done.41.came = bf16[448,768]{1,0:T(8,128)(2,1)S(1)} collective-permute-done((bf16[448,768]{1,0:T(8,128)(2,1)S(1)}, bf16[448,768]{1,0:T(8,128)(2,1)S(1)}, u32[]{:S(2)}, u32[]{:S(2)}) %collective-permute-start.41) | collective-permute-done | bytes 688160 | tf_op jit(solution)/shard_map/ppermute | solution.py:35
  392.0 5.0 %collective-permute-done.40.b = bf16[240,384]{1,0:T(8,128)(2,1)S(1)} collective-permute-done((bf16[240,384]{1,0:T(8,128)(2,1)S(1)}, bf16[240,384]{1,0:T(8,128)(2,1)S(1)}, u32[]{:S(2)}, u32[]{:S(2)}) %collective-permute-start.40) | collective-permute-done | bytes 184352 | tf_op jit(solution)/shard_map/ppermute | solution.py:35
  412.2 8.8 %collective-permute-done.42.b = bf16[240,768]{1,0:T(8,128)(2,1)S(1)} collective-permute-done((bf16[240,768]{1,0:T(8,128)(2,1)}, bf16[240,768]{1,0:T(8,128)(2,1)S(1)}, u32[]{:S(2)}, u32[]{:S(2)}) %collective-permute-start.42) | collective-permute-done | bytes 368672 | tf_op jit(solution)/shard_map/ppermute | solution.py:35
  424.7 8.0 %spread_patch_grad.1 = f32[4704,384]{1,0:T(8,128)} custom-call(s32[32]{0:T(128)} %select_reduce_fusion.order, s32[32]{0:T(128)} %count.5, s32[32,128]{1,0:T(8,128)} %pad.23.pos, f32[8,384]{1,0:T(8,128)} %pad.28.cols, bf16[4704,384]{1,0:T(8,128)(2,1)} %patches.5, bf16[2048,384]{1,0:T(8,128)(2,1)} %bitcast.52), custom_call_target="tpu_custom_call" | custom-call | bytes 26400000 | tf_op jit(solution)/shard_map/spread_patch_grad/pallas_call | solution.py:571
  440.7 6.8 %collective-permute-done.46 = bf16[240,384]{1,0:T(8,128)(2,1)S(1)} collective-permute-done((bf16[240,384]{1,0:T(8,128)(2,1)}, bf16[240,384]{1,0:T(8,128)(2,1)S(1)}, u32[]{:S(2)}, u32[]{:S(2)}) %collective-permute-start.46) | collective-permute-done | bytes 184352 | tf_op jit(solution)/shard_map/ppermute | solution.py:35
  462.7 12.5 %collective-permute-done.49.came = bf16[480,768]{1,0:T(8,128)(2,1)S(1)} collective-permute-done((bf16[480,768]{1,0:T(8,128)(2,1)S(1)}, bf16[480,768]{1,0:T(8,128)(2,1)S(1)}, u32[]{:S(2)}, u32[]{:S(2)}) %collective-permute-start.49) | collective-permute-done | bytes 737312 | tf_op jit(solution)/shard_map/ppermute | solution.py:35
  (355 shorter events, 220.3 us)
Async XLA Ops:
  19.0 22.2 %collective-permute-start.6 = (bf16[592,768]{1,0:T(8,128)(2,1)}, bf16[592,768]{1,0:T(8,128)(2,1)S(1)}, u32[]{:S(2)}, u32[]{:S(2)}) collective-permute-start(bf16[592,768]{1,0:T(8,128)(2,1)} %get-tuple-element.159), channel_id=1, source_target_pairs={{0,2},{1,3},{2,0},{3,1},{4,6},{5,7},{6,4},{7,5},{8,10},{9,11},{10,... | collective-permute-start | bytes 2727944 | tf_op jit(solution)/shard_map/ppermute | solution.py:35
  37.1 75.7 %collective-permute-start.5 = (bf16[1184,768]{1,0:T(8,128)(2,1)S(1)}, bf16[1184,768]{1,0:T(8,128)(2,1)}, u32[]{:S(2)}, u32[]{:S(2)}) collective-permute-start(bf16[1184,768]{1,0:T(8,128)(2,1)S(1)} %copy-done), channel_id=1, source_target_pairs={{0,1},{1,0},{2,3},{3,2},{4,5},{5,4},{6,7},{7,6},{8,9},{9,8},{10,11... | collective-permute-start | bytes 5455880 | tf_op jit(solution)/shard_map/ppermute | solution.py:35
  42.1 42.1 %all-to-all-start = ((bf16[8,256,384]{2,1,0:T(8,128)(2,1)}), bf16[8,256,384]{2,1,0:T(8,128)(2,1)S(1)}, u32[]{:S(2)}, u32[]{:S(2)}) async-start(bf16[8,256,384]{2,1,0:T(8,128)(2,1)} %bitcast.56), calls=%async_computation | async-start | bytes 3145728 | tf_op jit(solution)/shard_map/all_to_all | solution.py:756
  53.0 29.1 %collective-permute-start.8 = (bf16[832,768]{1,0:T(8,128)(2,1)}, bf16[832,768]{1,0:T(8,128)(2,1)}, u32[]{:S(2)}, u32[]{:S(2)}) collective-permute-start(bf16[832,768]{1,0:T(8,128)(2,1)} %get-tuple-element.162), channel_id=1, source_target_pairs={{0,2},{1,3},{2,0},{3,1},{4,6},{5,7},{6,4},{7,5},{8,10},{9,11},{10,... | collective-permute-start | bytes 3833864 | tf_op jit(solution)/shard_map/ppermute | solution.py:35
  53.6 34.5 %collective-permute-start.7 = (bf16[592,768]{1,0:T(8,128)(2,1)}, bf16[592,768]{1,0:T(8,128)(2,1)}, u32[]{:S(2)}, u32[]{:S(2)}) collective-permute-start(bf16[592,768]{1,0:T(8,128)(2,1)} %copy-done.16), channel_id=1, source_target_pairs={{0,4},{4,0},{8,12},{12,8},{16,20},{20,16},{24,28},{28,24},{1,5},{5... | collective-permute-start | bytes 2727944 | tf_op jit(solution)/shard_map/ppermute | solution.py:35
  90.9 27.6 %collective-permute-start.9 = (bf16[1184,768]{1,0:T(8,128)(2,1)}, bf16[1184,768]{1,0:T(8,128)(2,1)}, u32[]{:S(2)}, u32[]{:S(2)}) collective-permute-start(bf16[1184,768]{1,0:T(8,128)(2,1)} %join_weights.2.refs_5_.refs_2_), channel_id=1, source_target_pairs={{0,1},{1,0},{2,3},{3,2},{4,5},{5,4},{6,7},{7,6},{8,9},{9,8},{10,11... | collective-permute-start | bytes 5455880 | tf_op jit(solution)/shard_map/ppermute | solution.py:35
  90.9 20.2 %collective-permute-start.10 = (bf16[1024,384]{1,0:T(8,128)(2,1)}, bf16[1024,384]{1,0:T(8,128)(2,1)S(1)}, u32[]{:S(2)}, u32[]{:S(2)}) collective-permute-start(bf16[1024,384]{1,0:T(8,128)(2,1)} %get-tuple-element.164), channel_id=1, source_target_pairs={{0,2},{1,3},{2,0},{3,1},{4,6},{5,7},{6,4},{7,5},{8,10},{9,11},{10,... | collective-permute-start | bytes 2359304 | tf_op jit(solution)/shard_map/ppermute | solution.py:35
  91.4 24.3 %all-to-all-start.1 = ((bf16[8,256,128]{2,1,0:T(8,128)(2,1)}), bf16[8,256,128]{2,1,0:T(8,128)(2,1)}, u32[]{:S(2)}, u32[]{:S(2)}) async-start(bf16[8,256,128]{2,1,0:T(8,128)(2,1)} %bitcast.19), calls=%async_computation.1 | async-start | bytes 1048576 | tf_op jit(solution)/shard_map/all_to_all | solution.py:756
  112.2 37.6 %collective-permute-start.14 = (bf16[1664,768]{1,0:T(8,128)(2,1)}, bf16[1664,768]{1,0:T(8,128)(2,1)}, u32[]{:S(2)}, u32[]{:S(2)}) collective-permute-start(bf16[1664,768]{1,0:T(8,128)(2,1)} %get-tuple-element.178.refs_3_.refs_4_), channel_id=1, source_target_pairs={{0,1},{1,0},{2,3},{3,2},{4,5},{5,4},{6,7},{7,6},{8,9},{9,8},{10,11... | collective-permute-start | bytes 7667720 | tf_op jit(solution)/shard_map/ppermute | solution.py:35
  113.6 30.2 %collective-permute-start.15 = (bf16[832,768]{1,0:T(8,128)(2,1)}, bf16[832,768]{1,0:T(8,128)(2,1)S(1)}, u32[]{:S(2)}, u32[]{:S(2)}) collective-permute-start(bf16[832,768]{1,0:T(8,128)(2,1)} %collective-permute-done.8.direct), channel_id=1, source_target_pairs={{0,4},{4,0},{8,12},{12,8},{16,20},{20,16},{24,28},{28,24},{1,5},{5... | collective-permute-start | bytes 3833864 | tf_op jit(solution)/shard_map/ppermute | solution.py:35
  117.9 22.0 %collective-permute-start.12 = (bf16[1024,128]{1,0:T(8,128)(2,1)}, bf16[1024,128]{1,0:T(8,128)(2,1)}, u32[]{:S(2)}, u32[]{:S(2)}) collective-permute-start(bf16[1024,128]{1,0:T(8,128)(2,1)} %get-tuple-element.171), channel_id=1, source_target_pairs={{0,2},{1,3},{2,0},{3,1},{4,6},{5,7},{6,4},{7,5},{8,10},{9,11},{10,... | collective-permute-start | bytes 786440 | tf_op jit(solution)/shard_map/ppermute | solution.py:35
  196.4 37.4 %collective-permute-start.21 = (bf16[1920,768]{1,0:T(8,128)(2,1)}, bf16[1920,768]{1,0:T(8,128)(2,1)S(1)}, u32[]{:S(2)}, u32[]{:S(2)}) collective-permute-start(bf16[1920,768]{1,0:T(8,128)(2,1)} %get-tuple-element.206), channel_id=1, source_target_pairs={{0,1},{1,0},{2,3},{3,2},{4,5},{5,4},{6,7},{7,6},{8,9},{9,8},{10,11... | collective-permute-start | bytes 8847368 | tf_op jit(solution)/shard_map/ppermute | solution.py:35
  196.5 43.6 %collective-permute-start.20 = (bf16[896,768]{1,0:T(8,128)(2,1)}, bf16[896,768]{1,0:T(8,128)(2,1)}, u32[]{:S(2)}, u32[]{:S(2)}) collective-permute-start(bf16[896,768]{1,0:T(8,128)(2,1)} %get-tuple-element.203), channel_id=1, source_target_pairs={{0,2},{1,3},{2,0},{3,1},{4,6},{5,7},{6,4},{7,5},{8,10},{9,11},{10,... | collective-permute-start | bytes 4128776 | tf_op jit(solution)/shard_map/ppermute | solution.py:35
  218.7 27.0 %all-to-all-start.2 = ((bf16[8,256,128]{2,1,0:T(8,128)(2,1)}), bf16[8,256,128]{2,1,0:T(8,128)(2,1)S(1)}, u32[]{:S(2)}, u32[]{:S(2)}) async-start(bf16[8,256,128]{2,1,0:T(8,128)(2,1)} %bitcast.55), calls=%async_computation.2 | async-start | bytes 1048576 | tf_op jit(solution)/shard_map/all_to_all | solution.py:756
  231.1 33.2 %collective-permute-start.24 = (bf16[1024,384]{1,0:T(8,128)(2,1)}, bf16[1024,384]{1,0:T(8,128)(2,1)}, u32[]{:S(2)}, u32[]{:S(2)}) collective-permute-start(bf16[1024,384]{1,0:T(8,128)(2,1)} %get-tuple-element.220), channel_id=1, source_target_pairs={{0,2},{1,3},{2,0},{3,1},{4,6},{5,7},{6,4},{7,5},{8,10},{9,11},{10,... | collective-permute-start | bytes 2359304 | tf_op jit(solution)/shard_map/ppermute | solution.py:35
  245.2 20.3 %collective-permute-start.23 = (f32[32,768]{1,0:T(8,128)}, f32[32,768]{1,0:T(8,128)S(1)}, u32[]{:S(2)}, u32[]{:S(2)}) collective-permute-start(f32[32,768]{1,0:T(8,128)} %add.243), channel_id=1, source_target_pairs={{0,2},{1,3},{2,0},{3,1},{4,6},{5,7},{6,4},{7,5},{8,10},{9,11},{10,... | collective-permute-start | bytes 294920 | tf_op jit(solution)/shard_map/ppermute | solution.py:35
  266.6 35.2 %collective-permute-start.31 = (bf16[960,768]{1,0:T(8,128)(2,1)S(1)}, bf16[960,768]{1,0:T(8,128)(2,1)S(1)}, u32[]{:S(2)}, u32[]{:S(2)}) collective-permute-start(bf16[960,768]{1,0:T(8,128)(2,1)S(1)} %copy-done.49), channel_id=1, source_target_pairs={{0,2},{1,3},{2,0},{3,1},{4,6},{5,7},{6,4},{7,5},{8,10},{9,11},{10,... | collective-permute-start | bytes 4423688 | tf_op jit(solution)/shard_map/ppermute | solution.py:35
  278.3 56.4 %collective-permute-start.37 = (bf16[960,768]{1,0:T(8,128)(2,1)}, bf16[960,768]{1,0:T(8,128)(2,1)S(1)}, u32[]{:S(2)}, u32[]{:S(2)}) collective-permute-start(bf16[960,768]{1,0:T(8,128)(2,1)} %get-tuple-element.253), channel_id=1, source_target_pairs={{0,2},{1,3},{2,0},{3,1},{4,6},{5,7},{6,4},{7,5},{8,10},{9,11},{10,... | collective-permute-start | bytes 4423688 | tf_op jit(solution)/shard_map/ppermute | solution.py:35
  307.8 36.0 %collective-permute-start.33 = (bf16[1024,384]{1,0:T(8,128)(2,1)S(1)}, bf16[1024,384]{1,0:T(8,128)(2,1)S(1)}, u32[]{:S(2)}, u32[]{:S(2)}) collective-permute-start(bf16[1024,384]{1,0:T(8,128)(2,1)S(1)} %pad_maximum_fusion.1), channel_id=1, source_target_pairs={{0,1},{1,0},{2,3},{3,2},{4,5},{5,4},{6,7},{7,6},{8,9},{9,8},{10,11... | collective-permute-start | bytes 2359304 | tf_op jit(solution)/shard_map/ppermute | solution.py:35
  347.5 76.0 %all-to-all-start.3 = ((bf16[8,256,384]{2,1,0:T(8,128)(2,1)}), bf16[8,256,384]{2,1,0:T(8,128)(2,1)S(1)}, u32[]{:S(2)}, u32[]{:S(2)}) async-start(bf16[8,256,384]{2,1,0:T(8,128)(2,1)} %bitcast.53), calls=%async_computation.3 | async-start | bytes 3145728 | tf_op jit(solution)/shard_map/all_to_all | solution.py:756
  352.9 35.3 %collective-permute-start.41 = (bf16[448,768]{1,0:T(8,128)(2,1)S(1)}, bf16[448,768]{1,0:T(8,128)(2,1)S(1)}, u32[]{:S(2)}, u32[]{:S(2)}) collective-permute-start(bf16[448,768]{1,0:T(8,128)(2,1)S(1)} %maximum_select_fusion.2.own), channel_id=1, source_target_pairs={{0,4},{4,0},{8,12},{12,8},{16,20},{20,16},{24,28},{28,24},{1,5},{5... | collective-permute-start | bytes 2064392 | tf_op jit(solution)/shard_map/ppermute | solution.py:35
  354.9 47.0 %collective-permute-start.39 = (bf16[480,768]{1,0:T(8,128)(2,1)}, bf16[480,768]{1,0:T(8,128)(2,1)S(1)}, u32[]{:S(2)}, u32[]{:S(2)}) collective-permute-start(bf16[480,768]{1,0:T(8,128)(2,1)} %get-tuple-element.260), channel_id=1, source_target_pairs={{0,4},{4,0},{8,12},{12,8},{16,20},{20,16},{24,28},{28,24},{1,5},{5... | collective-permute-start | bytes 2211848 | tf_op jit(solution)/shard_map/ppermute | solution.py:35
  355.0 42.1 %collective-permute-start.40 = (bf16[240,384]{1,0:T(8,128)(2,1)S(1)}, bf16[240,384]{1,0:T(8,128)(2,1)S(1)}, u32[]{:S(2)}, u32[]{:S(2)}) collective-permute-start(bf16[240,384]{1,0:T(8,128)(2,1)S(1)} %copy-done.51), channel_id=1, source_target_pairs={{0,16},{4,20},{8,24},{12,28},{16,0},{20,4},{24,8},{28,12},{1,17},{... | collective-permute-start | bytes 552968 | tf_op jit(solution)/shard_map/ppermute | solution.py:35
  409.3 23.4 %collective-permute-start.45 = (bf16[240,768]{1,0:T(8,128)(2,1)S(1)}, bf16[240,768]{1,0:T(8,128)(2,1)S(1)}, u32[]{:S(2)}, u32[]{:S(2)}) collective-permute-start(bf16[240,768]{1,0:T(8,128)(2,1)S(1)} %maximum_select_fusion.3), channel_id=1, source_target_pairs={{0,8},{4,12},{8,0},{12,4},{16,24},{20,28},{24,16},{28,20},{1,9},{5... | collective-permute-start | bytes 1105928 | tf_op jit(solution)/shard_map/ppermute | solution.py:35
  (87 other events, 722.9 us)
